TPU v7x, 32 devices: a whole 2x2x4 slice. The times are simulated.
32 devices in a mesh: wide: 8 (over y, x, core), narrow: 4 (over z).
Axes of the slice: x: 2, y: 2, z: 4, core: 2. Of those that a mesh axis runs over, the one named last changes fastest.
Arguments:
- tokens: bfloat16 [64, 1024, 512], P(('wide', 'narrow')), may hold values from -6 to 6
- out_grad: bfloat16 [64, 1024, 512], P(('wide', 'narrow')), may hold values from -6 to 6
- group_ids: int32 [64], P(('wide', 'narrow')), may hold values from 0 to 3
- domain_weight: float32 [4], replicated, may hold values from 0.5 to 2
- attn_w: float32 [5, 512, 512], P(None, 'narrow'), as said below
- ffn_w: float32 [2, 2048, 512], P(None, 'narrow'), as said below
- attn_mom: float32 [5, 512, 512], P(None, 'narrow'), as said below
- ffn_mom: float32 [2, 2048, 512], P(None, 'narrow'), as said below
- ln_params: float32 [4, 512], replicated, as said below
- ln_first: float32 [4, 512], P(None, 'narrow')
- ln_second: float32 [4, 512], P(None, 'narrow'), as said below
Outputs:
- output: bfloat16 [64, 1024, 512], P(('wide', 'narrow'))
- input_grad: float32 [64, 1024, 512], P(('wide', 'narrow'))
- attn_grad: float32 [5, 512, 512], P(None, 'narrow')
- ffn_grad: float32 [2, 2048, 512], P(None, 'narrow')
- ln_grad: float32 [4, 512], P(None, 'narrow')
- attn_mom_new: float32 [5, 512, 512], P(None, 'narrow')
- ffn_mom_new: float32 [2, 2048, 512], P(None, 'narrow')
- attn_new: float32 [5, 512, 512], P(None, 'narrow')
- ffn_new: float32 [2, 2048, 512], P(None, 'narrow')
- attn_copy: bfloat16 [5, 512, 512], P(None, 'narrow')
- ffn_copy: bfloat16 [2, 2048, 512], P(None, 'narrow')
- ln_first_new: float32 [4, 512], P(None, 'narrow')
- ln_second_new: float32 [4, 512], P(None, 'narrow')
- ln_new: float32 [4, 512], P(None, 'narrow')
Inputs may be any that keep to these rules, and one draw needn't show every extreme that they name: `attn_mom`: independent entries; row scales of the momenta differ across rows. `ffn_mom`: independent entries. `attn_w`: independent entries. `ffn_w`: independent entries. `ln_params`: gains positive. `ln_second`: Positive.
All inputs are finite; a program needn't handle non-finite values.
Results may differ from a plain program's by a relative error of at most 0.014.
Values may be sent and summed in bfloat16 or wider, within the bound.
A program may use at most 256 MiB of HBM per device.

v0:
```python
import math

import jax
import jax.numpy as jnp
from jax import lax
from jax.sharding import PartitionSpec as P

D = 512
HEADS = 8
FF = 2048
NS_ITERS = 2
STEP = 10


norm_epsilon = 1e-05
momentum_keep = 0.5
quintic_lin = 3.4445
quintic_cube = -4.775
quintic_five = 2.0315
muon_rate = 0.7
muon_decay = 0.1
adam_rate = 0.2
beta_first = 0.9
beta_second = 0.999
adam_epsilon = 1e-08
highest = lax.Precision.HIGHEST


def running_sum(values, reverse):
    length = values.shape[0]
    block = min(128, length)
    count = length // block
    flat = values.reshape(count, block, -1)
    places = jnp.arange(block)
    order = jnp.arange(count)
    if reverse:
        within = (places[:, None] <= places[None, :]).astype(jnp.float32)
        before = (order[:, None] < order[None, :]).astype(jnp.float32)
    else:
        within = (places[:, None] >= places[None, :]).astype(jnp.float32)
        before = (order[:, None] > order[None, :]).astype(jnp.float32)
    inside = jnp.einsum("ts,bsk->btk", within, flat, precision=highest)
    block_sums = jnp.sum(flat, axis=1)
    offsets = jnp.dot(before, block_sums, precision=highest)
    return (inside + offsets[:, None, :]).reshape(values.shape)


def normalize(row_values):
    center = row_values - jnp.mean(row_values, axis=-1, keepdims=True)
    spread = jnp.mean(center * center, axis=-1, keepdims=True)
    inverse = lax.rsqrt(spread + norm_epsilon)
    return (center * inverse, inverse)


def norm_back(grad_rows, normed, inverse, gain):
    grad_gain = jnp.sum(grad_rows * normed, axis=0)
    grad_shift = jnp.sum(grad_rows, axis=0)
    grad_normed = grad_rows * gain
    centered = grad_normed - jnp.mean(grad_normed, axis=-1, keepdims=True)
    grad_values = inverse * (
        centered - normed * jnp.mean(grad_normed * normed, axis=-1, keepdims=True)
    )
    return (grad_gain, grad_shift, grad_values)


def causal_mask(offset, block_rows, length):
    rows_at = offset + jnp.arange(block_rows)
    return (rows_at[:, None] >= jnp.arange(length)[None, :]).astype(jnp.float32)


def block_forward(queries, key_rows, slot_weight, totals, offset, block_rows):
    length = key_rows.shape[0]
    scaling = queries.shape[-1] ** (-0.5)
    query_rows = lax.dynamic_slice_in_dim(queries, offset, block_rows, 0)
    total_rows = lax.dynamic_slice_in_dim(totals, offset, block_rows, 0)
    causal = causal_mask(offset, block_rows, length)
    raw_scores = jnp.einsum(
        "thd,shd->hts", query_rows, key_rows, preferred_element_type=jnp.float32
    )
    scores = (raw_scores * scaling * causal).astype(jnp.bfloat16)
    numerator = jnp.einsum("hts,shm->thm", scores, slot_weight, preferred_element_type=jnp.float32)
    slot_prob = jax.nn.softmax(numerator / total_rows, axis=-1)
    shares = (slot_prob / total_rows).astype(jnp.bfloat16)
    mixing_raw = jnp.einsum("thm,shm->hts", shares, slot_weight, preferred_element_type=jnp.float32)
    mixing = (mixing_raw * causal).astype(jnp.bfloat16)
    return (query_rows, total_rows, causal, scores, numerator, slot_prob, shares, mixing)


def attend_forward(queries, key_rows, value_rows, slot_weight, totals):
    length = queries.shape[0]
    block_rows = min(512, length)

    def one_block(offset):
        parts = block_forward(queries, key_rows, slot_weight, totals, offset, block_rows)
        mixing = parts[7]
        return jnp.einsum(
            "hts,shd->thd", mixing, value_rows, preferred_element_type=jnp.float32
        ).astype(jnp.bfloat16)

    offsets = jnp.arange(length // block_rows) * block_rows
    return lax.map(one_block, offsets).reshape(queries.shape)


def attend_backward(queries, key_rows, value_rows, slot_weight, totals, grad_attended):
    length = queries.shape[0]
    block_rows = min(512, length)
    scaling = queries.shape[-1] ** (-0.5)

    def one_block(running, offset):
        grad_keys, grad_values, grad_slots = running
        query_rows, total_rows, causal, scores, numerator, slot_prob, shares, mixing = (
            block_forward(queries, key_rows, slot_weight, totals, offset, block_rows)
        )
        grad_rows = lax.dynamic_slice_in_dim(grad_attended, offset, block_rows, 0)
        grad_mix_raw = jnp.einsum(
            "thd,shd->hts", grad_rows, value_rows, preferred_element_type=jnp.float32
        )
        grad_mixing = (grad_mix_raw * causal).astype(jnp.bfloat16)
        grad_values = grad_values + jnp.einsum(
            "hts,thd->shd", mixing, grad_rows, preferred_element_type=jnp.float32
        )
        grad_shares = jnp.einsum(
            "hts,shm->thm", grad_mixing, slot_weight, preferred_element_type=jnp.float32
        ).astype(jnp.bfloat16)
        grad_slots = grad_slots + jnp.einsum(
            "hts,thm->shm", grad_mixing, shares, preferred_element_type=jnp.float32
        )
        grad_share_f = grad_shares.astype(jnp.float32)
        grad_prob = grad_share_f / total_rows
        grad_logit = slot_prob * (
            grad_prob - jnp.sum(grad_prob * slot_prob, axis=-1, keepdims=True)
        )
        grad_numer = (grad_logit / total_rows).astype(jnp.bfloat16)
        grad_totals = -(grad_share_f * slot_prob + grad_logit * numerator) / (
            total_rows * total_rows
        )
        grad_score_raw = jnp.einsum(
            "thm,shm->hts", grad_numer, slot_weight, preferred_element_type=jnp.float32
        )
        grad_scores = (grad_score_raw * causal).astype(jnp.bfloat16)
        grad_slots = grad_slots + jnp.einsum(
            "hts,thm->shm", scores, grad_numer, preferred_element_type=jnp.float32
        )
        grad_query = (
            jnp.einsum("hts,shd->thd", grad_scores, key_rows, preferred_element_type=jnp.float32)
            * scaling
        )
        grad_keys = (
            grad_keys
            + jnp.einsum(
                "hts,thd->shd", grad_scores, query_rows, preferred_element_type=jnp.float32
            )
            * scaling
        )
        return ((grad_keys, grad_values, grad_slots), (grad_query, grad_totals))

    start_state = (
        jnp.zeros(key_rows.shape, jnp.float32),
        jnp.zeros(value_rows.shape, jnp.float32),
        jnp.zeros(slot_weight.shape, jnp.float32),
    )
    offsets = jnp.arange(length // block_rows) * block_rows
    (grad_keys, grad_values, grad_slots), (query_blocks, total_blocks) = lax.scan(
        one_block, start_state, offsets
    )
    grad_totals = total_blocks.reshape(totals.shape)
    grad_slots = grad_slots + running_sum(grad_totals, True)
    return (query_blocks.reshape(queries.shape), grad_keys, grad_values, grad_slots)


def gram_of(matrix):
    return jnp.einsum("jrd,jre->jde", matrix, matrix, precision=highest)


def quintic(matrix, gram):
    square = jnp.einsum("jde,jef->jdf", gram, gram, precision=highest)
    poly = quintic_cube * gram + quintic_five * square
    return quintic_lin * matrix + jnp.einsum("jrd,jde->jre", matrix, poly, precision=highest)


def gram_pair(attn_iter, ffn_iter):
    return lax.psum((gram_of(attn_iter), gram_of(ffn_iter)), "narrow")


def newton_rows(attn_iter, ffn_iter):
    for newton_turn in range(NS_ITERS):
        attn_gram, ffn_gram = gram_pair(attn_iter, ffn_iter)
        attn_iter = quintic(attn_iter, attn_gram)
        ffn_iter = quintic(ffn_iter, ffn_gram)
    return (attn_iter, ffn_iter)


def shards(
    tokens,
    out_grad,
    group_ids,
    domain_weight,
    attn_w,
    ffn_w,
    attn_mom,
    ffn_mom,
    ln_params,
    ln_first,
    ln_second,
):
    local_seqs, length, model_width = tokens.shape
    token_count = local_seqs * length
    member = (group_ids[:, None] == jnp.arange(domain_weight.shape[0])[None, :]).astype(jnp.int32)
    group_count = lax.psum(jnp.sum(member, axis=0), ("wide", "narrow"))
    chosen = member.astype(jnp.float32)
    weight_of = jnp.sum(chosen * domain_weight[None, :], axis=1)
    count_of = jnp.sum(chosen * group_count[None, :].astype(jnp.float32), axis=1)
    total_seqs = local_seqs * lax.axis_size("wide") * lax.axis_size("narrow")
    seq_weight = weight_of * total_seqs / (domain_weight.shape[0] * count_of)
    attn_low = lax.all_gather(attn_w.astype(jnp.bfloat16), "narrow", axis=1, tiled=True)
    flat_rows = tokens.reshape(token_count, model_width).astype(jnp.float32)
    normed_one, inverse_one = normalize(flat_rows)
    first_norm = (normed_one * ln_params[0] + ln_params[1]).astype(jnp.bfloat16)
    projected = jnp.einsum(
        "nd,jde->jne", first_norm, attn_low[:4], preferred_element_type=jnp.float32
    )
    head_shape = (local_seqs, length, HEADS, -1)
    queries = projected[0].astype(jnp.bfloat16).reshape(head_shape)
    key_rows = projected[1].astype(jnp.bfloat16).reshape(head_shape)
    value_rows = projected[2].astype(jnp.bfloat16).reshape(head_shape)
    expo_logits = jnp.exp(projected[3])
    slot_flat = expo_logits.astype(jnp.bfloat16)
    slot_weight = slot_flat.reshape(head_shape)
    totals = jax.vmap(lambda values: running_sum(values, False))(slot_weight.astype(jnp.float32))
    attended = lax.map(
        lambda pieces: attend_forward(*pieces), (queries, key_rows, value_rows, slot_weight, totals)
    )
    attended = attended.reshape(token_count, model_width)
    ffn_low = lax.all_gather(ffn_w.astype(jnp.bfloat16), "narrow", axis=1, tiled=True)
    mixed = flat_rows + jnp.dot(attended, attn_low[4], preferred_element_type=jnp.float32)
    normed_two, inverse_two = normalize(mixed)
    second_norm = (normed_two * ln_params[2] + ln_params[3]).astype(jnp.bfloat16)
    inner_act = jnp.einsum("nd,fd->nf", second_norm, ffn_low[0], preferred_element_type=jnp.float32)
    hidden = jax.nn.gelu(inner_act).astype(jnp.bfloat16)
    result = mixed + jnp.dot(hidden, ffn_low[1], preferred_element_type=jnp.float32)
    output = result.astype(jnp.bfloat16).reshape(tokens.shape)
    ffn_back = lax.all_gather(ffn_w.astype(jnp.bfloat16), "narrow", axis=1, tiled=True)
    grad_out = (out_grad.astype(jnp.float32) * seq_weight[:, None, None]).reshape(
        token_count, model_width
    )
    grad_final = grad_out.astype(jnp.bfloat16)
    grad_down = jnp.einsum("nf,nd->fd", hidden, grad_final, preferred_element_type=jnp.float32)
    grad_hidden = jnp.einsum(
        "nd,fd->nf", grad_final, ffn_back[1], preferred_element_type=jnp.float32
    ).astype(jnp.bfloat16)
    gelu_value, gelu_back = jax.vjp(jax.nn.gelu, inner_act)
    grad_inner = gelu_back(grad_hidden.astype(jnp.float32))[0].astype(jnp.bfloat16)
    grad_up = jnp.einsum("nf,nd->fd", grad_inner, second_norm, preferred_element_type=jnp.float32)
    grad_second = jnp.einsum(
        "nf,fd->nd", grad_inner, ffn_back[0], preferred_element_type=jnp.float32
    )
    gain_two, shift_two, grad_through = norm_back(
        grad_second, normed_two, inverse_two, ln_params[2]
    )
    grad_mixed = grad_out + grad_through
    attn_back = lax.all_gather(attn_w.astype(jnp.bfloat16), "narrow", axis=1, tiled=True)
    grad_att = grad_mixed.astype(jnp.bfloat16)
    grad_outproj = jnp.einsum("nd,ne->de", attended, grad_att, preferred_element_type=jnp.float32)
    grad_attended = jnp.einsum(
        "ne,de->nd", grad_att, attn_back[4], preferred_element_type=jnp.float32
    ).astype(jnp.bfloat16)
    grad_attended = grad_attended.reshape(head_shape)
    grad_query, grad_keys, grad_values, grad_slots = lax.map(
        lambda pieces: attend_backward(*pieces),
        (queries, key_rows, value_rows, slot_weight, totals, grad_attended),
    )
    grad_slot_low = grad_slots.reshape(token_count, model_width).astype(jnp.bfloat16)
    grad_logits = (grad_slot_low.astype(jnp.float32) * expo_logits).astype(jnp.bfloat16)
    grad_stack = jnp.stack(
        [
            grad_query.reshape(token_count, model_width).astype(jnp.bfloat16),
            grad_keys.reshape(token_count, model_width).astype(jnp.bfloat16),
            grad_values.reshape(token_count, model_width).astype(jnp.bfloat16),
            grad_logits,
        ]
    )
    grad_inproj = jnp.einsum(
        "nd,jne->jde", first_norm, grad_stack, preferred_element_type=jnp.float32
    )
    grad_first = jnp.einsum(
        "jne,jde->nd", grad_stack, attn_back[:4], preferred_element_type=jnp.float32
    )
    gain_one, shift_one, grad_lower = norm_back(grad_first, normed_one, inverse_one, ln_params[0])
    input_grad = (grad_mixed + grad_lower).reshape(tokens.shape)
    attn_full = jnp.concatenate([grad_inproj, grad_outproj[None]], axis=0)
    ffn_full = jnp.stack([grad_up, grad_down])
    ln_full = jnp.stack([gain_one, shift_one, gain_two, shift_two])
    attn_part, ffn_part, ln_part = (
        lax.psum_scatter(attn_full, "narrow", scatter_dimension=1, tiled=True),
        lax.psum_scatter(ffn_full, "narrow", scatter_dimension=1, tiled=True),
        lax.psum_scatter(ln_full, "narrow", scatter_dimension=1, tiled=True),
    )
    attn_grad, ffn_grad, ln_grad = lax.psum((attn_part, ffn_part, ln_part), "wide")
    attn_moment = momentum_keep * attn_mom + attn_grad
    ffn_moment = momentum_keep * ffn_mom + ffn_grad
    attn_squared, ffn_squared = lax.psum(
        (
            jnp.sum(attn_moment * attn_moment, axis=(1, 2)),
            jnp.sum(ffn_moment * ffn_moment, axis=(1, 2)),
        ),
        "narrow",
    )
    attn_scale = jnp.sqrt(attn_squared)[:, None, None] + 1e-07
    ffn_scale = jnp.sqrt(ffn_squared)[:, None, None] + 1e-07
    attn_ortho, ffn_ortho = newton_rows(attn_moment / attn_scale, ffn_moment / ffn_scale)
    keep_factor = 1.0 - muon_rate * muon_decay
    attn_new = keep_factor * attn_w - muon_rate * 0.2 * math.sqrt(max(D, D)) * attn_ortho
    ffn_new = keep_factor * ffn_w - muon_rate * 0.2 * math.sqrt(max(FF, D)) * ffn_ortho
    shard_width = ln_first.shape[1]
    own_params = lax.dynamic_slice_in_dim(
        ln_params, lax.axis_index("narrow") * shard_width, shard_width, 1
    )
    first_new = beta_first * ln_first + (1.0 - beta_first) * ln_grad
    second_new = beta_second * ln_second + (1.0 - beta_second) * ln_grad * ln_grad
    first_fix = 1.0 - beta_first**STEP
    second_fix = 1.0 - beta_second**STEP
    ln_new = own_params - adam_rate * (first_new / first_fix) / (
        jnp.sqrt(second_new / second_fix) + adam_epsilon
    )
    return (
        output,
        input_grad,
        attn_grad,
        ffn_grad,
        ln_grad,
        attn_moment,
        ffn_moment,
        attn_new,
        ffn_new,
        attn_new.astype(jnp.bfloat16),
        ffn_new.astype(jnp.bfloat16),
        first_new,
        second_new,
        ln_new,
    )


def solution(mesh):
    return jax.shard_map(
        shards,
        mesh=mesh,
        in_specs=(
            P(("wide", "narrow"), None, None),
            P(("wide", "narrow"), None, None),
            P(("wide", "narrow")),
            P(),
            P(None, "narrow", None),
            P(None, "narrow", None),
            P(None, "narrow", None),
            P(None, "narrow", None),
            P(),
            P(None, "narrow"),
            P(None, "narrow"),
        ),
        out_specs=(
            P(("wide", "narrow"), None, None),
            P(("wide", "narrow"), None, None),
            P(None, "narrow", None),
            P(None, "narrow", None),
            P(None, "narrow"),
            P(None, "narrow", None),
            P(None, "narrow", None),
            P(None, "narrow", None),
            P(None, "narrow", None),
            P(None, "narrow", None),
            P(None, "narrow", None),
            P(None, "narrow"),
            P(None, "narrow"),
            P(None, "narrow"),
        ),
        check_vma=False,
    )
```

profile of v0, /device:TPU:0, one launch (start us, length us, event | category | flops | bytes accessed | tf_op | source)
XLA Modules:
  0.0 1660.2 jit_solution(4258155091554859374)
XLA Ops:
  12.6 44.7 %psum.70 = s32[4]{0:T(128)S(1)} all-reduce(s32[4]{0:T(128)S(1)} %fusion.130), channel_id=1, replica_groups=mesh['wide'=8,'narrow'=4] {'wide','narrow'}, use_global_device_ids=true, to_apply=%region_13.14 | all-reduce | flops 4 | bytes 32 | tf_op jit(solution)/shard_map/psum | solution.py:209
  68.7 10.4 fusion.148
  79.0 10.4 fusion.146
  141.3 104.1 %while.56 = (s32[]{:T(128)}, bf16[2,1024,8,64]{3,2,1,0:T(8,128)(2,1)}, bf16[2,1024,8,64]{1,3,2,0:T(8,128)(2,1)}, f32[2,1024,8,64]{1,3,2,0:T(8,128)}, bf16[2,1024...) while((s32[]{:T(128)}, ...), condition=%wide.region_8.9_spmd, body=%wide.region_3.8_spmd.sunk | while | flops 2168193536 | bytes 35691940 | solution.py:230
  150.7 38.7 %while.59 = (s32[]{:T(128)}, bf16[2,512,8,64]{1,3,2,0:T(8,128)(2,1)}, s32[2]{0:T(128)S(1)}, bf16[1024,8,64]{0,2,1:T(8,128)(2,1)}, bf16[1024,8,64]{0,2,1:T(8,128)...) while((s32[]{:T(128)}, ...), condition=%wide.region_7.7_spmd, body=%wide.region_4.6_spmd.sunk | while | flops 2168193536 | bytes 17865904 | solution.py:101
  154.1 8.2 fusion.287
  162.5 7.7 fusion.288
  173.6 8.0 fusion.287
  181.8 7.6 fusion.288
  202.6 38.7 %while.59 = (s32[]{:T(128)}, bf16[2,512,8,64]{1,3,2,0:T(8,128)(2,1)}, s32[2]{0:T(128)S(1)}, bf16[1024,8,64]{0,2,1:T(8,128)(2,1)}, bf16[1024,8,64]{0,2,1:T(8,128)...) while((s32[]{:T(128)}, ...), condition=%wide.region_7.7_spmd, body=%wide.region_4.6_spmd.sunk | while | flops 2168193536 | bytes 17865904 | solution.py:101
  206.0 8.2 fusion.287
  214.3 7.7 fusion.288
  225.4 8.0 fusion.287
  233.7 7.6 fusion.288
  245.4 6.7 reshape.275
  257.3 13.4 fusion.97
  270.7 18.2 %fusion.51 = bf16[2048,2048]{1,0:T(8,128)(2,1)} fusion(f32[2048,2048]{1,0:T(8,128)} %fusion.97, bf16[2048,512]{1,0:T(8,128)(2,1)S(1)} %bitcast.351, bf16[2,2048,512]{2,1,0:T(8,128)(2,1)S(1)} %copy-done.79), kind=kOutput, calls=%fused_computation.95 | convolution fusion | flops 4387241984 | bytes 29360128 | tf_op jit(solution)/shard_map/nd,fd->nf/dot_general | solution.py:248
  289.0 8.8 multiply_reduce_fusion.1
  314.3 347.0 %while.58 = (s32[]{:T(128)}, bf16[2,1024,8,64]{3,2,1,0:T(8,128)(2,1)}, bf16[2,1024,8,64]{1,3,2,0:T(8,128)(2,1)}, bf16[2,1024,8,64]{1,3,2,0:T(8,128)(2,1)}, bf16[...) while((s32[]{:T(128)}, ...), condition=%wide.region_24.25_spmd, body=%wide.region_17.24_spmd.sunk | while | flops 6759268864 | bytes 321003744 | solution.py:268
  332.1 134.2 %while.60 = (s32[]{:T(128)}, f32[1024,8,64]{0,2,1:T(8,128)}, f32[1024,8,64]{0,2,1:T(8,128)}, f32[1024,8,64]{0,2,1:T(8,128)}, bf16[2,512,8,64]{1,3,2,0:T(8,128)(2...) while((s32[]{:T(128)}, f32[1024,8,64]{0,2,1:T(8,128)}, ...), condition=%wide.region_22.22_spmd.clone, body=%wide.region_18.21_spmd.clone.sunk | while | flops 5951984128 | bytes 246488912 | solution.py:163
  363.3 19.6 %dynamic_update_slice.49 = f32[2,512,8,64]{1,0,3,2:T(2,128)} dynamic-update-slice(f32[2,512,8,64]{1,0,3,2:T(2,128)} %get-tuple-element.879, f32[1,512,8,64]{1,0,3,2:T(1,128)} %copy.273, s32[]{:T(128)S(6)} %copy.282, s32[]{:T(128)} %constant.78.clone.1..sunk.3..sunk, s32[]{:T(128)} %constant.78.clone.1..sunk.3..sunk, s32[]{:T(128)} %constant.78.clone.1..sunk.3..sunk) | dynamic-update-slice | bytes 2097156 | tf_op jit(solution)/shard_map/while/body/eval_jaxpr/while/body/jit(dynamic_update_index_in_dim)/dynamic_update_slice | solution.py:163
  430.0 19.6 %dynamic_update_slice.49 = f32[2,512,8,64]{1,0,3,2:T(2,128)} dynamic-update-slice(f32[2,512,8,64]{1,0,3,2:T(2,128)} %get-tuple-element.879, f32[1,512,8,64]{1,0,3,2:T(1,128)} %copy.273, s32[]{:T(128)S(6)} %copy.282, s32[]{:T(128)} %constant.78.clone.1..sunk.3..sunk, s32[]{:T(128)} %constant.78.clone.1..sunk.3..sunk, s32[]{:T(128)} %constant.78.clone.1..sunk.3..sunk) | dynamic-update-slice | bytes 2097156 | tf_op jit(solution)/shard_map/while/body/eval_jaxpr/while/body/jit(dynamic_update_index_in_dim)/dynamic_update_slice | solution.py:163
  449.6 7.1 bitcast_add_fusion.10
  499.4 134.2 %while.60 = (s32[]{:T(128)}, f32[1024,8,64]{0,2,1:T(8,128)}, f32[1024,8,64]{0,2,1:T(8,128)}, f32[1024,8,64]{0,2,1:T(8,128)}, bf16[2,512,8,64]{1,3,2,0:T(8,128)(2...) while((s32[]{:T(128)}, f32[1024,8,64]{0,2,1:T(8,128)}, ...), condition=%wide.region_22.22_spmd.clone, body=%wide.region_18.21_spmd.clone.sunk | while | flops 5951984128 | bytes 246488912 | solution.py:163
  530.6 19.6 %dynamic_update_slice.49 = f32[2,512,8,64]{1,0,3,2:T(2,128)} dynamic-update-slice(f32[2,512,8,64]{1,0,3,2:T(2,128)} %get-tuple-element.879, f32[1,512,8,64]{1,0,3,2:T(1,128)} %copy.273, s32[]{:T(128)S(6)} %copy.282, s32[]{:T(128)} %constant.78.clone.1..sunk.3..sunk, s32[]{:T(128)} %constant.78.clone.1..sunk.3..sunk, s32[]{:T(128)} %constant.78.clone.1..sunk.3..sunk) | dynamic-update-slice | bytes 2097156 | tf_op jit(solution)/shard_map/while/body/eval_jaxpr/while/body/jit(dynamic_update_index_in_dim)/dynamic_update_slice | solution.py:163
  597.3 19.6 %dynamic_update_slice.49 = f32[2,512,8,64]{1,0,3,2:T(2,128)} dynamic-update-slice(f32[2,512,8,64]{1,0,3,2:T(2,128)} %get-tuple-element.879, f32[1,512,8,64]{1,0,3,2:T(1,128)} %copy.273, s32[]{:T(128)S(6)} %copy.282, s32[]{:T(128)} %constant.78.clone.1..sunk.3..sunk, s32[]{:T(128)} %constant.78.clone.1..sunk.3..sunk, s32[]{:T(128)} %constant.78.clone.1..sunk.3..sunk) | dynamic-update-slice | bytes 2097156 | tf_op jit(solution)/shard_map/while/body/eval_jaxpr/while/body/jit(dynamic_update_index_in_dim)/dynamic_update_slice | solution.py:163
  616.9 7.1 bitcast_add_fusion.10
  661.2 6.5 reshape.277
  673.4 6.6 reshape.278
  684.3 6.6 reshape.279
  695.5 7.5 reshape.280
  720.4 9.4 convolution_bitcast_fusion.3
  729.8 9.8 convolution_bitcast_fusion.2
  744.0 65.2 %reduce-scatter.6.cloned.1.call-done = f32[5,128,512]{1,2,0:T(8,128)} async-done(((f32[5,512,512]{1,2,0:T(8,128)}), f32[5,128,512]{1,2,0:T(8,128)}) %reduce-scatter.6.cloned.1.call-update) | async-done | bytes 1310736 | tf_op jit(solution)/shard_map/reduce_scatter | solution.py:294
  809.2 147.2 %reduce-scatter.8.cloned.1.call-done = f32[2,512,512]{2,1,0:T(8,128)} async-done(((f32[2,2048,512]{2,1,0:T(8,128)}), f32[2,512,512]{2,1,0:T(8,128)}) %reduce-scatter.8.cloned.1.call-update) | async-done | bytes 2097168 | tf_op jit(solution)/shard_map/reduce_scatter | solution.py:295
  956.9 76.0 %all-reduce.8.cloned.1.call-done = (f32[5,128,512]{1,2,0:T(8,128)}, f32[2,512,512]{2,1,0:T(8,128)}) async-done(((f32[5,128,512]{1,2,0:T(8,128)}, f32[2,512,512]{2,1,0:T(8,128)}), (f32[5,128,512]{1,2,0:T(8,128)}, f32[2,512,512]{2,1,0:T(8,128)})) %all-reduce.8.cloned.1.call-update) | async-done | bytes 3407888 | tf_op jit(solution)/shard_map/psum | solution.py:298
  1037.2 12.1 all-reduce.1
  1062.4 11.7 fusion.67
  1075.2 240.2 %all-reduce.12.cloned.1.call-done = (f32[5,512,512]{2,1,0:T(8,128)}, f32[2,512,512]{2,1,0:T(8,128)}) async-done(((f32[5,512,512]{2,1,0:T(8,128)}, f32[2,512,512]{2,1,0:T(8,128)}), (f32[5,512,512]{2,1,0:T(8,128)}, f32[2,512,512]{2,1,0:T(8,128)})) %all-reduce.12.cloned.1.call-update) | async-done | bytes 7340048 | tf_op jit(solution)/shard_map/psum | solution.py:182
  1327.5 9.7 fusion.155
  1337.2 8.7 fusion.105
  1360.0 7.0 fusion.79
  1368.8 10.1 add_convert_fusion
  1379.9 14.0 psum.73
  1399.5 213.8 %all-reduce.10.cloned.1.call-done = (f32[5,512,512]{2,1,0:T(8,128)}, f32[2,512,512]{2,1,0:T(8,128)}) async-done(((f32[5,512,512]{2,1,0:T(8,128)}, f32[2,512,512]{2,1,0:T(8,128)}), (f32[5,512,512]{2,1,0:T(8,128)}, f32[2,512,512]{2,1,0:T(8,128)})) %all-reduce.10.cloned.1.call-update) | async-done | bytes 7340048 | tf_op jit(solution)/shard_map/psum | solution.py:182
  1619.3 8.0 fusion.151
  1627.3 9.2 fusion.157
  1636.6 10.0 fusion.150
  (537 shorter events, 457.5 us)
Async XLA Ops:
  7.2 61.5 %all-gather.3.cloned.1.call-start = ((), (), s32[]{:S(2)}) async-start(), calls=%async_computation.3 | async-start | bytes 3276800 | tf_op jit(solution)/shard_map/all_gather | solution.py:215
  9.5 47.9 %copy-start.20 = (bf16[2,1024,512]{2,1,0:T(8,128)(2,1)S(1)}, bf16[2,1024,512]{2,1,0:T(8,128)(2,1)}, u32[]{:S(2)}) copy-start(bf16[2,1024,512]{2,1,0:T(8,128)(2,1)} %param.19) | copy-start | bytes 6291460
  9.5 247.7 %all-gather.5.cloned.1.call-start = ((), (), s32[]{:S(2)}) async-start(), calls=%async_computation.4 | async-start | bytes 5242880 | tf_op jit(solution)/shard_map/all_gather | solution.py:234
  12.4 45.3 %copy-start.67 = (f32[4,512]{1,0:T(4,128)S(1)}, f32[4,512]{1,0:T(4,128)}, u32[]{:S(2)}) copy-start(f32[4,512]{1,0:T(4,128)} %param.27) | copy-start | bytes 24580
  12.4 796.8 %reduce-scatter.6.cloned.1.call-start = ((), (), s32[]{:S(2)}) async-start(), calls=%async_computation.5 | async-start | bytes 6553600 | tf_op jit(solution)/shard_map/reduce_scatter | solution.py:294
  79.0 10.4 copy-start.27
  117.3 5.7 copy-start.44
  126.6 5.6 copy-start.43
  245.4 6.8 copy-start.21
  255.3 42.6 %copy-start.57 = (f32[2048]{0:T(1024)}, f32[2048]{0:T(1024)S(1)}, u32[]{:S(2)}) copy-start(f32[2048]{0:T(1024)S(1)} %broadcast_multiply_fusion.4) | copy-start | bytes 24580
  257.2 40.6 %copy-start.63 = (f32[2048]{0:T(1024)}, f32[2048]{0:T(1024)S(1)}, u32[]{:S(2)}) copy-start(f32[2048]{0:T(1024)S(1)} %add_rsqrt_fusion) | copy-start | bytes 24580
  257.3 13.4 copy-start.54
  257.3 13.4 copy-start.79
  270.7 18.2 %copy-start.24 = (f32[2048,512]{1,0:T(8,128)S(1)}, f32[2048,512]{1,0:T(8,128)}, u32[]{:S(2)}) copy-start(f32[2048,512]{1,0:T(8,128)} %copy-done.23) | copy-start | bytes 12582916
  289.0 8.8 copy-start.28
  673.4 6.6 copy-start.47
  684.3 6.6 copy-start.46
  703.0 4.7 copy-start.39
  703.0 4.8 copy-start.49
  703.0 5.3 copy-start.50
  703.0 5.9 copy-start.51
  709.0 4.7 copy-start.56
  716.7 239.7 %reduce-scatter.8.cloned.1.call-start = ((), (), s32[]{:S(2)}) async-start(), calls=%async_computation.6 | async-start | bytes 10485760 | tf_op jit(solution)/shard_map/reduce_scatter | solution.py:295
  743.9 212.6 %copy-start.55 = (f32[5,128,512]{2,1,0:T(8,128)S(1)}, f32[5,128,512]{2,1,0:T(8,128)}, u32[]{:S(2)}) copy-start(f32[5,128,512]{2,1,0:T(8,128)} %param.25) | copy-start | bytes 3932164
  744.0 289.0 %all-reduce.8.cloned.1.call-start = ((), (), s32[]{:S(2)}) async-start(), calls=%async_computation.8 | async-start | bytes 6815744 | tf_op jit(solution)/shard_map/psum | solution.py:298
  956.4 359.0 %all-reduce.12.cloned.1.call-start = ((), (), s32[]{:S(2)}) async-start(), calls=%async_computation.10 | async-start | bytes 14680064 | tf_op jit(solution)/shard_map/psum | solution.py:182
  1034.7 19.9 %copy-start.36 = (f32[5,128,512]{1,2,0:T(8,128)}, f32[5,128,512]{1,2,0:T(8,128)S(1)}, u32[]{:S(2)}) copy-start(f32[5,128,512]{1,2,0:T(8,128)S(1)} %get-tuple-element.501) | copy-start | bytes 3932164
  1037.2 17.4 %copy-start.48 = (f32[2,512,512]{2,1,0:T(8,128)}, f32[2,512,512]{2,1,0:T(8,128)S(1)}, u32[]{:S(2)}) copy-start(f32[2,512,512]{2,1,0:T(8,128)S(1)} %get-tuple-element.1032) | copy-start | bytes 6291460
  1060.9 13.3 copy-start.75
  1060.9 13.2 copy-start.76
  1060.9 318.0 %reduce-scatter.10.cloned.1.call-start = ((), (), s32[]{:S(2)}) async-start(), calls=%async_computation.7 | async-start | bytes 327680
  1075.0 538.3 %all-reduce.10.cloned.1.call-start = ((), (), s32[]{:S(2)}) async-start(), calls=%async_computation.9 | async-start | bytes 14680064 | tf_op jit(solution)/shard_map/psum | solution.py:182
  1315.4 5.9 copy-start.42
  1315.4 12.1 slice-start.2
  1321.3 6.2 slice-start.3
  1327.5 24.7 %copy-start.33 = (f32[2,512,512]{2,1,0:T(8,128)}, f32[2,512,512]{2,1,0:T(8,128)S(1)}, u32[]{:S(2)}) copy-start(f32[2,512,512]{2,1,0:T(8,128)S(1)} %multiply_add_fusion) | copy-start | bytes 6291460
  1327.5 9.7 copy-start.37
  1360.0 7.1 copy-start.26
  1360.0 8.8 copy-start.80
  1368.8 25.1 %copy-start.71 = (f32[4,128]{1,0:T(4,128)S(1)}, f32[4,128]{1,0:T(4,128)}, u32[]{:S(2)}) copy-start(f32[4,128]{1,0:T(4,128)} %param.29) | copy-start | bytes 6148
  1368.8 25.1 %copy-start.72 = (f32[4,128]{1,0:T(4,128)S(1)}, f32[4,128]{1,0:T(4,128)}, u32[]{:S(2)}) copy-start(f32[4,128]{1,0:T(4,128)} %param.28) | copy-start | bytes 6148
  1378.9 19.2 %copy-start.38 = (f32[5,128,512]{1,2,0:T(8,128)S(1)}, f32[5,128,512]{1,2,0:T(8,128)}, u32[]{:S(2)}) copy-start(f32[5,128,512]{1,2,0:T(8,128)} %copy-done.36) | copy-start | bytes 3932164
  1393.9 5.6 copy-start.70
  1613.3 5.9 copy-start.34
  1613.3 13.9 slice-start
  1619.3 8.0 slice-start.1
  1627.3 9.3 copy-start.45
  1646.5 5.1 copy-start.41
  (108 other events, 272.3 us)
Sparse Core Ops, SparseCore 0:
  10.2 58.4 all-gather.2
  70.8 79.4 all-gather.4
  716.8 92.3 reduce-scatter.5
  811.4 144.9 reduce-scatter.7
  959.7 73.2 all-reduce.7
  1061.0 254.4 all-reduce.11
  1318.3 18.5 reduce-scatter.9
  1357.3 255.9 all-reduce.9
where the time goes:
time: 1680 us; the launch traced here: 1660 us
  waiting for transfers between devices  746 us (44%)
  matrix products  378 us (22%)
  local copies, waits for them, and re-layouts  334 us (20%)
  other arithmetic  85.4 us (5%)
  blocking collectives  70.8 us (4%)
  loops' own time  29.5 us (2%)
    psum x2, waiting for transfers between devices, gram_pair(): return lax.psum((gram_of(attn_iter), gram_of(ffn_iter)), 'narrow')  454 us
    reduce_scatter x1, waiting for transfers between devices, shards(): lax.psum_scatter(ffn_full, 'narrow', scatter_dimension=1, tiled=True)  147 us
    dynamic_update_slice x8, local copies, waits for them, and re-layouts, attend_backward(): lax.scan(one_block, start_state, offsets)  86.8 us
    psum x1, waiting for transfers between devices, shards(): lax.psum((attn_part, ffn_part, ln_part), 'wide')  76 us
    reduce_scatter x1, waiting for transfers between devices, shards(): lax.psum_scatter(attn_full, 'narrow', scatter_dimension=1, tiled=True)  65.2 us
    squeeze x18, local copies, waits for them, and re-layouts, shards(): lax.map(lambda pieces: attend_forward(*pieces), (queries, key_rows, value...  45.3 us
    psum x1, blocking collectives, shards(): group_count = lax.psum(jnp.sum(member, axis=0), ('wide', 'narrow'))  44.7 us
  transfers between devices with their start and end apart: 8, of which 6 were waited for; matrix products, arithmetic and copies ran while one was open for 18% of the time, Pallas kernels for 0%

commit v1 on v0

v1 whole, which is shorter than its diff:
```python
import functools
import math

import jax
import jax.numpy as jnp
from jax import lax
from jax.experimental import pallas as pl
from jax.experimental.pallas import tpu as pltpu
from jax.sharding import PartitionSpec as P

D = 512
HEADS = 8
HEAD_DIM = 64
FF = 2048
STEP = 10

norm_epsilon = 1e-05
momentum_keep = 0.5
quintic_lin = 3.4445
quintic_cube = -4.775
quintic_five = 2.0315
muon_rate = 0.7
muon_decay = 0.1
adam_rate = 0.2
beta_first = 0.9
beta_second = 0.999
adam_epsilon = 1e-08

CHUNK = 128
PAIR = 2 * HEAD_DIM
PAIRS = HEADS // 2
VMEM_BYTES = 60 * 1024 * 1024
low_type = jnp.bfloat16
wide_type = jnp.float32


def dot_nn(left, right):
    return lax.dot_general(left, right, (((1,), (0,)), ((), ())), preferred_element_type=wide_type)


def dot_nt(left, right):
    return lax.dot_general(left, right, (((1,), (1,)), ((), ())), preferred_element_type=wide_type)


def dot_tn(left, right):
    return lax.dot_general(left, right, (((0,), (0,)), ((), ())), preferred_element_type=wide_type)


def normalize(rows):
    center = rows - jnp.mean(rows, axis=-1, keepdims=True)
    spread = jnp.mean(center * center, axis=-1, keepdims=True)
    inverse = lax.rsqrt(spread + norm_epsilon)
    return center * inverse, inverse


def norm_back(grad_rows, normed, inverse, gain):
    grad_normed = grad_rows * gain
    mean_grad = jnp.mean(grad_normed, axis=-1, keepdims=True)
    mean_cross = jnp.mean(grad_normed * normed, axis=-1, keepdims=True)
    return inverse * (grad_normed - mean_grad - normed * mean_cross)


def project_kernel(x_ref, w_ref, ln_ref, q_ref, k_ref, v_ref, a_ref):
    normed, _ = normalize(x_ref[...].astype(wide_type))
    first = (normed * ln_ref[0:1, :] + ln_ref[1:2, :]).astype(low_type)
    q_ref[...] = dot_nn(first, w_ref[0]).astype(low_type)
    k_ref[...] = dot_nn(first, w_ref[1]).astype(low_type)
    v_ref[...] = dot_nn(first, w_ref[2]).astype(low_type)
    a_ref[...] = jnp.exp(dot_nn(first, w_ref[3])).astype(low_type)


def project(rows, weights, ln_params):
    count = rows.shape[0]
    block = 512
    row_spec = pl.BlockSpec((block, D), lambda i: (i, 0))
    return pl.pallas_call(
        project_kernel,
        grid=(count // block,),
        in_specs=[
            row_spec,
            pl.BlockSpec((4, D, D), lambda i: (0, 0, 0)),
            pl.BlockSpec((4, D), lambda i: (0, 0)),
        ],
        out_specs=[row_spec] * 4,
        out_shape=[jax.ShapeDtypeStruct((count, D), low_type)] * 4,
        compiler_params=pltpu.CompilerParams(vmem_limit_bytes=VMEM_BYTES),
        name="project",
    )(rows, weights, ln_params)


def lane_of(shape):
    return lax.broadcasted_iota(jnp.int32, shape, 1)


def row_of(shape):
    return lax.broadcasted_iota(jnp.int32, shape, 0)


def split_pair(pair, first_head):
    zero = jnp.zeros_like(pair)
    return jnp.concatenate(
        [jnp.where(first_head, pair, zero), jnp.where(first_head, zero, pair)], axis=0
    )


def head_reduce(values, first_head, op, neutral):
    left = op(jnp.where(first_head, values, neutral), axis=-1, keepdims=True)
    right = op(jnp.where(first_head, neutral, values), axis=-1, keepdims=True)
    return jnp.where(first_head, left, right)


def attend_kernel(
    q_ref, k_ref, v_ref, a_ref, att_ref, share_ref, logit_ref, total_ref, state_ref, state, carry
):
    seqs = q_ref.shape[0]

    @pl.when(pl.program_id(0) == 0)
    def _():
        state[...] = jnp.zeros_like(state)
        carry[...] = jnp.zeros_like(carry)

    first_head = lane_of((CHUNK, PAIR)) < HEAD_DIM
    causal = row_of((CHUNK, 2 * CHUNK)) >= lane_of((CHUNK, 2 * CHUNK)) % CHUNK
    same_head = (row_of((PAIR, 2 * PAIR)) // HEAD_DIM) == (
        (lane_of((PAIR, 2 * PAIR)) // HEAD_DIM) % 2
    )
    lower = (row_of((CHUNK, CHUNK)) >= lane_of((CHUNK, CHUNK))).astype(low_type)
    for seq in range(seqs):
        slot_all = a_ref[seq]
        total_all = dot_nn(lower, slot_all) + carry[seq]
        total_ref[seq] = total_all
        carry[seq] = total_all[CHUNK - 1 :, :]
        inv_all = 1.0 / total_all
        for pair in range(PAIRS):
            lanes = slice(pair * PAIR, (pair + 1) * PAIR)
            q = q_ref[seq, :, lanes] * low_type(HEAD_DIM**-0.5)
            k = k_ref[seq, :, lanes]
            v = v_ref[seq, :, lanes]
            a = a_ref[seq, :, lanes]
            inv = inv_all[:, lanes]
            a_two = split_pair(a, first_head)
            now = jnp.where(same_head, state[seq, pair], 0.0).astype(low_type)
            state_ref[0, seq, pair] = now
            scores = jnp.where(causal, dot_nt(q, split_pair(k, first_head)), 0.0).astype(low_type)
            numer = dot_nn(scores, a_two) + dot_nt(q, now[:, :PAIR])
            logit = numer * inv
            logit_ref[seq, :, lanes] = logit
            expo = jnp.exp(logit - head_reduce(logit, first_head, jnp.max, -jnp.inf))
            share = expo * (inv / head_reduce(expo, first_head, jnp.sum, 0.0))
            share = share.astype(low_type)
            share_ref[seq, :, lanes] = share
            mix = jnp.where(causal, dot_nt(share, a_two), 0.0).astype(low_type)
            att = dot_nn(mix, split_pair(v, first_head)) + dot_nn(share, now[:, PAIR:])
            att_ref[seq, :, lanes] = att.astype(low_type)
            state[seq, pair] += dot_tn(a, jnp.concatenate([k, v], axis=1))


def attend(q, k, v, a):
    seqs, length, _ = q.shape
    chunks = length // CHUNK
    block = pl.BlockSpec((seqs, CHUNK, D), lambda i: (0, i, 0))
    low_out = jax.ShapeDtypeStruct(q.shape, low_type)
    wide_out = jax.ShapeDtypeStruct(q.shape, wide_type)
    return pl.pallas_call(
        attend_kernel,
        grid=(chunks,),
        in_specs=[block] * 4,
        out_specs=[
            block,
            block,
            block,
            block,
            pl.BlockSpec((1, seqs, PAIRS, PAIR, 2 * PAIR), lambda i: (i, 0, 0, 0, 0)),
        ],
        out_shape=[
            low_out,
            low_out,
            wide_out,
            wide_out,
            jax.ShapeDtypeStruct((chunks, seqs, PAIRS, PAIR, 2 * PAIR), low_type),
        ],
        scratch_shapes=[
            pltpu.VMEM((seqs, PAIRS, PAIR, 2 * PAIR), wide_type),
            pltpu.VMEM((seqs, 1, D), wide_type),
        ],
        compiler_params=pltpu.CompilerParams(vmem_limit_bytes=VMEM_BYTES),
        name="attend",
    )(q, k, v, a)


def attend_back_kernel(
    q_ref,
    k_ref,
    v_ref,
    a_ref,
    share_ref,
    logit_ref,
    total_ref,
    datt_ref,
    state_ref,
    dq_ref,
    dk_ref,
    dv_ref,
    de_ref,
    state,
    carry,
):
    seqs = q_ref.shape[0]

    @pl.when(pl.program_id(0) == 0)
    def _():
        state[...] = jnp.zeros_like(state)
        carry[...] = jnp.zeros_like(carry)

    scaling = HEAD_DIM**-0.5
    first_head = lane_of((CHUNK, PAIR)) < HEAD_DIM
    causal = row_of((CHUNK, 2 * CHUNK)) >= lane_of((CHUNK, 2 * CHUNK)) % CHUNK
    anti = row_of((CHUNK, 2 * CHUNK)) <= lane_of((CHUNK, 2 * CHUNK)) % CHUNK
    same_head = (row_of((PAIR, 2 * PAIR)) // HEAD_DIM) == (
        (lane_of((PAIR, 2 * PAIR)) // HEAD_DIM) % 2
    )
    upper = (row_of((CHUNK, CHUNK)) <= lane_of((CHUNK, CHUNK))).astype(low_type)
    for seq in range(seqs):
        for pair in range(PAIRS):
            lanes = slice(pair * PAIR, (pair + 1) * PAIR)
            q = q_ref[seq, :, lanes] * low_type(scaling)
            k = k_ref[seq, :, lanes]
            v = v_ref[seq, :, lanes]
            a = a_ref[seq, :, lanes]
            share = share_ref[seq, :, lanes]
            logit = logit_ref[seq, :, lanes]
            total = total_ref[seq, :, lanes]
            datt = datt_ref[seq, :, lanes]
            inv = 1.0 / total
            before = state_ref[0, seq, pair]
            after = jnp.where(same_head, state[seq, pair], 0.0).astype(low_type)
            q_two = split_pair(q, first_head)
            k_two = split_pair(k, first_head)
            v_two = split_pair(v, first_head)
            a_two = split_pair(a, first_head)
            share_two = split_pair(share, first_head)
            datt_two = split_pair(datt, first_head)

            dmix = jnp.where(causal, dot_nt(datt, v_two), 0.0).astype(low_type)
            dshare = dot_nn(dmix, a_two) + dot_nt(datt, before[:, PAIR:])
            prob = share.astype(wide_type) * total
            dprob = dshare * inv
            dlogit = prob * (dprob - head_reduce(dprob * prob, first_head, jnp.sum, 0.0))
            dnumer = (dlogit * inv).astype(low_type)
            dtotal = -(dprob * prob + dlogit * logit) * inv
            dnumer_two = split_pair(dnumer, first_head)
            dscores = jnp.where(causal, dot_nt(dnumer, a_two), 0.0).astype(low_type)
            dq = (dot_nn(dscores, k_two) + dot_nn(dnumer, before[:, :PAIR])) * scaling
            dq_ref[seq, :, lanes] = dq.astype(low_type)

            mix_t = jnp.where(anti, dot_nt(a, share_two), 0.0).astype(low_type)
            dscores_t = jnp.where(anti, dot_nt(a, dnumer_two), 0.0).astype(low_type)
            dmix_t = jnp.where(anti, dot_nt(v, datt_two), 0.0).astype(low_type)
            scores_t = jnp.where(anti, dot_nt(k, q_two), 0.0).astype(low_type)
            later = dot_nn(a, after)
            dv = dot_nn(mix_t, datt_two) + later[:, PAIR:]
            dv_ref[seq, :, lanes] = dv.astype(low_type)
            dk = dot_nn(dscores_t, q_two) + later[:, :PAIR]
            dk_ref[seq, :, lanes] = dk.astype(low_type)

            dtotal_high = dtotal.astype(low_type)
            dtotal_low = (dtotal - dtotal_high.astype(wide_type)).astype(low_type)
            tail = (
                dot_nn(upper, dtotal_high)
                + dot_nn(upper, dtotal_low)
                + carry[seq, :, lanes]
            )
            carry[seq, :, lanes] = tail[0:1, :]
            da = (
                dot_nn(dmix_t, share_two)
                + dot_nn(scores_t, dnumer_two)
                + dot_nt(jnp.concatenate([k, v], axis=1), after)
                + tail
            )
            de = da.astype(low_type).astype(wide_type) * a.astype(wide_type)
            de_ref[seq, :, lanes] = de.astype(low_type)
            state[seq, pair, :, :PAIR] += dot_tn(dnumer, q)
            state[seq, pair, :, PAIR:] += dot_tn(share, datt)


def attend_back(q, k, v, a, share, logit, total, datt, states):
    seqs, length, _ = q.shape
    chunks = length // CHUNK
    block = pl.BlockSpec((seqs, CHUNK, D), lambda i: (0, chunks - 1 - i, 0))
    return pl.pallas_call(
        attend_back_kernel,
        grid=(chunks,),
        in_specs=[block] * 8
        + [
            pl.BlockSpec(
                (1, seqs, PAIRS, PAIR, 2 * PAIR), lambda i: (chunks - 1 - i, 0, 0, 0, 0)
            )
        ],
        out_specs=[block] * 4,
        out_shape=[jax.ShapeDtypeStruct(q.shape, low_type)] * 4,
        scratch_shapes=[
            pltpu.VMEM((seqs, PAIRS, PAIR, 2 * PAIR), wide_type),
            pltpu.VMEM((seqs, 1, D), wide_type),
        ],
        compiler_params=pltpu.CompilerParams(vmem_limit_bytes=VMEM_BYTES),
        name="attend_back",
    )(q, k, v, a, share, logit, total, datt, states)


FF_BLOCK = 512
gelu_root = math.sqrt(2.0 / math.pi)
gelu_cube = 0.044715


def feed_kernel(
    weight_ref,
    x_ref,
    att_ref,
    og_ref,
    wo_ref,
    ffn_ref,
    ln_ref,
    out_ref,
    dx_ref,
    datt_ref,
    gup_ref,
    gdown_ref,
    go_ref,
    gln_ref,
    up_sum,
    down_sum,
    o_sum,
    *,
    per_seq,
):
    step = pl.program_id(0)

    @pl.when(step == 0)
    def _():
        up_sum[...] = jnp.zeros_like(up_sum)
        down_sum[...] = jnp.zeros_like(down_sum)
        o_sum[...] = jnp.zeros_like(o_sum)
        gln_ref[...] = jnp.zeros_like(gln_ref)

    att = att_ref[...]
    mixed = x_ref[...].astype(wide_type) + dot_nn(att, wo_ref[...])
    normed, inverse = normalize(mixed)
    second = (normed * ln_ref[2:3, :] + ln_ref[3:4, :]).astype(low_type)
    dout = og_ref[...].astype(wide_type) * weight_ref[step // per_seq]
    dy = dout.astype(low_type)
    second_t = second.T
    dy_t = dy.T
    result = mixed
    dsecond = jnp.zeros_like(mixed)
    for part in range(FF // FF_BLOCK):
        rows = slice(part * FF_BLOCK, (part + 1) * FF_BLOCK)
        up = ffn_ref[0, rows, :]
        down = ffn_ref[1, rows, :]
        inner = dot_nt(second, up)
        square = inner * inner
        bend = jnp.tanh(inner * (gelu_root + (gelu_root * gelu_cube) * square))
        half = 0.5 + 0.5 * bend
        hidden = (inner * half).astype(low_type)
        slope = half + (0.5 * inner) * (1.0 - bend * bend) * (
            gelu_root + (3.0 * gelu_root * gelu_cube) * square
        )
        result = result + dot_nn(hidden, down)
        down_sum[:, rows] += dot_nn(dy_t, hidden)
        dinner = (dot_nt(dy, down) * slope).astype(low_type)
        up_sum[:, rows] += dot_nn(second_t, dinner)
        dsecond = dsecond + dot_nn(dinner, up)
    out_ref[...] = result.astype(low_type)
    gln_ref[0:1, :] += jnp.sum(dsecond * normed, axis=0, keepdims=True)
    gln_ref[1:2, :] += jnp.sum(dsecond, axis=0, keepdims=True)
    dmixed = dout + norm_back(dsecond, normed, inverse, ln_ref[2:3, :])
    dx_ref[...] = dmixed
    datt = dmixed.astype(low_type)
    o_sum[...] += dot_tn(att, datt)
    datt_ref[...] = dot_nt(datt, wo_ref[...]).astype(low_type)

    @pl.when(step == pl.num_programs(0) - 1)
    def _():
        gup_ref[...] = up_sum[...].astype(low_type)
        gdown_ref[...] = down_sum[...].astype(low_type)
        go_ref[...] = o_sum[...].astype(low_type)


def feed(seq_weight, rows, att, grad, wo, ffn, ln_params, length):
    count = rows.shape[0]
    block = 256
    row_spec = pl.BlockSpec((block, D), lambda i: (i, 0))

    def whole(*shape):
        return pl.BlockSpec(shape, lambda i: (0,) * len(shape))

    return pl.pallas_call(
        functools.partial(feed_kernel, per_seq=length // block),
        grid=(count // block,),
        in_specs=[
            pl.BlockSpec(memory_space=pltpu.SMEM),
            row_spec,
            row_spec,
            row_spec,
            whole(D, D),
            whole(2, FF, D),
            whole(4, D),
        ],
        out_specs=[
            row_spec,
            row_spec,
            row_spec,
            whole(D, FF),
            whole(D, FF),
            whole(D, D),
            whole(2, D),
        ],
        out_shape=[
            jax.ShapeDtypeStruct((count, D), low_type),
            jax.ShapeDtypeStruct((count, D), wide_type),
            jax.ShapeDtypeStruct((count, D), low_type),
            jax.ShapeDtypeStruct((D, FF), low_type),
            jax.ShapeDtypeStruct((D, FF), low_type),
            jax.ShapeDtypeStruct((D, D), low_type),
            jax.ShapeDtypeStruct((2, D), wide_type),
        ],
        scratch_shapes=[
            pltpu.VMEM((D, FF), wide_type),
            pltpu.VMEM((D, FF), wide_type),
            pltpu.VMEM((D, D), wide_type),
        ],
        compiler_params=pltpu.CompilerParams(vmem_limit_bytes=VMEM_BYTES),
        name="feed",
    )(seq_weight, rows, att, grad, wo, ffn, ln_params)


def project_back_kernel(
    x_ref,
    dx_ref,
    dq_ref,
    dk_ref,
    dv_ref,
    de_ref,
    w_ref,
    ln_ref,
    grad_ref,
    gw_ref,
    gln_ref,
    w_sum,
):
    step = pl.program_id(0)

    @pl.when(step == 0)
    def _():
        w_sum[...] = jnp.zeros_like(w_sum)
        gln_ref[...] = jnp.zeros_like(gln_ref)

    normed, inverse = normalize(x_ref[...].astype(wide_type))
    first_t = (normed * ln_ref[0:1, :] + ln_ref[1:2, :]).astype(low_type).T
    dfirst = jnp.zeros(normed.shape, wide_type)
    for place, ref in enumerate((dq_ref, dk_ref, dv_ref, de_ref)):
        part = ref[...]
        w_sum[place] += dot_nn(first_t, part)
        dfirst = dfirst + dot_nt(part, w_ref[place])
    gln_ref[0:1, :] += jnp.sum(dfirst * normed, axis=0, keepdims=True)
    gln_ref[1:2, :] += jnp.sum(dfirst, axis=0, keepdims=True)
    grad_ref[...] = dx_ref[...] + norm_back(dfirst, normed, inverse, ln_ref[0:1, :])

    @pl.when(step == pl.num_programs(0) - 1)
    def _():
        gw_ref[...] = w_sum[...].astype(low_type)


def project_back(rows, dx, dq, dk, dv, de, weights, ln_params):
    count = rows.shape[0]
    block = 256
    row_spec = pl.BlockSpec((block, D), lambda i: (i, 0))

    def whole(*shape):
        return pl.BlockSpec(shape, lambda i: (0,) * len(shape))

    return pl.pallas_call(
        project_back_kernel,
        grid=(count // block,),
        in_specs=[row_spec] * 6 + [whole(4, D, D), whole(4, D)],
        out_specs=[row_spec, whole(4, D, D), whole(2, D)],
        out_shape=[
            jax.ShapeDtypeStruct((count, D), wide_type),
            jax.ShapeDtypeStruct((4, D, D), low_type),
            jax.ShapeDtypeStruct((2, D), wide_type),
        ],
        scratch_shapes=[pltpu.VMEM((4, D, D), wide_type)],
        compiler_params=pltpu.CompilerParams(vmem_limit_bytes=VMEM_BYTES),
        name="project_back",
    )(rows, dx, dq, dk, dv, de, weights, ln_params)


def newton_poly(gram):
    scale = jnp.sqrt(jnp.trace(gram)) + 1e-07
    eye = jnp.eye(D, dtype=wide_type)
    gram_one = gram * (1.0 / (scale * scale))
    poly_one = quintic_lin * eye + quintic_cube * gram_one + quintic_five * (gram_one @ gram_one)
    gram_two = (gram_one @ poly_one) @ poly_one
    poly_two = quintic_lin * eye + quintic_cube * gram_two + quintic_five * (gram_two @ gram_two)
    return (poly_one @ poly_two) * (1.0 / scale)


def sum_rows(stack, rows_at):
    wide = lax.axis_size("wide")
    narrow = lax.axis_size("narrow")
    mats = stack.shape[0]
    share = D // narrow // wide
    parts = stack.reshape(mats, narrow, wide, share, D)
    parts = lax.psum_scatter(parts, "wide", scatter_dimension=2, tiled=False)
    parts = lax.psum_scatter(parts, "narrow", scatter_dimension=1, tiled=False)
    return lax.all_gather(parts, "wide", axis=1, tiled=True)


def shards(
    tokens,
    out_grad,
    group_ids,
    domain_weight,
    attn_w,
    ffn_w,
    attn_mom,
    ffn_mom,
    ln_params,
    ln_first,
    ln_second,
):
    local_seqs, length, _ = tokens.shape
    token_count = local_seqs * length
    wide = lax.axis_size("wide")
    narrow = lax.axis_size("narrow")
    member = (group_ids[:, None] == jnp.arange(domain_weight.shape[0])[None, :]).astype(jnp.int32)
    group_count = lax.psum(jnp.sum(member, axis=0), ("wide", "narrow"))
    chosen = member.astype(wide_type)
    weight_of = jnp.sum(chosen * domain_weight[None, :], axis=1)
    count_of = jnp.sum(chosen * group_count[None, :].astype(wide_type), axis=1)
    total_seqs = local_seqs * wide * narrow
    seq_weight = weight_of * total_seqs / (domain_weight.shape[0] * count_of)

    attn_low = lax.all_gather(attn_w.astype(low_type), "narrow", axis=1, tiled=True)
    ffn_low = lax.all_gather(ffn_w.astype(low_type), "narrow", axis=1, tiled=True)
    rows = tokens.reshape(token_count, D)
    in_w, out_w = attn_low[:4], attn_low[4]
    q, k, v, a = project(rows, in_w, ln_params)
    head = (local_seqs, length, D)
    q, k, v, a = (item.reshape(head) for item in (q, k, v, a))
    att, share, logit, total, states = attend(q, k, v, a)
    output, dx, datt, gup, gdown, go, gln_two = feed(
        seq_weight,
        rows,
        att.reshape(token_count, D),
        out_grad.reshape(token_count, D),
        out_w,
        ffn_low,
        ln_params,
        length,
    )
    dq, dk, dv, de = attend_back(q, k, v, a, share, logit, total, datt.reshape(head), states)
    dq, dk, dv, de = (item.reshape(token_count, D) for item in (dq, dk, dv, de))
    input_grad, gw, gln_one = project_back(rows, dx, dq, dk, dv, de, in_w, ln_params)

    attn_grad = sum_rows(jnp.concatenate([gw, go[None]], axis=0), None).astype(wide_type)
    ffn_t = jnp.stack([gup, gdown])
    ffn_t = lax.psum_scatter(ffn_t, "wide", scatter_dimension=1, tiled=True)
    ffn_t = lax.psum_scatter(ffn_t, "narrow", scatter_dimension=2, tiled=True)
    ffn_t = lax.all_gather(ffn_t, "wide", axis=1, tiled=True)
    ffn_grad = jnp.swapaxes(ffn_t, 1, 2).astype(wide_type)
    ln_full = jnp.concatenate([gln_one, gln_two], axis=0)
    ln_sum = lax.psum(ln_full, ("wide", "narrow"))
    shard_width = ln_first.shape[1]
    ln_grad = lax.dynamic_slice_in_dim(
        ln_sum, lax.axis_index("narrow") * shard_width, shard_width, 1
    )

    attn_moment = momentum_keep * attn_mom + attn_grad
    ffn_moment = momentum_keep * ffn_mom + ffn_grad
    mats = attn_w.shape[0] + ffn_w.shape[0]
    attn_rows = attn_w.shape[1]
    ffn_rows = ffn_w.shape[1]
    padded = jnp.concatenate(
        [
            jnp.pad(attn_moment.astype(low_type), ((0, 0), (0, ffn_rows - attn_rows), (0, 0))),
            ffn_moment.astype(low_type),
        ],
        axis=0,
    )
    mine = lax.dynamic_index_in_dim(
        padded, jnp.minimum(lax.axis_index("wide"), mats - 1), 0, keepdims=False
    )
    gram = lax.psum(dot_tn(mine, mine), "narrow")
    poly = lax.all_gather(newton_poly(gram).astype(low_type), "wide", axis=0, tiled=False)[:mats]
    attn_ortho = jnp.einsum(
        "jrd,jde->jre",
        attn_moment.astype(low_type),
        poly[: attn_w.shape[0]],
        preferred_element_type=wide_type,
    )
    ffn_ortho = jnp.einsum(
        "jrd,jde->jre",
        ffn_moment.astype(low_type),
        poly[attn_w.shape[0] :],
        preferred_element_type=wide_type,
    )
    keep_factor = 1.0 - muon_rate * muon_decay
    attn_new = keep_factor * attn_w - muon_rate * 0.2 * math.sqrt(D) * attn_ortho
    ffn_new = keep_factor * ffn_w - muon_rate * 0.2 * math.sqrt(FF) * ffn_ortho
    own_params = lax.dynamic_slice_in_dim(
        ln_params, lax.axis_index("narrow") * shard_width, shard_width, 1
    )
    first_new = beta_first * ln_first + (1.0 - beta_first) * ln_grad
    second_new = beta_second * ln_second + (1.0 - beta_second) * ln_grad * ln_grad
    first_fix = 1.0 - beta_first**STEP
    second_fix = 1.0 - beta_second**STEP
    ln_new = own_params - adam_rate * (first_new / first_fix) / (
        jnp.sqrt(second_new / second_fix) + adam_epsilon
    )
    return (
        output.reshape(tokens.shape),
        input_grad.reshape(tokens.shape),
        attn_grad,
        ffn_grad,
        ln_grad,
        attn_moment,
        ffn_moment,
        attn_new,
        ffn_new,
        attn_new.astype(low_type),
        ffn_new.astype(low_type),
        first_new,
        second_new,
        ln_new,
    )


def solution(mesh):
    split = P(("wide", "narrow"), None, None)
    rows = P(None, "narrow", None)
    lanes = P(None, "narrow")
    inner = jax.shard_map(
        shards,
        mesh=mesh,
        in_specs=(
            split,
            split,
            P(("wide", "narrow")),
            P(),
            rows,
            rows,
            rows,
            rows,
            P(),
            lanes,
            lanes,
        ),
        out_specs=(
            split,
            split,
            rows,
            rows,
            lanes,
            rows,
            rows,
            rows,
            rows,
            rows,
            rows,
            lanes,
            lanes,
            lanes,
        ),
        check_vma=False,
    )
    return inner
```

time: 1680 us -> 528 us (0.31); the launches traced: 1660 us -> 527 us
  waiting for transfers between devices: 746 us -> 184 us
  matrix products: 378 us -> 17.3 us
  local copies, waits for them, and re-layouts: 334 us -> 20.2 us
  Pallas kernels: 0 us -> 171 us
  other arithmetic: 85.4 us -> 23.8 us
  loops' own time: 29.5 us -> 0 us
  blocking collectives: 70.8 us -> 94.9 us
    psum x3 -> x1, waiting for transfers between devices: 530 us -> 52.1 us  [shards(): gram = lax.psum(dot_tn(mine, mine), 'narrow')]
    dot_general x74 -> x6, matrix products: 345 us -> 17.3 us  [the longest x1 3.85 us: newton_poly(): return poly_one @ poly_two * (1.0 / scale)]
    pallas_call x0 -> x5, Pallas kernels: none -> 171 us  [the longest x1 51.7 us: feed(): pl.pallas_call(functools.partial(feed_kernel, per_seq=length // block), g...]
    reduce_scatter x2 -> x4, waiting for transfers between devices: 212 us -> 83.1 us  [the longest x1 41.7 us: sum_rows(): parts = lax.psum_scatter(parts, 'wide', scatter_dimension=2, tiled=False)]
    dynamic_update_slice x14 -> x0, local copies, waits for them, and re-layouts: 95.1 us -> none  [the longest x8 86.8 us: attend_backward(): lax.scan(one_block, start_state, offsets)]
    while x181 -> x0, local copies, waits for them, and re-layouts: 60.3 us -> none
    convert_element_type x11 -> x1, local copies, waits for them, and re-layouts: 58.9 us -> 1.32 us  [shards(): ffn_moment.astype(low_type)]
    all_gather x2 -> x4, waiting for transfers between devices: 3.77 us -> 48.6 us  [the longest x1 25.8 us: shards(): lax.all_gather(ffn_w.astype(low_type), 'narrow', axis=1, tiled=True)]
  transfers between devices with their start and end apart: 8 -> 9, of which waited for: 6 -> 7; matrix products, arithmetic and copies ran while one was open for 18% -> 5% of each run, Pallas kernels for 0% -> 23%
where the time goes in v1:
time: 528 us; the launch traced here: 527 us
  waiting for transfers between devices  184 us (35%)
  Pallas kernels  171 us (32%)
  blocking collectives  94.9 us (18%)
  other arithmetic  23.8 us (5%)
  local copies, waits for them, and re-layouts  20.2 us (4%)
  matrix products  17.3 us (3%)
  between operations  14.8 us (3%)
    psum x1, waiting for transfers between devices, shards(): gram = lax.psum(dot_tn(mine, mine), 'narrow')  52.1 us
    pallas_call x1, Pallas kernels, feed(): pl.pallas_call(functools.partial(feed_kernel, per_seq=length // block), g...  51.7 us
    pallas_call x1, Pallas kernels, attend_back(): pl.pallas_call(attend_back_kernel, grid=(chunks,), in_specs=[block] * 8 +...  50.1 us
    psum x1, blocking collectives, shards(): group_count = lax.psum(jnp.sum(member, axis=0), ('wide', 'narrow'))  44.1 us
    pallas_call x1, Pallas kernels, attend(): pl.pallas_call(attend_kernel, grid=(chunks,), in_specs=[block] * 4, out_s...  42.3 us
    reduce_scatter x1, waiting for transfers between devices, sum_rows(): parts = lax.psum_scatter(parts, 'wide', scatter_dimension=2, tiled=False)  41.7 us
    psum x1, blocking collectives, shards(): ln_sum = lax.psum(ln_full, ('wide', 'narrow'))  40.4 us
    all_gather x1, waiting for transfers between devices, shards(): lax.all_gather(ffn_w.astype(low_type), 'narrow', axis=1, tiled=True)  25.8 us
  transfers between devices with their start and end apart: 9, of which 7 were waited for; matrix products, arithmetic and copies ran while one was open for 5% of the time, Pallas kernels for 23%

profile of v1, /device:TPU:0, one launch (start us, length us, event | category | flops | bytes accessed | tf_op | source)
XLA Modules:
  0.0 527.0 jit_solution(1812270038505184480)
XLA Ops:
  7.2 2.4 convert_element_type.48
  9.7 0.0 all-gather.9.cloned.1.call-start
  9.7 1.1 convert_element_type.49
  10.8 0.0 reduce-scatter.9.cloned.1.call-start
  10.9 0.1 fusion.28
  11.0 44.1 %psum.21 = s32[4]{0:T(128)S(1)} all-reduce(s32[4]{0:T(128)S(1)} %fusion.28), channel_id=1, replica_groups=mesh['wide'=8,'narrow'=4] {'wide','narrow'}, use_global_device_ids=true, to_apply=%region_2.0 | all-reduce | flops 4 | bytes 32 | tf_op jit(solution)/shard_map/psum | solution.py:536
  55.1 0.2 multiply_reduce_fusion.1
  55.3 0.5 multiply_divide_fusion.weight_ref
  55.8 12.8 %all-gather.7.cloned.1.call-done = bf16[5,512,512]{2,1,0:T(8,128)(2,1)} async-done(((bf16[5,128,512]{2,1,0:T(8,128)(2,1)}), bf16[5,512,512]{2,1,0:T(8,128)(2,1)}) %all-gather.7.cloned.1.call-update) | async-done | bytes 2621456 | tf_op jit(solution)/shard_map/all_gather | solution.py:543
  68.6 3.0 slice.21.w_ref
  71.6 8.8 %project.1 = (bf16[2048,512]{1,0:T(8,128)(2,1)}, bf16[2048,512]{1,0:T(8,128)(2,1)}, bf16[2048,512]{1,0:T(8,128)(2,1)}, bf16[2048,512]{1,0:T(8,128)(2,1)}) custom-call(bf16[2048,512]{1,0:T(8,128)(2,1)} %bitcast.44, bf16[4,512,512]{2,1,0:T(8,128)(2,1)} %slice.21.w_ref, f32[4,512]{1,0:T(4,128)} %ln_ref.5), custom_call_target="tpu_custom_call" | custom-call | tf_op jit(solution)/shard_map/project/pallas_call | solution.py:76
  80.4 42.3 %attend.1 = (bf16[2,1024,512]{2,1,0:T(8,128)(2,1)}, bf16[2,1024,512]{2,1,0:T(8,128)(2,1)}, f32[2,1024,512]{2,1,0:T(8,128)}, f32[2,1024,512]{2,1,0:T(8,128)}, bf16[8,2,4,128,256]{4,3,2,1,0:T(8,128)(2,1)}) custom-call(bf16[2,1024,512]{2,1,0:T(8,128)(2,1)} %bitcast.49, bf16[2,1024,512]{2,1,0:T(8,128)(2,1)} %bitcast.51, bf16[2,1024,512]{2,1,0:T(8,128)(2,1)} %bitcast.53, ...), custom_call_target="tpu_custom_call" | custom-call | tf_op jit(solution)/shard_map/attend/pallas_call | solution.py:164
  122.7 1.9 slice_bitcast_fusion.wo_ref
  124.6 25.8 %all-gather.9.cloned.1.call-done.ffn_ref = bf16[2,2048,512]{2,1,0:T(8,128)(2,1)} async-done(((bf16[2,512,512]{2,1,0:T(8,128)(2,1)}), bf16[2,2048,512]{2,1,0:T(8,128)(2,1)}) %all-gather.9.cloned.1.call-update) | async-done | bytes 4194320 | tf_op jit(solution)/shard_map/all_gather | solution.py:544
  150.3 51.7 %feed.1 = (bf16[2048,512]{1,0:T(8,128)(2,1)}, f32[2048,512]{1,0:T(8,128)}, bf16[2048,512]{1,0:T(8,128)(2,1)}, bf16[512,2048]{1,0:T(8,128)(2,1)}, bf16[512,2048]{...) custom-call(f32[2]{0:T(128)} %multiply_divide_fusion.weight_ref, bf16[2048,512]{1,0:T(8,128)(2,1)} %bitcast.45, ...), custom_call_target="tpu_custom_call" | custom-call | tf_op jit(solution)/shard_map/feed/pallas_call | solution.py:396
  202.0 4.6 pad_maximum_fusion
  206.6 0.2 reduce-scatter.5.cloned.1.call-start
  206.9 50.1 %attend_back.1 = (bf16[2,1024,512]{2,1,0:T(8,128)(2,1)}, bf16[2,1024,512]{2,1,0:T(8,128)(2,1)}, bf16[2,1024,512]{2,1,0:T(8,128)(2,1)}, bf16[2,1024,512]{2,1,0:T(8,128)(2,1)}) custom-call(bf16[2,1024,512]{2,1,0:T(8,128)(2,1)} %bitcast.50, bf16[2,1024,512]{2,1,0:T(8,128)(2,1)} %bitcast.52, bf16[2,1024,512]{2,1,0:T(8,128)(2,1)} %bitcast.54, ...), custom_call_target="tpu_custom_call" | custom-call | tf_op jit(solution)/shard_map/attend_back/pallas_call | solution.py:290
  257.0 18.2 %project_back.1 = (f32[2048,512]{1,0:T(8,128)}, bf16[4,512,512]{2,1,0:T(8,128)(2,1)}, f32[2,512]{1,0:T(2,128)}) custom-call(bf16[2048,512]{1,0:T(8,128)(2,1)} %bitcast.46, f32[2048,512]{1,0:T(8,128)} %get-tuple-element.43.dx_ref, bf16[2048,512]{1,0:T(8,128)(2,1)} %bitcast.63, bf16[2048,512]{1,0:T(8,128)(2,1)} %bitcast.64, bf16[2048,512]{1,0:T(8,128)(2,1)} %bitcast.65, ...), custom_call_target="tpu_custom_call" | custom-call | tf_op jit(solution)/shard_map/project_back/pallas_call | solution.py:481
  275.2 1.8 pad_maximum_fusion.1
  277.1 1.8 copy.40
  278.9 0.5 reduce-scatter.11.cloned.1.call-update
  279.5 41.7 %reduce-scatter.5.cloned.1.call-done = bf16[5,4,1,16,512]{4,3,0,1,2:T(8,128)(2,1)} async-done(((bf16[5,4,8,16,512]{4,3,0,1,2:T(8,128)(2,1)}), bf16[5,4,1,16,512]{4,3,0,1,2:T(8,128)(2,1)}) %reduce-scatter.5.cloned.1.call-update) | async-done | bytes 327696 | tf_op jit(solution)/shard_map/reduce_scatter | solution.py:513
  321.3 23.8 %reduce-scatter.11.cloned.1.call-done = bf16[2,64,512]{2,1,0:T(8,128)(2,1)} async-done(((bf16[2,64,2048]{2,1,0:T(8,128)(2,1)}), bf16[2,64,512]{2,1,0:T(8,128)(2,1)}) %reduce-scatter.11.cloned.1.call-update) | async-done | bytes 131088 | tf_op jit(solution)/shard_map/reduce_scatter | solution.py:568
  345.2 2.9 copy.34
  348.0 17.6 %reduce-scatter.7.cloned.1.call-done = bf16[5,1,16,512]{3,2,0,1:T(8,128)(2,1)} async-done(((bf16[5,4,16,512]{3,2,0,1:T(8,128)(2,1)}), bf16[5,1,16,512]{3,2,0,1:T(8,128)(2,1)}) %reduce-scatter.7.cloned.1.call-update) | async-done | bytes 81936 | tf_op jit(solution)/shard_map/reduce_scatter | solution.py:514
  365.6 10.4 %all-gather = bf16[5,1,128,512]{3,2,0,1:T(8,128)(2,1)S(1)} all-gather(bf16[5,1,16,512]{3,2,0,1:T(8,128)(2,1)} %reduce-scatter.7.cloned.1.call-done), channel_id=2, replica_groups=mesh['wide'=8,'narrow'=4] {'wide'}, dimensions={2}, use_global_device_ids=true | all-gather | bytes 737280 | tf_op jit(solution)/shard_map/all_gather | solution.py:515
  376.0 3.5 fusion.38
  379.5 10.0 %all-gather.11.cloned.1.call-done = bf16[2,512,512]{2,1,0:T(8,128)(2,1)} async-done(((bf16[2,64,512]{2,1,0:T(8,128)(2,1)}), bf16[2,512,512]{2,1,0:T(8,128)(2,1)}) %all-gather.11.cloned.1.call-update) | async-done | bytes 1048592 | tf_op jit(solution)/shard_map/all_gather | solution.py:569
  389.5 3.6 fusion.37
  393.1 1.3 copy.35
  394.4 2.5 fusion.14
  397.0 52.1 %all-reduce.3.cloned.1.call-done = f32[512,512]{1,0:T(8,128)} async-done(((f32[512,512]{1,0:T(8,128)}), f32[512,512]{1,0:T(8,128)}) %all-reduce.3.cloned.1.call-update) | async-done | bytes 1048592 | tf_op jit(solution)/shard_map/psum | solution.py:593
  449.1 1.9 select_reduce_fusion
  451.8 3.3 fusion.5
  455.2 3.2 fusion.2
  458.4 3.8 fusion.6
  462.3 40.4 %psum.22 = f32[4,512]{1,0:T(4,128)S(1)} all-reduce(f32[4,512]{1,0:T(4,128)S(1)} %pad_maximum_fusion.2), channel_id=1, replica_groups=mesh['wide'=8,'narrow'=4] {'wide','narrow'}, use_global_device_ids=true, to_apply=%region_8.0 | all-reduce | flops 2048 | bytes 16384 | tf_op jit(solution)/shard_map/psum | solution.py:572
  502.7 1.3 divide_subtract_fusion
  504.0 2.9 copy.38
  506.9 2.8 convert_bitcast_fusion
  509.7 2.9 copy.37
  512.6 1.2 slice-done
  513.8 2.5 fusion.40
  516.3 1.7 slice-done.1
  518.1 0.4 copy-done.1
  518.4 0.2 copy-done.2
  518.6 1.8 fusion.39
  (38 shorter events, 0.4 us)
Async XLA Ops:
  7.2 2.5 copy-start
  7.2 61.4 %all-gather.7.cloned.1.call-start = ((), (), s32[]{:S(2)}) async-start(), calls=%async_computation.4 | async-start | bytes 3276800 | tf_op jit(solution)/shard_map/all_gather | solution.py:543
  9.6 1.3 copy-start.9
  9.6 45.5 %copy-start.8 = (f32[4]{0:T(128)S(1)}, f32[4]{0:T(128)}, u32[]{:S(2)}) copy-start(f32[4]{0:T(128)} %param.14) | copy-start | bytes 52
  9.7 140.7 %all-gather.9.cloned.1.call-start = ((), (), s32[]{:S(2)}) async-start(), calls=%async_computation.5 | async-start | bytes 5242880 | tf_op jit(solution)/shard_map/all_gather | solution.py:544
  10.8 268.0 %reduce-scatter.9.cloned.1.call-start = ((), (), s32[]{:S(2)}) async-start(), calls=%async_computation.8 | async-start | bytes 4718592 | tf_op jit(solution)/shard_map/reduce_scatter | solution.py:567
  206.6 114.6 %reduce-scatter.5.cloned.1.call-start = ((), (), s32[]{:S(2)}) async-start(), calls=%async_computation.6 | async-start | bytes 2949120 | tf_op jit(solution)/shard_map/reduce_scatter | solution.py:513
  257.0 18.3 %copy-start.3 = (bf16[512,512]{1,0:T(8,128)(2,1)S(1)}, bf16[512,512]{1,0:T(8,128)(2,1)}, u32[]{:S(2)}) copy-start(bf16[512,512]{1,0:T(8,128)(2,1)} %get-tuple-element.55) | copy-start | bytes 1572868
  278.8 66.2 %reduce-scatter.11.cloned.1.call-start = ((), (), s32[]{:S(2)}) async-start(), calls=%async_computation.9 | async-start | bytes 655360 | tf_op jit(solution)/shard_map/reduce_scatter | solution.py:568
  279.4 86.2 %reduce-scatter.7.cloned.1.call-start = ((), (), s32[]{:S(2)}) async-start(), calls=%async_computation.7 | async-start | bytes 409600 | tf_op jit(solution)/shard_map/reduce_scatter | solution.py:514
  321.2 68.2 %all-gather.11.cloned.1.call-start = ((), (), s32[]{:S(2)}) async-start(), calls=%async_computation.10 | async-start | bytes 1179648 | tf_op jit(solution)/shard_map/all_gather | solution.py:569
  345.1 104.0 %all-reduce.3.cloned.1.call-start = ((), (), s32[]{:S(2)}) async-start(), calls=%async_computation.11 | async-start | bytes 2097152 | tf_op jit(solution)/shard_map/psum | solution.py:593
  397.0 115.6 %all-gather.13.cloned.1.call-start = ((), (), s32[]{:S(2)}) async-start(), calls=%async_computation.12 | async-start | bytes 4718592 | tf_op jit(solution)/shard_map/all_gather | solution.py:594
  458.4 3.9 copy-start.4
  458.4 3.9 copy-start.5
  458.4 44.3 %copy-start.6 = (f32[4,128]{1,0:T(4,128)S(1)}, f32[4,128]{1,0:T(4,128)}, u32[]{:S(2)}) copy-start(f32[4,128]{1,0:T(4,128)} %param.21) | copy-start | bytes 6148
  458.4 44.3 %copy-start.7 = (f32[4,128]{1,0:T(4,128)S(1)}, f32[4,128]{1,0:T(4,128)}, u32[]{:S(2)}) copy-start(f32[4,128]{1,0:T(4,128)} %param.20) | copy-start | bytes 6148
  512.6 1.2 slice-start
  516.3 1.7 slice-start.1
  516.3 2.1 copy-start.1
  516.3 2.3 copy-start.2
Sparse Core Ops, SparseCore 0:
  10.2 58.3 all-gather.6
  70.7 79.5 all-gather.8
  206.8 49.9 reduce-scatter.8
  279.0 42.2 reduce-scatter.4
  323.4 21.5 reduce-scatter.10
  347.3 18.2 reduce-scatter.6
  367.7 21.7 all-gather.10
  397.1 52.0 all-reduce.2
  462.4 36.3 all-gather.12

commit v2 on v1

--- a/solution.py
+++ b/solution.py
@@ -60,34 +60,6 @@
     return inverse * (grad_normed - mean_grad - normed * mean_cross)
 
 
-def project_kernel(x_ref, w_ref, ln_ref, q_ref, k_ref, v_ref, a_ref):
-    normed, _ = normalize(x_ref[...].astype(wide_type))
-    first = (normed * ln_ref[0:1, :] + ln_ref[1:2, :]).astype(low_type)
-    q_ref[...] = dot_nn(first, w_ref[0]).astype(low_type)
-    k_ref[...] = dot_nn(first, w_ref[1]).astype(low_type)
-    v_ref[...] = dot_nn(first, w_ref[2]).astype(low_type)
-    a_ref[...] = jnp.exp(dot_nn(first, w_ref[3])).astype(low_type)
-
-
-def project(rows, weights, ln_params):
-    count = rows.shape[0]
-    block = 512
-    row_spec = pl.BlockSpec((block, D), lambda i: (i, 0))
-    return pl.pallas_call(
-        project_kernel,
-        grid=(count // block,),
-        in_specs=[
-            row_spec,
-            pl.BlockSpec((4, D, D), lambda i: (0, 0, 0)),
-            pl.BlockSpec((4, D), lambda i: (0, 0)),
-        ],
-        out_specs=[row_spec] * 4,
-        out_shape=[jax.ShapeDtypeStruct((count, D), low_type)] * 4,
-        compiler_params=pltpu.CompilerParams(vmem_limit_bytes=VMEM_BYTES),
-        name="project",
-    )(rows, weights, ln_params)
-
-
 def lane_of(shape):
     return lax.broadcasted_iota(jnp.int32, shape, 1)
 
@@ -107,85 +79,6 @@
     left = op(jnp.where(first_head, values, neutral), axis=-1, keepdims=True)
     right = op(jnp.where(first_head, neutral, values), axis=-1, keepdims=True)
     return jnp.where(first_head, left, right)
-
-
-def attend_kernel(
-    q_ref, k_ref, v_ref, a_ref, att_ref, share_ref, logit_ref, total_ref, state_ref, state, carry
-):
-    seqs = q_ref.shape[0]
-
-    @pl.when(pl.program_id(0) == 0)
-    def _():
-        state[...] = jnp.zeros_like(state)
-        carry[...] = jnp.zeros_like(carry)
-
-    first_head = lane_of((CHUNK, PAIR)) < HEAD_DIM
-    causal = row_of((CHUNK, 2 * CHUNK)) >= lane_of((CHUNK, 2 * CHUNK)) % CHUNK
-    same_head = (row_of((PAIR, 2 * PAIR)) // HEAD_DIM) == (
-        (lane_of((PAIR, 2 * PAIR)) // HEAD_DIM) % 2
-    )
-    lower = (row_of((CHUNK, CHUNK)) >= lane_of((CHUNK, CHUNK))).astype(low_type)
-    for seq in range(seqs):
-        slot_all = a_ref[seq]
-        total_all = dot_nn(lower, slot_all) + carry[seq]
-        total_ref[seq] = total_all
-        carry[seq] = total_all[CHUNK - 1 :, :]
-        inv_all = 1.0 / total_all
-        for pair in range(PAIRS):
-            lanes = slice(pair * PAIR, (pair + 1) * PAIR)
-            q = q_ref[seq, :, lanes] * low_type(HEAD_DIM**-0.5)
-            k = k_ref[seq, :, lanes]
-            v = v_ref[seq, :, lanes]
-            a = a_ref[seq, :, lanes]
-            inv = inv_all[:, lanes]
-            a_two = split_pair(a, first_head)
-            now = jnp.where(same_head, state[seq, pair], 0.0).astype(low_type)
-            state_ref[0, seq, pair] = now
-            scores = jnp.where(causal, dot_nt(q, split_pair(k, first_head)), 0.0).astype(low_type)
-            numer = dot_nn(scores, a_two) + dot_nt(q, now[:, :PAIR])
-            logit = numer * inv
-            logit_ref[seq, :, lanes] = logit
-            expo = jnp.exp(logit - head_reduce(logit, first_head, jnp.max, -jnp.inf))
-            share = expo * (inv / head_reduce(expo, first_head, jnp.sum, 0.0))
-            share = share.astype(low_type)
-            share_ref[seq, :, lanes] = share
-            mix = jnp.where(causal, dot_nt(share, a_two), 0.0).astype(low_type)
-            att = dot_nn(mix, split_pair(v, first_head)) + dot_nn(share, now[:, PAIR:])
-            att_ref[seq, :, lanes] = att.astype(low_type)
-            state[seq, pair] += dot_tn(a, jnp.concatenate([k, v], axis=1))
-
-
-def attend(q, k, v, a):
-    seqs, length, _ = q.shape
-    chunks = length // CHUNK
-    block = pl.BlockSpec((seqs, CHUNK, D), lambda i: (0, i, 0))
-    low_out = jax.ShapeDtypeStruct(q.shape, low_type)
-    wide_out = jax.ShapeDtypeStruct(q.shape, wide_type)
-    return pl.pallas_call(
-        attend_kernel,
-        grid=(chunks,),
-        in_specs=[block] * 4,
-        out_specs=[
-            block,
-            block,
-            block,
-            block,
-            pl.BlockSpec((1, seqs, PAIRS, PAIR, 2 * PAIR), lambda i: (i, 0, 0, 0, 0)),
-        ],
-        out_shape=[
-            low_out,
-            low_out,
-            wide_out,
-            wide_out,
-            jax.ShapeDtypeStruct((chunks, seqs, PAIRS, PAIR, 2 * PAIR), low_type),
-        ],
-        scratch_shapes=[
-            pltpu.VMEM((seqs, PAIRS, PAIR, 2 * PAIR), wide_type),
-            pltpu.VMEM((seqs, 1, D), wide_type),
-        ],
-        compiler_params=pltpu.CompilerParams(vmem_limit_bytes=VMEM_BYTES),
-        name="attend",
-    )(q, k, v, a)
 
 
 def attend_back_kernel(
@@ -313,6 +206,7 @@
 
 
 def feed_kernel(
+    ids_ref,
     weight_ref,
     x_ref,
     att_ref,
@@ -346,7 +240,9 @@
     mixed = x_ref[...].astype(wide_type) + dot_nn(att, wo_ref[...])
     normed, inverse = normalize(mixed)
     second = (normed * ln_ref[2:3, :] + ln_ref[3:4, :]).astype(low_type)
-    dout = og_ref[...].astype(wide_type) * weight_ref[step // per_seq]
+    mine = lane_of((1, LANES)) == ids_ref[step // per_seq]
+    weight = jnp.sum(jnp.where(mine, weight_ref[0:1, :], 0.0), axis=1, keepdims=True)
+    dout = og_ref[...].astype(wide_type) * weight
     dy = dout.astype(low_type)
     second_t = second.T
     dy_t = dy.T
@@ -385,7 +281,7 @@
         go_ref[...] = o_sum[...].astype(low_type)
 
 
-def feed(seq_weight, rows, att, grad, wo, ffn, ln_params, length):
+def feed(ids, weights, rows, att, grad, wo, ffn, ln_params, length):
     count = rows.shape[0]
     block = 256
     row_spec = pl.BlockSpec((block, D), lambda i: (i, 0))
@@ -398,6 +294,7 @@
         grid=(count // block,),
         in_specs=[
             pl.BlockSpec(memory_space=pltpu.SMEM),
+            whole(8, LANES),
             row_spec,
             row_spec,
             row_spec,
@@ -430,7 +327,7 @@
         ],
         compiler_params=pltpu.CompilerParams(vmem_limit_bytes=VMEM_BYTES),
         name="feed",
-    )(seq_weight, rows, att, grad, wo, ffn, ln_params)
+    )(ids, weights, rows, att, grad, wo, ffn, ln_params)
 
 
 def project_back_kernel(
@@ -492,6 +389,361 @@
         compiler_params=pltpu.CompilerParams(vmem_limit_bytes=VMEM_BYTES),
         name="project_back",
     )(rows, dx, dq, dk, dv, de, weights, ln_params)
+
+
+MESH = pl.DeviceIdType.MESH
+LANES = 128
+
+
+def remote(src, dst, send_sem, recv_sem, device):
+    return pltpu.make_async_remote_copy(
+        src_ref=src,
+        dst_ref=dst,
+        send_sem=send_sem,
+        recv_sem=recv_sem,
+        device_id=device,
+        device_id_type=MESH,
+    )
+
+
+def greet(devices):
+    barrier = pltpu.get_barrier_semaphore()
+    for device in devices:
+        pl.semaphore_signal(barrier, inc=1, device_id=device, device_id_type=MESH)
+    pl.semaphore_wait(barrier, len(devices))
+
+
+def attend_chunk(q_all, k_all, v_all, a_all, consts, refs, seq):
+    first_head, causal, same_head, lower = consts
+    att_ref, share_ref, logit_ref, total_ref, state_ref, state, carry = refs
+    total_all = dot_nn(lower, a_all) + carry[seq]
+    total_ref[seq] = total_all
+    carry[seq] = total_all[CHUNK - 1 :, :]
+    inv_all = 1.0 / total_all
+    for pair in range(PAIRS):
+        lanes = slice(pair * PAIR, (pair + 1) * PAIR)
+        q = q_all[:, lanes] * low_type(HEAD_DIM**-0.5)
+        k = k_all[:, lanes]
+        v = v_all[:, lanes]
+        a = a_all[:, lanes]
+        inv = inv_all[:, lanes]
+        a_two = split_pair(a, first_head)
+        now = jnp.where(same_head, state[seq, pair], 0.0).astype(low_type)
+        state_ref[0, seq, pair] = now
+        scores = jnp.where(causal, dot_nt(q, split_pair(k, first_head)), 0.0).astype(low_type)
+        numer = dot_nn(scores, a_two) + dot_nt(q, now[:, :PAIR])
+        logit = numer * inv
+        logit_ref[seq, :, lanes] = logit
+        expo = jnp.exp(logit - head_reduce(logit, first_head, jnp.max, -jnp.inf))
+        share = expo * (inv / head_reduce(expo, first_head, jnp.sum, 0.0))
+        share = share.astype(low_type)
+        share_ref[seq, :, lanes] = share
+        mix = jnp.where(causal, dot_nt(share, a_two), 0.0).astype(low_type)
+        att = dot_nn(mix, split_pair(v, first_head)) + dot_nn(share, now[:, PAIR:])
+        att_ref[seq, :, lanes] = att.astype(low_type)
+        state[seq, pair] += dot_tn(a, jnp.concatenate([k, v], axis=1))
+
+
+def forward_kernel(
+    ids_ref,
+    dw_ref,
+    x_ref,
+    ln_ref,
+    attn_ref,
+    ffn_ref,
+    q_ref,
+    k_ref,
+    v_ref,
+    a_ref,
+    att_ref,
+    share_ref,
+    logit_ref,
+    total_ref,
+    state_ref,
+    weight_ref,
+    in_hbm,
+    out_hbm,
+    ffn_hbm,
+    state,
+    carry,
+    in_w,
+    own,
+    own_ffn,
+    counts,
+    counts_z,
+    counts_w,
+    in_send,
+    in_recv,
+    in_pass,
+    in_got,
+    ffn_send,
+    ffn_recv,
+    ffn_pass,
+    ffn_got,
+    out_send,
+    out_recv,
+    out_pass,
+    out_got,
+    cz_send,
+    cz_recv,
+    cw_send,
+    cw_recv,
+    local_sems,
+    *,
+    wide,
+    narrow,
+    total_seqs,
+    groups,
+):
+    step = pl.program_id(0)
+    steps = pl.num_programs(0)
+    seqs = x_ref.shape[0]
+    w = lax.axis_index("wide")
+    z = lax.axis_index("narrow")
+    core = lax.rem(w, 2)
+    mate = (w + 1 - 2 * core, z)
+    other = 1 - core
+    rows = attn_ref.shape[1]
+    ffn_rows = ffn_ref.shape[1]
+    half = rows // 2
+    hops = list(range(1, narrow))
+    hops.sort(key=lambda hop: min(hop, narrow - hop))
+    column = [(w, lax.rem(z + hop, narrow)) for hop in hops]
+    plane = [(lax.rem(w + hop, wide), z) for hop in range(1, wide)]
+
+    def at(owner, size):
+        return pl.ds(pl.multiple_of(owner * size, size), size)
+
+    def from_z(place):
+        return lax.rem(z + narrow - hops[place], narrow)
+
+    def half_at(owner, part):
+        start = owner * rows + part * half
+        return pl.ds(pl.multiple_of(start, half), half)
+
+    def in_out(place):
+        return remote(
+            own.at[pl.ds(2 * core, 2)],
+            in_w.at[pl.ds(2 * core, 2), at(z, rows)],
+            in_send.at[place],
+            in_recv.at[place],
+            column[place],
+        )
+
+    def in_on(place):
+        block = in_w.at[pl.ds(2 * core, 2), at(from_z(place), rows)]
+        return remote(block, block, in_pass.at[place], in_got.at[place], mate)
+
+    def ffn_out(place):
+        return remote(
+            own_ffn.at[core],
+            ffn_hbm.at[core, at(z, ffn_rows)],
+            ffn_send.at[place],
+            ffn_recv.at[place],
+            column[place],
+        )
+
+    def ffn_on(place):
+        block = ffn_hbm.at[core, at(from_z(place), ffn_rows)]
+        return remote(block, block, ffn_pass.at[place], ffn_got.at[place], mate)
+
+    def out_out(place):
+        return remote(
+            own.at[4, pl.ds(pl.multiple_of(core * half, half), half)],
+            out_hbm.at[half_at(z, core)],
+            out_send.at[place],
+            out_recv.at[place],
+            column[place],
+        )
+
+    def out_on(place):
+        block = out_hbm.at[half_at(from_z(place), core)]
+        return remote(block, block, out_pass.at[place], out_got.at[place], mate)
+
+    def count_z(place):
+        return remote(
+            counts, counts_z.at[place], cz_send.at[place], cz_recv.at[place], column[place]
+        )
+
+    def count_w(place):
+        return remote(
+            counts, counts_w.at[place], cw_send.at[place], cw_recv.at[place], plane[place]
+        )
+
+    keep_ffn = pltpu.make_async_copy(own_ffn, ffn_hbm.at[:, at(z, ffn_rows)], local_sems.at[0])
+    keep_out = pltpu.make_async_copy(own.at[4], out_hbm.at[at(z, rows)], local_sems.at[1])
+    keep_in = pltpu.make_async_copy(in_w, in_hbm, local_sems.at[2])
+
+    @pl.when(step == 0)
+    def _():
+        state[...] = jnp.zeros_like(state)
+        carry[...] = jnp.zeros_like(carry)
+        own[...] = attn_ref[...].astype(low_type)
+        greet(column + plane)
+        for place in range(narrow - 1):
+            in_out(place).start()
+        for place in range(4):
+            in_w[place, at(z, rows), :] = own[place]
+        own_ffn[...] = ffn_ref[...].astype(low_type)
+        lanes = lane_of((8, LANES))
+        count = jnp.zeros((8, LANES), wide_type)
+        for seq in range(seqs):
+            count = count + (lanes == ids_ref[seq]).astype(wide_type)
+        counts[...] = count
+        for place in range(narrow - 1):
+            in_out(place).wait_recv()
+            in_on(place).start()
+        for place in range(narrow - 1):
+            count_z(place).start()
+            ffn_out(place).start()
+            out_out(place).start()
+        keep_ffn.start()
+        keep_out.start()
+        for place in range(narrow - 1):
+            in_on(place).wait_recv()
+        keep_in.start()
+
+    @pl.when(step == 1)
+    def _():
+        for place in range(narrow - 1):
+            count_z(place).wait()
+        total = counts[...]
+        for place in range(narrow - 1):
+            total = total + counts_z[place]
+        counts[...] = total
+        for place in range(wide - 1):
+            count_w(place).start()
+
+    @pl.when(step == 2)
+    def _():
+        for place in range(wide - 1):
+            count_w(place).wait()
+        total = counts[...]
+        for place in range(wide - 1):
+            total = total + counts_w[place]
+        lanes = lane_of((8, LANES))
+        values = jnp.zeros((8, LANES), wide_type)
+        for group in range(groups):
+            values = values + jnp.where(lanes == group, dw_ref[group], 0.0)
+        weight_ref[...] = values * total_seqs / (groups * jnp.maximum(total, 1.0))
+
+    @pl.when(step == steps - 3)
+    def _():
+        for place in range(narrow - 1):
+            out_out(place).wait_recv()
+            out_on(place).start()
+            ffn_out(place).wait_recv()
+            ffn_on(place).start()
+
+    first_head = lane_of((CHUNK, PAIR)) < HEAD_DIM
+    causal = row_of((CHUNK, 2 * CHUNK)) >= lane_of((CHUNK, 2 * CHUNK)) % CHUNK
+    same_head = (row_of((PAIR, 2 * PAIR)) // HEAD_DIM) == (
+        (lane_of((PAIR, 2 * PAIR)) // HEAD_DIM) % 2
+    )
+    lower = (row_of((CHUNK, CHUNK)) >= lane_of((CHUNK, CHUNK))).astype(low_type)
+    normed, _ = normalize(x_ref[...].reshape(seqs * CHUNK, D).astype(wide_type))
+    first = (normed * ln_ref[0:1, :] + ln_ref[1:2, :]).astype(low_type)
+    q_all = dot_nn(first, in_w[0]).astype(low_type)
+    k_all = dot_nn(first, in_w[1]).astype(low_type)
+    v_all = dot_nn(first, in_w[2]).astype(low_type)
+    a_all = jnp.exp(dot_nn(first, in_w[3])).astype(low_type)
+    q_ref[...] = q_all.reshape(q_ref.shape)
+    k_ref[...] = k_all.reshape(q_ref.shape)
+    v_ref[...] = v_all.reshape(q_ref.shape)
+    a_ref[...] = a_all.reshape(q_ref.shape)
+    for seq in range(seqs):
+        part = slice(seq * CHUNK, (seq + 1) * CHUNK)
+        attend_chunk(
+            q_all[part],
+            k_all[part],
+            v_all[part],
+            a_all[part],
+            (first_head, causal, same_head, lower),
+            (att_ref, share_ref, logit_ref, total_ref, state_ref, state, carry),
+            seq,
+        )
+
+    @pl.when(step == steps - 1)
+    def _():
+        keep_ffn.wait()
+        keep_out.wait()
+        keep_in.wait()
+        for place in range(narrow - 1):
+            in_out(place).wait_send()
+            in_on(place).wait_send()
+            out_out(place).wait_send()
+            out_on(place).wait()
+            ffn_out(place).wait_send()
+            ffn_on(place).wait()
+
+
+def forward(tokens, ids, dw, ln_params, attn_w, ffn_w):
+    seqs, length, _ = tokens.shape
+    chunks = length // CHUNK
+    wide = lax.axis_size("wide")
+    narrow = lax.axis_size("narrow")
+    block = pl.BlockSpec((seqs, CHUNK, D), lambda i: (0, i, 0))
+    low_out = jax.ShapeDtypeStruct(tokens.shape, low_type)
+    wide_out = jax.ShapeDtypeStruct(tokens.shape, wide_type)
+    any_spec = pl.BlockSpec(memory_space=pl.ANY)
+    near, far = (narrow - 1,), (wide - 1,)
+
+    def whole(*shape):
+        return pl.BlockSpec(shape, lambda i: (0,) * len(shape))
+
+    return pl.pallas_call(
+        functools.partial(
+            forward_kernel,
+            wide=wide,
+            narrow=narrow,
+            total_seqs=seqs * wide * narrow,
+            groups=dw.shape[0],
+        ),
+        grid=(chunks,),
+        in_specs=[
+            pl.BlockSpec(memory_space=pltpu.SMEM),
+            pl.BlockSpec(memory_space=pltpu.SMEM),
+            block,
+            whole(4, D),
+            whole(*attn_w.shape),
+            whole(*ffn_w.shape),
+        ],
+        out_specs=[block] * 8
+        + [
+            pl.BlockSpec((1, seqs, PAIRS, PAIR, 2 * PAIR), lambda i: (i, 0, 0, 0, 0)),
+            whole(8, LANES),
+            any_spec,
+            any_spec,
+            any_spec,
+        ],
+        out_shape=[low_out] * 6
+        + [
+            wide_out,
+            wide_out,
+            jax.ShapeDtypeStruct((chunks, seqs, PAIRS, PAIR, 2 * PAIR), low_type),
+            jax.ShapeDtypeStruct((8, LANES), wide_type),
+            jax.ShapeDtypeStruct((4, D, D), low_type),
+            jax.ShapeDtypeStruct((D, D), low_type),
+            jax.ShapeDtypeStruct((2, FF, D), low_type),
+        ],
+        scratch_shapes=[
+            pltpu.VMEM((seqs, PAIRS, PAIR, 2 * PAIR), wide_type),
+            pltpu.VMEM((seqs, 1, D), wide_type),
+            pltpu.VMEM((4, D, D), low_type),
+            pltpu.VMEM(attn_w.shape, low_type),
+            pltpu.VMEM(ffn_w.shape, low_type),
+            pltpu.VMEM((8, LANES), wide_type),
+            pltpu.VMEM((narrow - 1, 8, LANES), wide_type),
+            pltpu.VMEM((wide - 1, 8, LANES), wide_type),
+        ]
+        + [pltpu.SemaphoreType.DMA(near)] * 14
+        + [pltpu.SemaphoreType.DMA(far)] * 2
+        + [pltpu.SemaphoreType.DMA((3,))],
+        compiler_params=pltpu.CompilerParams(
+            vmem_limit_bytes=VMEM_BYTES, collective_id=0, has_side_effects=True
+        ),
+        name="forward",
+    )(ids, dw, tokens, ln_params, attn_w, ffn_w)
 
 
 def newton_poly(gram):
@@ -532,24 +784,14 @@
     token_count = local_seqs * length
     wide = lax.axis_size("wide")
     narrow = lax.axis_size("narrow")
-    member = (group_ids[:, None] == jnp.arange(domain_weight.shape[0])[None, :]).astype(jnp.int32)
-    group_count = lax.psum(jnp.sum(member, axis=0), ("wide", "narrow"))
-    chosen = member.astype(wide_type)
-    weight_of = jnp.sum(chosen * domain_weight[None, :], axis=1)
-    count_of = jnp.sum(chosen * group_count[None, :].astype(wide_type), axis=1)
-    total_seqs = local_seqs * wide * narrow
-    seq_weight = weight_of * total_seqs / (domain_weight.shape[0] * count_of)
-
-    attn_low = lax.all_gather(attn_w.astype(low_type), "narrow", axis=1, tiled=True)
-    ffn_low = lax.all_gather(ffn_w.astype(low_type), "narrow", axis=1, tiled=True)
     rows = tokens.reshape(token_count, D)
-    in_w, out_w = attn_low[:4], attn_low[4]
-    q, k, v, a = project(rows, in_w, ln_params)
     head = (local_seqs, length, D)
-    q, k, v, a = (item.reshape(head) for item in (q, k, v, a))
-    att, share, logit, total, states = attend(q, k, v, a)
+    q, k, v, a, att, share, logit, total, states, weights, in_w, out_w, ffn_low = forward(
+        tokens, group_ids, domain_weight, ln_params, attn_w, ffn_w
+    )
     output, dx, datt, gup, gdown, go, gln_two = feed(
-        seq_weight,
+        group_ids,
+        weights,
         rows,
         att.reshape(token_count, D),
         out_grad.reshape(token_count, D),

time: 528 us -> 487 us (0.922)
  Pallas kernels: 171 us -> 223 us
  blocking collectives: 94.9 us -> 50.8 us
  waiting for transfers between devices: 184 us -> 150 us
  other arithmetic: 23.8 us -> 16.8 us
  local copies, waits for them, and re-layouts: 20.2 us -> 13.2 us
    pallas_call x2 -> x1, Pallas kernels: 51 us -> 103 us  [forward(): pl.pallas_call(functools.partial(forward_kernel, wide=wide, narrow=narrow...]
    psum x1 -> x0, blocking collectives: 44.1 us -> none  [shards(): group_count = lax.psum(jnp.sum(member, axis=0), ('wide', 'narrow'))]
    all_gather x2 -> x0, waiting for transfers between devices: 38.5 us -> none  [the longest x1 25.8 us: shards(): lax.all_gather(ffn_w.astype(low_type), 'narrow', axis=1, tiled=True)]
  transfers between devices with their start and end apart: 9 -> 7, of which waited for: 7 -> 5; matrix products, arithmetic and copies ran while one was open for 5% -> 3% of each run, Pallas kernels for 23% -> 14%
where the time goes in v2:
time: 487 us
  Pallas kernels  223 us (46%)
  waiting for transfers between devices  150 us (31%)
  blocking collectives  50.8 us (10%)
  matrix products  17.2 us (4%)
  other arithmetic  16.8 us (3%)
  between operations  15 us (3%)
  local copies, waits for them, and re-layouts  13.2 us (3%)
    pallas_call x1, Pallas kernels, forward(): pl.pallas_call(functools.partial(forward_kernel, wide=wide, narrow=narrow...  103 us
    psum x1, waiting for transfers between devices, shards(): gram = lax.psum(dot_tn(mine, mine), 'narrow')  52.2 us
    pallas_call x1, Pallas kernels, feed(): pl.pallas_call(functools.partial(feed_kernel, per_seq=length // block), g...  51.8 us
    pallas_call x1, Pallas kernels, attend_back(): pl.pallas_call(attend_back_kernel, grid=(chunks,), in_specs=[block] * 8 +...  50.1 us
    reduce_scatter x1, waiting for transfers between devices, sum_rows(): parts = lax.psum_scatter(parts, 'wide', scatter_dimension=2, tiled=False)  43.3 us
    psum x1, blocking collectives, shards(): ln_sum = lax.psum(ln_full, ('wide', 'narrow'))  40.4 us
    reduce_scatter x1, waiting for transfers between devices, shards(): ffn_t = lax.psum_scatter(ffn_t, 'narrow', scatter_dimension=2, tiled=True)  23.9 us
    reduce_scatter x1, waiting for transfers between devices, sum_rows(): parts = lax.psum_scatter(parts, 'narrow', scatter_dimension=1, tiled=False)  18.7 us
  transfers between devices with their start and end apart: 7, of which 5 were waited for; matrix products, arithmetic and copies ran while one was open for 3% of the time, Pallas kernels for 14%

profile of v2, /device:TPU:0, one launch (start us, length us, event | category | flops | bytes accessed | tf_op | source)
XLA Modules:
  0.0 487.0 jit_solution(16340957778242500572)
XLA Ops:
  7.2 0.0 reduce-scatter.9.cloned.1.call-start
  7.2 103.2 %forward.1 = (bf16[2,1024,512]{2,1,0:T(8,128)(2,1)}, bf16[2,1024,512]{2,1,0:T(8,128)(2,1)}, bf16[2,1024,512]{2,1,0:T(8,128)(2,1)}, bf16[2,1024,512]{2,1,0:T(8,12...) custom-call(s32[2]{0:T(128)} %ids_ref.3, ...), custom_call_target="tpu_custom_call" | custom-call | tf_op jit(solution)/shard_map/forward/pallas_call | solution.py:694
  110.4 51.8 %feed.1 = (bf16[2048,512]{1,0:T(8,128)(2,1)}, f32[2048,512]{1,0:T(8,128)}, bf16[2048,512]{1,0:T(8,128)(2,1)}, bf16[512,2048]{1,0:T(8,128)(2,1)}, bf16[512,2048]{...) custom-call(s32[2]{0:T(128)} %ids_ref.3, f32[8,128]{1,0:T(8,128)} %get-tuple-element.41.weight_ref, ...), custom_call_target="tpu_custom_call" | custom-call | tf_op jit(solution)/shard_map/feed/pallas_call | solution.py:292
  162.2 4.5 pad_maximum_fusion
  166.8 0.0 reduce-scatter.9.cloned.1.call-update
  166.8 0.2 reduce-scatter.5.cloned.1.call-start
  167.0 50.1 %attend_back.1 = (bf16[2,1024,512]{2,1,0:T(8,128)(2,1)}, bf16[2,1024,512]{2,1,0:T(8,128)(2,1)}, bf16[2,1024,512]{2,1,0:T(8,128)(2,1)}, bf16[2,1024,512]{2,1,0:T(8,128)(2,1)}) custom-call(bf16[2,1024,512]{2,1,0:T(8,128)(2,1)} %get-tuple-element.47.q_ref, bf16[2,1024,512]{2,1,0:T(8,128)(2,1)} %get-tuple-element.48.k_ref, ...), custom_call_target="tpu_custom_call" | custom-call | tf_op jit(solution)/shard_map/attend_back/pallas_call | solution.py:183
  217.1 18.3 %project_back.1 = (f32[2048,512]{1,0:T(8,128)}, bf16[4,512,512]{2,1,0:T(8,128)(2,1)}, f32[2,512]{1,0:T(2,128)}) custom-call(bf16[2048,512]{1,0:T(8,128)(2,1)} %bitcast.39, f32[2048,512]{1,0:T(8,128)} %get-tuple-element.46.dx_ref, bf16[2048,512]{1,0:T(8,128)(2,1)} %bitcast.48, bf16[2048,512]{1,0:T(8,128)(2,1)} %bitcast.49, bf16[2048,512]{1,0:T(8,128)(2,1)} %bitcast.50, ...), custom_call_target="tpu_custom_call" | custom-call | tf_op jit(solution)/shard_map/project_back/pallas_call | solution.py:378
  235.4 1.8 pad_maximum_fusion.1
  237.3 1.7 copy.33
  239.0 0.0 reduce-scatter.5.cloned.1.call-update
  239.0 0.0 reduce-scatter.11.cloned.1.call-start
  239.1 0.0 reduce-scatter.9.cloned.1.call-done
  239.1 0.7 reduce-scatter.11.cloned.1.call-update
  239.8 0.0 reduce-scatter.7.cloned.1.call-start
  239.8 43.3 %reduce-scatter.5.cloned.1.call-done = bf16[5,4,1,16,512]{4,3,0,1,2:T(8,128)(2,1)} async-done(((bf16[5,4,8,16,512]{4,3,0,1,2:T(8,128)(2,1)}), bf16[5,4,1,16,512]{4,3,0,1,2:T(8,128)(2,1)}) %reduce-scatter.5.cloned.1.call-update) | async-done | bytes 327696 | tf_op jit(solution)/shard_map/reduce_scatter | solution.py:765
  283.1 0.0 reduce-scatter.7.cloned.1.call-update
  283.1 0.0 all-gather.5.cloned.1.call-start
  283.2 23.9 %reduce-scatter.11.cloned.1.call-done = bf16[2,64,512]{2,1,0:T(8,128)(2,1)} async-done(((bf16[2,64,2048]{2,1,0:T(8,128)(2,1)}), bf16[2,64,512]{2,1,0:T(8,128)(2,1)}) %reduce-scatter.11.cloned.1.call-update) | async-done | bytes 131088 | tf_op jit(solution)/shard_map/reduce_scatter | solution.py:810
  307.1 0.0 all-gather.5.cloned.1.call-update
  307.1 0.0 all-reduce.3.cloned.1.call-start
  307.2 1.8 copy.27
  309.0 18.7 %reduce-scatter.7.cloned.1.call-done = bf16[5,1,16,512]{3,2,0,1:T(8,128)(2,1)} async-done(((bf16[5,4,16,512]{3,2,0,1:T(8,128)(2,1)}), bf16[5,1,16,512]{3,2,0,1:T(8,128)(2,1)}) %reduce-scatter.7.cloned.1.call-update) | async-done | bytes 81936 | tf_op jit(solution)/shard_map/reduce_scatter | solution.py:766
  327.7 10.3 %all-gather = bf16[5,1,128,512]{3,2,0,1:T(8,128)(2,1)S(1)} all-gather(bf16[5,1,16,512]{3,2,0,1:T(8,128)(2,1)} %reduce-scatter.7.cloned.1.call-done), channel_id=2, replica_groups=mesh['wide'=8,'narrow'=4] {'wide'}, dimensions={2}, use_global_device_ids=true | all-gather | bytes 737280 | tf_op jit(solution)/shard_map/all_gather | solution.py:767
  338.1 2.1 fusion.37
  340.2 11.2 %all-gather.5.cloned.1.call-done = bf16[2,512,512]{2,1,0:T(8,128)(2,1)} async-done(((bf16[2,64,512]{2,1,0:T(8,128)(2,1)}), bf16[2,512,512]{2,1,0:T(8,128)(2,1)}) %all-gather.5.cloned.1.call-update) | async-done | bytes 1048592 | tf_op jit(solution)/shard_map/all_gather | solution.py:811
  351.4 2.3 fusion.36
  353.7 1.3 copy.28
  355.0 2.5 fusion.14
  357.5 0.0 all-reduce.3.cloned.1.call-update
  357.5 0.0 all-gather.7.cloned.1.call-start
  357.6 52.2 %all-reduce.3.cloned.1.call-done = f32[512,512]{1,0:T(8,128)} async-done(((f32[512,512]{1,0:T(8,128)}), f32[512,512]{1,0:T(8,128)}) %all-reduce.3.cloned.1.call-update) | async-done | bytes 1048592 | tf_op jit(solution)/shard_map/psum | solution.py:835
  409.8 1.9 select_reduce_fusion
  412.5 3.3 fusion.5
  415.8 3.2 fusion.2
  419.0 3.8 fusion.6
  422.8 0.0 all-gather.7.cloned.1.call-update
  422.9 40.4 %psum.14 = f32[4,512]{1,0:T(4,128)S(1)} all-reduce(f32[4,512]{1,0:T(4,128)S(1)} %pad_maximum_fusion.2), channel_id=1, replica_groups=mesh['wide'=8,'narrow'=4] {'wide','narrow'}, use_global_device_ids=true, to_apply=%region_4.0 | all-reduce | flops 2048 | bytes 16384 | tf_op jit(solution)/shard_map/psum | solution.py:814
  463.3 1.3 divide_subtract_fusion
  464.6 1.8 copy.31
  466.4 2.8 convert_bitcast_fusion
  469.2 3.0 copy.30
  472.3 1.2 slice-done
  473.5 2.5 fusion.39
  476.0 1.7 slice-done.1
  477.8 0.4 copy-done.1
  478.1 0.2 copy-done.2
  478.3 1.8 fusion.38
  (22 shorter events, 0.0 us)
Async XLA Ops:
  7.2 231.9 %reduce-scatter.9.cloned.1.call-start = ((), (), s32[]{:S(2)}) async-start(), calls=%async_computation.6 | async-start | bytes 4718592 | tf_op jit(solution)/shard_map/reduce_scatter | solution.py:809
  166.8 116.3 %reduce-scatter.5.cloned.1.call-start = ((), (), s32[]{:S(2)}) async-start(), calls=%async_computation.4 | async-start | bytes 2949120 | tf_op jit(solution)/shard_map/reduce_scatter | solution.py:765
  217.1 18.3 %copy-start.5 = (bf16[512,512]{1,0:T(8,128)(2,1)S(1)}, bf16[512,512]{1,0:T(8,128)(2,1)}, u32[]{:S(2)}) copy-start(bf16[512,512]{1,0:T(8,128)(2,1)} %get-tuple-element.63) | copy-start | bytes 1572868
  239.0 68.2 %copy-start.3 = (f32[2,512,512]{2,1,0:T(8,128)S(1)}, f32[2,512,512]{2,1,0:T(8,128)}, u32[]{:S(2)}) copy-start(f32[2,512,512]{2,1,0:T(8,128)} %param.18) | copy-start | bytes 6291460
  239.0 68.1 %reduce-scatter.11.cloned.1.call-start = ((), (), s32[]{:S(2)}) async-start(), calls=%async_computation.7 | async-start | bytes 655360 | tf_op jit(solution)/shard_map/reduce_scatter | solution.py:810
  239.8 87.9 %reduce-scatter.7.cloned.1.call-start = ((), (), s32[]{:S(2)}) async-start(), calls=%async_computation.5 | async-start | bytes 409600 | tf_op jit(solution)/shard_map/reduce_scatter | solution.py:766
  283.1 68.2 %all-gather.5.cloned.1.call-start = ((), (), s32[]{:S(2)}) async-start(), calls=%async_computation.8 | async-start | bytes 1179648 | tf_op jit(solution)/shard_map/all_gather | solution.py:811
  307.1 102.7 %all-reduce.3.cloned.1.call-start = ((), (), s32[]{:S(2)}) async-start(), calls=%async_computation.9 | async-start | bytes 2097152 | tf_op jit(solution)/shard_map/psum | solution.py:835
  307.2 30.9 %copy-start.4 = (f32[5,128,512]{2,1,0:T(8,128)S(1)}, f32[5,128,512]{2,1,0:T(8,128)}, u32[]{:S(2)}) copy-start(f32[5,128,512]{2,1,0:T(8,128)} %param.17) | copy-start | bytes 3932164
  357.5 114.7 %all-gather.7.cloned.1.call-start = ((), (), s32[]{:S(2)}) async-start(), calls=%async_computation.10 | async-start | bytes 4718592 | tf_op jit(solution)/shard_map/all_gather | solution.py:836
  419.0 3.8 copy-start.6
  419.0 3.9 copy-start.7
  419.0 44.3 %copy-start.8 = (f32[4,128]{1,0:T(4,128)S(1)}, f32[4,128]{1,0:T(4,128)}, u32[]{:S(2)}) copy-start(f32[4,128]{1,0:T(4,128)} %param.21) | copy-start | bytes 6148
  419.0 44.3 %copy-start.9 = (f32[4,128]{1,0:T(4,128)S(1)}, f32[4,128]{1,0:T(4,128)}, u32[]{:S(2)}) copy-start(f32[4,128]{1,0:T(4,128)} %param.20) | copy-start | bytes 6148
  469.2 3.0 copy-start
  472.3 1.2 slice-start
  476.0 1.7 slice-start.1
  476.0 2.1 copy-start.1
  476.0 2.3 copy-start.2
Sparse Core Ops, SparseCore 0:
  166.9 51.6 reduce-scatter.8
  239.2 43.8 reduce-scatter.4
  285.5 21.5 reduce-scatter.10
  309.3 18.3 reduce-scatter.6
  329.6 21.6 all-gather.4
  357.7 52.0 all-reduce.2
  422.9 36.3 all-gather.6

commit v3 on v2

--- a/solution.py
+++ b/solution.py
@@ -81,30 +81,22 @@
     return jnp.where(first_head, left, right)
 
 
-def attend_back_kernel(
-    q_ref,
-    k_ref,
-    v_ref,
-    a_ref,
-    share_ref,
-    logit_ref,
-    total_ref,
-    datt_ref,
-    state_ref,
-    dq_ref,
-    dk_ref,
-    dv_ref,
-    de_ref,
-    state,
-    carry,
-):
-    seqs = q_ref.shape[0]
-
-    @pl.when(pl.program_id(0) == 0)
-    def _():
-        state[...] = jnp.zeros_like(state)
-        carry[...] = jnp.zeros_like(carry)
-
+def attend_back_chunk(refs, state, carry):
+    (
+        q_ref,
+        k_ref,
+        v_ref,
+        a_ref,
+        share_ref,
+        logit_ref,
+        before_ref,
+        datt_ref,
+        state_ref,
+        dq_ref,
+        dk_ref,
+        dv_ref,
+        de_ref,
+    ) = refs
     scaling = HEAD_DIM**-0.5
     first_head = lane_of((CHUNK, PAIR)) < HEAD_DIM
     causal = row_of((CHUNK, 2 * CHUNK)) >= lane_of((CHUNK, 2 * CHUNK)) % CHUNK
@@ -112,82 +104,109 @@
     same_head = (row_of((PAIR, 2 * PAIR)) // HEAD_DIM) == (
         (lane_of((PAIR, 2 * PAIR)) // HEAD_DIM) % 2
     )
+    lower = (row_of((CHUNK, CHUNK)) >= lane_of((CHUNK, CHUNK))).astype(low_type)
     upper = (row_of((CHUNK, CHUNK)) <= lane_of((CHUNK, CHUNK))).astype(low_type)
-    for seq in range(seqs):
+
+    def masked(mask, raw):
+        return jnp.where(mask, raw, 0.0).astype(low_type)
+
+    items = []
+    for seq in range(q_ref.shape[0]):
+        total = dot_nn(lower, a_ref[seq]) + before_ref[0, seq]
+        inv = 1.0 / total
         for pair in range(PAIRS):
             lanes = slice(pair * PAIR, (pair + 1) * PAIR)
-            q = q_ref[seq, :, lanes] * low_type(scaling)
-            k = k_ref[seq, :, lanes]
-            v = v_ref[seq, :, lanes]
-            a = a_ref[seq, :, lanes]
-            share = share_ref[seq, :, lanes]
-            logit = logit_ref[seq, :, lanes]
-            total = total_ref[seq, :, lanes]
-            datt = datt_ref[seq, :, lanes]
-            inv = 1.0 / total
-            before = state_ref[0, seq, pair]
-            after = jnp.where(same_head, state[seq, pair], 0.0).astype(low_type)
-            q_two = split_pair(q, first_head)
-            k_two = split_pair(k, first_head)
-            v_two = split_pair(v, first_head)
-            a_two = split_pair(a, first_head)
-            share_two = split_pair(share, first_head)
-            datt_two = split_pair(datt, first_head)
-
-            dmix = jnp.where(causal, dot_nt(datt, v_two), 0.0).astype(low_type)
-            dshare = dot_nn(dmix, a_two) + dot_nt(datt, before[:, PAIR:])
-            prob = share.astype(wide_type) * total
-            dprob = dshare * inv
-            dlogit = prob * (dprob - head_reduce(dprob * prob, first_head, jnp.sum, 0.0))
-            dnumer = (dlogit * inv).astype(low_type)
-            dtotal = -(dprob * prob + dlogit * logit) * inv
-            dnumer_two = split_pair(dnumer, first_head)
-            dscores = jnp.where(causal, dot_nt(dnumer, a_two), 0.0).astype(low_type)
-            dq = (dot_nn(dscores, k_two) + dot_nn(dnumer, before[:, :PAIR])) * scaling
-            dq_ref[seq, :, lanes] = dq.astype(low_type)
-
-            mix_t = jnp.where(anti, dot_nt(a, share_two), 0.0).astype(low_type)
-            dscores_t = jnp.where(anti, dot_nt(a, dnumer_two), 0.0).astype(low_type)
-            dmix_t = jnp.where(anti, dot_nt(v, datt_two), 0.0).astype(low_type)
-            scores_t = jnp.where(anti, dot_nt(k, q_two), 0.0).astype(low_type)
-            later = dot_nn(a, after)
-            dv = dot_nn(mix_t, datt_two) + later[:, PAIR:]
-            dv_ref[seq, :, lanes] = dv.astype(low_type)
-            dk = dot_nn(dscores_t, q_two) + later[:, :PAIR]
-            dk_ref[seq, :, lanes] = dk.astype(low_type)
-
-            dtotal_high = dtotal.astype(low_type)
-            dtotal_low = (dtotal - dtotal_high.astype(wide_type)).astype(low_type)
-            tail = (
-                dot_nn(upper, dtotal_high)
-                + dot_nn(upper, dtotal_low)
-                + carry[seq, :, lanes]
+            items.append(
+                dict(seq=seq, pair=pair, lanes=lanes, total=total[:, lanes], inv=inv[:, lanes])
             )
-            carry[seq, :, lanes] = tail[0:1, :]
-            da = (
-                dot_nn(dmix_t, share_two)
-                + dot_nn(scores_t, dnumer_two)
-                + dot_nt(jnp.concatenate([k, v], axis=1), after)
-                + tail
-            )
-            de = da.astype(low_type).astype(wide_type) * a.astype(wide_type)
-            de_ref[seq, :, lanes] = de.astype(low_type)
-            state[seq, pair, :, :PAIR] += dot_tn(dnumer, q)
-            state[seq, pair, :, PAIR:] += dot_tn(share, datt)
-
-
-def attend_back(q, k, v, a, share, logit, total, datt, states):
+
+    def load(t):
+        seq, lanes = t["seq"], t["lanes"]
+        t["k"] = k_ref[seq, :, lanes]
+        t["v"] = v_ref[seq, :, lanes]
+        t["a"] = a_ref[seq, :, lanes]
+        t["share"] = share_ref[seq, :, lanes]
+        t["datt"] = datt_ref[seq, :, lanes]
+        t["q"] = q_ref[seq, :, lanes] * low_type(scaling)
+        t["before"] = state_ref[0, seq, t["pair"]]
+        t["after"] = jnp.where(same_head, state[seq, t["pair"]], 0.0).astype(low_type)
+        t["v_two"] = split_pair(t["v"], first_head)
+        t["a_two"] = split_pair(t["a"], first_head)
+        t["dmix"] = masked(causal, dot_nt(t["datt"], t["v_two"]))
+
+    def gather(t):
+        t["share_two"] = split_pair(t["share"], first_head)
+        t["datt_two"] = split_pair(t["datt"], first_head)
+        t["dshare"] = dot_nn(t["dmix"], t["a_two"]) + dot_nt(t["datt"], t["before"][:, PAIR:])
+
+    def soften(t):
+        logit = logit_ref[t["seq"], :, t["lanes"]].astype(wide_type)
+        prob = t["share"].astype(wide_type) * t["total"]
+        cross = t["dshare"] * t["inv"] * prob
+        dlogit = cross - prob * head_reduce(cross, first_head, jnp.sum, 0.0)
+        t["dnumer"] = (dlogit * t["inv"]).astype(low_type)
+        t["dtotal"] = -(cross + dlogit * logit) * t["inv"]
+        t["mix_t"] = masked(anti, dot_nt(t["a"], t["share_two"]))
+        t["dmix_t"] = masked(anti, dot_nt(t["v"], t["datt_two"]))
+
+    def blend(t):
+        t["dnumer_two"] = split_pair(t["dnumer"], first_head)
+        t["dscores"] = masked(causal, dot_nt(t["dnumer"], t["a_two"]))
+        t["dscores_t"] = masked(anti, dot_nt(t["a"], t["dnumer_two"]))
+        t["k_two"] = split_pair(t["k"], first_head)
+        t["q_two"] = split_pair(t["q"], first_head)
+        t["scores_t"] = masked(anti, dot_nt(t["k"], t["q_two"]))
+        t["later"] = dot_nn(t["a"], t["after"])
+
+    def finish(t):
+        seq, lanes = t["seq"], t["lanes"]
+        dq = dot_nn(t["dscores"], t["k_two"]) + dot_nn(t["dnumer"], t["before"][:, :PAIR])
+        dq_ref[seq, :, lanes] = (dq * scaling).astype(low_type)
+        dv = dot_nn(t["mix_t"], t["datt_two"]) + t["later"][:, PAIR:]
+        dv_ref[seq, :, lanes] = dv.astype(low_type)
+        dk = dot_nn(t["dscores_t"], t["q_two"]) + t["later"][:, :PAIR]
+        dk_ref[seq, :, lanes] = dk.astype(low_type)
+        high = t["dtotal"].astype(low_type)
+        rest = (t["dtotal"] - high.astype(wide_type)).astype(low_type)
+        tail = dot_nn(upper, high) + dot_nn(upper, rest) + carry[seq, :, lanes]
+        carry[seq, :, lanes] = tail[0:1, :]
+        da = dot_nn(t["dmix_t"], t["share_two"]) + dot_nn(t["scores_t"], t["dnumer_two"])
+        da = da + dot_nt(jnp.concatenate([t["k"], t["v"]], axis=1), t["after"]) + tail
+        de = da.astype(low_type).astype(wide_type) * t["a"].astype(wide_type)
+        de_ref[seq, :, lanes] = de.astype(low_type)
+        state[seq, t["pair"], :, :PAIR] += dot_tn(t["dnumer"], t["q"])
+        state[seq, t["pair"], :, PAIR:] += dot_tn(t["share"], t["datt"])
+
+    for stage in (load, gather, soften, blend, finish):
+        for item in items:
+            stage(item)
+
+
+def attend_back_kernel(*refs):
+    *blocks, state, carry = refs
+
+    @pl.when(pl.program_id(0) == 0)
+    def _():
+        state[...] = jnp.zeros_like(state)
+        carry[...] = jnp.zeros_like(carry)
+
+    attend_back_chunk(blocks, state, carry)
+
+
+def attend_back(q, k, v, a, share, logit, before, datt, states):
     seqs, length, _ = q.shape
     chunks = length // CHUNK
     block = pl.BlockSpec((seqs, CHUNK, D), lambda i: (0, chunks - 1 - i, 0))
     return pl.pallas_call(
         attend_back_kernel,
         grid=(chunks,),
-        in_specs=[block] * 8
+        in_specs=[block] * 6
         + [
+            pl.BlockSpec((1, seqs, 1, D), lambda i: (chunks - 1 - i, 0, 0, 0)),
+            block,
             pl.BlockSpec(
                 (1, seqs, PAIRS, PAIR, 2 * PAIR), lambda i: (chunks - 1 - i, 0, 0, 0, 0)
-            )
+            ),
         ],
         out_specs=[block] * 4,
         out_shape=[jax.ShapeDtypeStruct(q.shape, low_type)] * 4,
@@ -197,7 +216,7 @@
         ],
         compiler_params=pltpu.CompilerParams(vmem_limit_bytes=VMEM_BYTES),
         name="attend_back",
-    )(q, k, v, a, share, logit, total, datt, states)
+    )(q, k, v, a, share, logit, before, datt, states)
 
 
 FF_BLOCK = 512
@@ -246,13 +265,20 @@
     dy = dout.astype(low_type)
     second_t = second.T
     dy_t = dy.T
-    result = mixed
-    dsecond = jnp.zeros_like(mixed)
-    for part in range(FF // FF_BLOCK):
-        rows = slice(part * FF_BLOCK, (part + 1) * FF_BLOCK)
-        up = ffn_ref[0, rows, :]
-        down = ffn_ref[1, rows, :]
-        inner = dot_nt(second, up)
+    parts = [dict(rows=slice(part * FF_BLOCK, (part + 1) * FF_BLOCK)) for part in range(FF // FF_BLOCK)]
+
+    def open_part(t):
+        t["up"] = ffn_ref[0, t["rows"], :]
+        t["down"] = ffn_ref[1, t["rows"], :]
+        t["inner"] = dot_nt(second, t["up"])
+        t["dhidden"] = dot_nt(dy, t["down"])
+
+    result, dsecond = mixed, 0.0
+    open_part(parts[0])
+    for place, t in enumerate(parts):
+        if place + 1 < len(parts):
+            open_part(parts[place + 1])
+        inner = t["inner"]
         square = inner * inner
         bend = jnp.tanh(inner * (gelu_root + (gelu_root * gelu_cube) * square))
         half = 0.5 + 0.5 * bend
@@ -260,11 +286,11 @@
         slope = half + (0.5 * inner) * (1.0 - bend * bend) * (
             gelu_root + (3.0 * gelu_root * gelu_cube) * square
         )
-        result = result + dot_nn(hidden, down)
-        down_sum[:, rows] += dot_nn(dy_t, hidden)
-        dinner = (dot_nt(dy, down) * slope).astype(low_type)
-        up_sum[:, rows] += dot_nn(second_t, dinner)
-        dsecond = dsecond + dot_nn(dinner, up)
+        dinner = (t["dhidden"] * slope).astype(low_type)
+        result = result + dot_nn(hidden, t["down"])
+        down_sum[:, t["rows"]] += dot_nn(dy_t, hidden)
+        up_sum[:, t["rows"]] += dot_nn(second_t, dinner)
+        dsecond = dsecond + dot_nn(dinner, t["up"])
     out_ref[...] = result.astype(low_type)
     gln_ref[0:1, :] += jnp.sum(dsecond * normed, axis=0, keepdims=True)
     gln_ref[1:2, :] += jnp.sum(dsecond, axis=0, keepdims=True)
@@ -283,7 +309,7 @@
 
 def feed(ids, weights, rows, att, grad, wo, ffn, ln_params, length):
     count = rows.shape[0]
-    block = 256
+    block = 512
     row_spec = pl.BlockSpec((block, D), lambda i: (i, 0))
 
     def whole(*shape):
@@ -351,13 +377,14 @@
         w_sum[...] = jnp.zeros_like(w_sum)
         gln_ref[...] = jnp.zeros_like(gln_ref)
 
+    parts = (dq_ref, dk_ref, dv_ref, de_ref)
+    dfirst = dot_nt(dq_ref[...], w_ref[0])
+    for place in range(1, 4):
+        dfirst = dfirst + dot_nt(parts[place][...], w_ref[place])
     normed, inverse = normalize(x_ref[...].astype(wide_type))
     first_t = (normed * ln_ref[0:1, :] + ln_ref[1:2, :]).astype(low_type).T
-    dfirst = jnp.zeros(normed.shape, wide_type)
-    for place, ref in enumerate((dq_ref, dk_ref, dv_ref, de_ref)):
-        part = ref[...]
-        w_sum[place] += dot_nn(first_t, part)
-        dfirst = dfirst + dot_nt(part, w_ref[place])
+    for place in range(4):
+        w_sum[place] += dot_nn(first_t, parts[place][...])
     gln_ref[0:1, :] += jnp.sum(dfirst * normed, axis=0, keepdims=True)
     gln_ref[1:2, :] += jnp.sum(dfirst, axis=0, keepdims=True)
     grad_ref[...] = dx_ref[...] + norm_back(dfirst, normed, inverse, ln_ref[0:1, :])
@@ -369,7 +396,7 @@
 
 def project_back(rows, dx, dq, dk, dv, de, weights, ln_params):
     count = rows.shape[0]
-    block = 256
+    block = 512
     row_spec = pl.BlockSpec((block, D), lambda i: (i, 0))
 
     def whole(*shape):
@@ -413,35 +440,68 @@
     pl.semaphore_wait(barrier, len(devices))
 
 
-def attend_chunk(q_all, k_all, v_all, a_all, consts, refs, seq):
-    first_head, causal, same_head, lower = consts
-    att_ref, share_ref, logit_ref, total_ref, state_ref, state, carry = refs
-    total_all = dot_nn(lower, a_all) + carry[seq]
-    total_ref[seq] = total_all
-    carry[seq] = total_all[CHUNK - 1 :, :]
-    inv_all = 1.0 / total_all
-    for pair in range(PAIRS):
-        lanes = slice(pair * PAIR, (pair + 1) * PAIR)
-        q = q_all[:, lanes] * low_type(HEAD_DIM**-0.5)
-        k = k_all[:, lanes]
-        v = v_all[:, lanes]
-        a = a_all[:, lanes]
-        inv = inv_all[:, lanes]
-        a_two = split_pair(a, first_head)
-        now = jnp.where(same_head, state[seq, pair], 0.0).astype(low_type)
-        state_ref[0, seq, pair] = now
-        scores = jnp.where(causal, dot_nt(q, split_pair(k, first_head)), 0.0).astype(low_type)
-        numer = dot_nn(scores, a_two) + dot_nt(q, now[:, :PAIR])
-        logit = numer * inv
-        logit_ref[seq, :, lanes] = logit
-        expo = jnp.exp(logit - head_reduce(logit, first_head, jnp.max, -jnp.inf))
-        share = expo * (inv / head_reduce(expo, first_head, jnp.sum, 0.0))
-        share = share.astype(low_type)
-        share_ref[seq, :, lanes] = share
-        mix = jnp.where(causal, dot_nt(share, a_two), 0.0).astype(low_type)
-        att = dot_nn(mix, split_pair(v, first_head)) + dot_nn(share, now[:, PAIR:])
-        att_ref[seq, :, lanes] = att.astype(low_type)
-        state[seq, pair] += dot_tn(a, jnp.concatenate([k, v], axis=1))
+def attend_chunks(q_all, k_all, v_all, a_all, refs, seqs):
+    att_ref, share_ref, logit_ref, before_ref, state_ref, state, carry = refs
+    first_head = lane_of((CHUNK, PAIR)) < HEAD_DIM
+    causal = row_of((CHUNK, 2 * CHUNK)) >= lane_of((CHUNK, 2 * CHUNK)) % CHUNK
+    same_head = (row_of((PAIR, 2 * PAIR)) // HEAD_DIM) == (
+        (lane_of((PAIR, 2 * PAIR)) // HEAD_DIM) % 2
+    )
+    lower = (row_of((CHUNK, CHUNK)) >= lane_of((CHUNK, CHUNK))).astype(low_type)
+    items = []
+    for seq in range(seqs):
+        part = slice(seq * CHUNK, (seq + 1) * CHUNK)
+        before = carry[seq]
+        before_ref[0, seq] = before
+        total = dot_nn(lower, a_all[part]) + before
+        carry[seq] = total[CHUNK - 1 :, :]
+        inv = 1.0 / total
+        for pair in range(PAIRS):
+            lanes = slice(pair * PAIR, (pair + 1) * PAIR)
+            items.append(
+                dict(
+                    seq=seq,
+                    pair=pair,
+                    lanes=lanes,
+                    q=q_all[part, lanes] * low_type(HEAD_DIM**-0.5),
+                    k=k_all[part, lanes],
+                    v=v_all[part, lanes],
+                    a=a_all[part, lanes],
+                    inv=inv[:, lanes],
+                )
+            )
+
+    def score(t):
+        t["a_two"] = split_pair(t["a"], first_head)
+        t["now"] = jnp.where(same_head, state[t["seq"], t["pair"]], 0.0).astype(low_type)
+        state_ref[0, t["seq"], t["pair"]] = t["now"]
+        raw = dot_nt(t["q"], split_pair(t["k"], first_head))
+        t["scores"] = jnp.where(causal, raw, 0.0).astype(low_type)
+
+    def gather(t):
+        numer = dot_nn(t["scores"], t["a_two"]) + dot_nt(t["q"], t["now"][:, :PAIR])
+        t["logit"] = numer * t["inv"]
+        logit_ref[t["seq"], :, t["lanes"]] = t["logit"].astype(low_type)
+
+    def soften(t):
+        expo = jnp.exp(t["logit"] - head_reduce(t["logit"], first_head, jnp.max, -jnp.inf))
+        share = expo * (t["inv"] / head_reduce(expo, first_head, jnp.sum, 0.0))
+        t["share"] = share.astype(low_type)
+        share_ref[t["seq"], :, t["lanes"]] = t["share"]
+
+    def blend(t):
+        raw = dot_nt(t["share"], t["a_two"])
+        t["mix"] = jnp.where(causal, raw, 0.0).astype(low_type)
+
+    def finish(t):
+        att = dot_nn(t["mix"], split_pair(t["v"], first_head))
+        att = att + dot_nn(t["share"], t["now"][:, PAIR:])
+        att_ref[t["seq"], :, t["lanes"]] = att.astype(low_type)
+        state[t["seq"], t["pair"]] += dot_tn(t["a"], jnp.concatenate([t["k"], t["v"]], axis=1))
+
+    for stage in (score, gather, soften, blend, finish):
+        for item in items:
+            stage(item)
 
 
 def forward_kernel(
@@ -458,7 +518,7 @@
     att_ref,
     share_ref,
     logit_ref,
-    total_ref,
+    before_ref,
     state_ref,
     weight_ref,
     in_hbm,
@@ -472,18 +532,11 @@
     counts,
     counts_z,
     counts_w,
-    in_send,
-    in_recv,
-    in_pass,
-    in_got,
-    ffn_send,
-    ffn_recv,
-    ffn_pass,
-    ffn_got,
-    out_send,
-    out_recv,
-    out_pass,
-    out_got,
+    in_sems,
+    in_far,
+    ffn_sems,
+    ffn_far,
+    out_sems,
     cz_send,
     cz_recv,
     cw_send,
@@ -506,10 +559,12 @@
     rows = attn_ref.shape[1]
     ffn_rows = ffn_ref.shape[1]
     half = rows // 2
+    quarter = ffn_rows // 4
+    chip = lax.rem(w // 2, 4)
     hops = list(range(1, narrow))
-    hops.sort(key=lambda hop: min(hop, narrow - hop))
     column = [(w, lax.rem(z + hop, narrow)) for hop in hops]
     plane = [(lax.rem(w + hop, wide), z) for hop in range(1, wide)]
+    chips = [(w - 2 * chip + 2 * lax.rem(chip + hop, 4), z) for hop in range(1, 4)]
 
     def at(owner, size):
         return pl.ds(pl.multiple_of(owner * size, size), size)
@@ -517,48 +572,59 @@
     def from_z(place):
         return lax.rem(z + narrow - hops[place], narrow)
 
-    def half_at(owner, part):
-        start = owner * rows + part * half
-        return pl.ds(pl.multiple_of(start, half), half)
-
-    def in_out(place):
+    def in_part(owner, matrix):
+        return in_w.at[matrix, at(2 * owner + core, half)]
+
+    def in_z(place):
         return remote(
-            own.at[pl.ds(2 * core, 2)],
-            in_w.at[pl.ds(2 * core, 2), at(z, rows)],
-            in_send.at[place],
-            in_recv.at[place],
+            own.at[chip, at(core, half)],
+            in_part(z, chip),
+            in_sems.at[0, place],
+            in_sems.at[1, place],
             column[place],
         )
 
-    def in_on(place):
-        block = in_w.at[pl.ds(2 * core, 2), at(from_z(place), rows)]
-        return remote(block, block, in_pass.at[place], in_got.at[place], mate)
-
-    def ffn_out(place):
+    def in_chip(place, hop):
+        block = in_part(from_z(place), chip)
         return remote(
-            own_ffn.at[core],
-            ffn_hbm.at[core, at(z, ffn_rows)],
-            ffn_send.at[place],
-            ffn_recv.at[place],
+            block, block, in_far.at[0, place, hop], in_far.at[1, place, hop], chips[hop]
+        )
+
+    def in_core(place):
+        block = in_w.at[:, at(2 * from_z(place) + core, half)]
+        return remote(block, block, in_sems.at[2, place], in_sems.at[3, place], mate)
+
+    def ffn_z(place):
+        return remote(
+            own_ffn.at[core, at(chip, quarter)],
+            ffn_hbm.at[core, at(4 * z + chip, quarter)],
+            ffn_sems.at[0, place],
+            ffn_sems.at[1, place],
             column[place],
         )
 
-    def ffn_on(place):
+    def ffn_chip(place, hop):
+        block = ffn_hbm.at[core, at(4 * from_z(place) + chip, quarter)]
+        return remote(
+            block, block, ffn_far.at[0, place, hop], ffn_far.at[1, place, hop], chips[hop]
+        )
+
+    def ffn_core(place):
         block = ffn_hbm.at[core, at(from_z(place), ffn_rows)]
-        return remote(block, block, ffn_pass.at[place], ffn_got.at[place], mate)
-
-    def out_out(place):
+        return remote(block, block, ffn_sems.at[2, place], ffn_sems.at[3, place], mate)
+
+    def out_z(place):
         return remote(
-            own.at[4, pl.ds(pl.multiple_of(core * half, half), half)],
-            out_hbm.at[half_at(z, core)],
-            out_send.at[place],
-            out_recv.at[place],
+            own.at[4, at(core, half)],
+            out_hbm.at[at(2 * z + core, half)],
+            out_sems.at[0, place],
+            out_sems.at[1, place],
             column[place],
         )
 
-    def out_on(place):
-        block = out_hbm.at[half_at(from_z(place), core)]
-        return remote(block, block, out_pass.at[place], out_got.at[place], mate)
+    def out_core(place):
+        block = out_hbm.at[at(2 * from_z(place) + core, half)]
+        return remote(block, block, out_sems.at[2, place], out_sems.at[3, place], mate)
 
     def count_z(place):
         return remote(
@@ -581,7 +647,7 @@
         own[...] = attn_ref[...].astype(low_type)
         greet(column + plane)
         for place in range(narrow - 1):
-            in_out(place).start()
+            in_z(place).start()
         for place in range(4):
             in_w[place, at(z, rows), :] = own[place]
         own_ffn[...] = ffn_ref[...].astype(low_type)
@@ -591,16 +657,21 @@
             count = count + (lanes == ids_ref[seq]).astype(wide_type)
         counts[...] = count
         for place in range(narrow - 1):
-            in_out(place).wait_recv()
-            in_on(place).start()
+            in_z(place).wait_recv()
+            for hop in range(3):
+                in_chip(place, hop).start()
         for place in range(narrow - 1):
-            count_z(place).start()
-            ffn_out(place).start()
-            out_out(place).start()
+            for hop in range(3):
+                in_chip(place, hop).wait_recv()
+            in_core(place).start()
         keep_ffn.start()
         keep_out.start()
         for place in range(narrow - 1):
-            in_on(place).wait_recv()
+            count_z(place).start()
+            out_z(place).start()
+            ffn_z(place).start()
+        for place in range(narrow - 1):
+            in_core(place).wait_recv()
         keep_in.start()
 
     @pl.when(step == 1)
@@ -627,20 +698,22 @@
             values = values + jnp.where(lanes == group, dw_ref[group], 0.0)
         weight_ref[...] = values * total_seqs / (groups * jnp.maximum(total, 1.0))
 
-    @pl.when(step == steps - 3)
+    @pl.when(step == steps // 2 - 1)
     def _():
         for place in range(narrow - 1):
-            out_out(place).wait_recv()
-            out_on(place).start()
-            ffn_out(place).wait_recv()
-            ffn_on(place).start()
-
-    first_head = lane_of((CHUNK, PAIR)) < HEAD_DIM
-    causal = row_of((CHUNK, 2 * CHUNK)) >= lane_of((CHUNK, 2 * CHUNK)) % CHUNK
-    same_head = (row_of((PAIR, 2 * PAIR)) // HEAD_DIM) == (
-        (lane_of((PAIR, 2 * PAIR)) // HEAD_DIM) % 2
-    )
-    lower = (row_of((CHUNK, CHUNK)) >= lane_of((CHUNK, CHUNK))).astype(low_type)
+            out_z(place).wait_recv()
+            out_core(place).start()
+            ffn_z(place).wait_recv()
+            for hop in range(3):
+                ffn_chip(place, hop).start()
+
+    @pl.when(step == steps - 2)
+    def _():
+        for place in range(narrow - 1):
+            for hop in range(3):
+                ffn_chip(place, hop).wait_recv()
+            ffn_core(place).start()
+
     normed, _ = normalize(x_ref[...].reshape(seqs * CHUNK, D).astype(wide_type))
     first = (normed * ln_ref[0:1, :] + ln_ref[1:2, :]).astype(low_type)
     q_all = dot_nn(first, in_w[0]).astype(low_type)
@@ -651,17 +724,14 @@
     k_ref[...] = k_all.reshape(q_ref.shape)
     v_ref[...] = v_all.reshape(q_ref.shape)
     a_ref[...] = a_all.reshape(q_ref.shape)
-    for seq in range(seqs):
-        part = slice(seq * CHUNK, (seq + 1) * CHUNK)
-        attend_chunk(
-            q_all[part],
-            k_all[part],
-            v_all[part],
-            a_all[part],
-            (first_head, causal, same_head, lower),
-            (att_ref, share_ref, logit_ref, total_ref, state_ref, state, carry),
-            seq,
-        )
+    attend_chunks(
+        q_all,
+        k_all,
+        v_all,
+        a_all,
+        (att_ref, share_ref, logit_ref, before_ref, state_ref, state, carry),
+        seqs,
+    )
 
     @pl.when(step == steps - 1)
     def _():
@@ -669,12 +739,15 @@
         keep_out.wait()
         keep_in.wait()
         for place in range(narrow - 1):
-            in_out(place).wait_send()
-            in_on(place).wait_send()
-            out_out(place).wait_send()
-            out_on(place).wait()
-            ffn_out(place).wait_send()
-            ffn_on(place).wait()
+            in_z(place).wait_send()
+            in_core(place).wait_send()
+            out_z(place).wait_send()
+            out_core(place).wait()
+            ffn_z(place).wait_send()
+            for hop in range(3):
+                in_chip(place, hop).wait_send()
+                ffn_chip(place, hop).wait_send()
+            ffn_core(place).wait()
 
 
 def forward(tokens, ids, dw, ln_params, attn_w, ffn_w):
@@ -684,9 +757,7 @@
     narrow = lax.axis_size("narrow")
     block = pl.BlockSpec((seqs, CHUNK, D), lambda i: (0, i, 0))
     low_out = jax.ShapeDtypeStruct(tokens.shape, low_type)
-    wide_out = jax.ShapeDtypeStruct(tokens.shape, wide_type)
     any_spec = pl.BlockSpec(memory_space=pl.ANY)
-    near, far = (narrow - 1,), (wide - 1,)
 
     def whole(*shape):
         return pl.BlockSpec(shape, lambda i: (0,) * len(shape))
@@ -708,18 +779,18 @@
             whole(*attn_w.shape),
             whole(*ffn_w.shape),
         ],
-        out_specs=[block] * 8
+        out_specs=[block] * 7
         + [
+            pl.BlockSpec((1, seqs, 1, D), lambda i: (i, 0, 0, 0)),
             pl.BlockSpec((1, seqs, PAIRS, PAIR, 2 * PAIR), lambda i: (i, 0, 0, 0, 0)),
             whole(8, LANES),
             any_spec,
             any_spec,
             any_spec,
         ],
-        out_shape=[low_out] * 6
+        out_shape=[low_out] * 7
         + [
-            wide_out,
-            wide_out,
+            jax.ShapeDtypeStruct((chunks, seqs, 1, D), wide_type),
             jax.ShapeDtypeStruct((chunks, seqs, PAIRS, PAIR, 2 * PAIR), low_type),
             jax.ShapeDtypeStruct((8, LANES), wide_type),
             jax.ShapeDtypeStruct((4, D, D), low_type),
@@ -736,8 +807,17 @@
             pltpu.VMEM((narrow - 1, 8, LANES), wide_type),
             pltpu.VMEM((wide - 1, 8, LANES), wide_type),
         ]
-        + [pltpu.SemaphoreType.DMA(near)] * 14
-        + [pltpu.SemaphoreType.DMA(far)] * 2
+        + [
+            pltpu.SemaphoreType.DMA((4, narrow - 1)),
+            pltpu.SemaphoreType.DMA((2, narrow - 1, 3)),
+            pltpu.SemaphoreType.DMA((4, narrow - 1)),
+            pltpu.SemaphoreType.DMA((2, narrow - 1, 3)),
+            pltpu.SemaphoreType.DMA((4, narrow - 1)),
+            pltpu.SemaphoreType.DMA((narrow - 1,)),
+            pltpu.SemaphoreType.DMA((narrow - 1,)),
+            pltpu.SemaphoreType.DMA((wide - 1,)),
+            pltpu.SemaphoreType.DMA((wide - 1,)),
+        ]
         + [pltpu.SemaphoreType.DMA((3,))],
         compiler_params=pltpu.CompilerParams(
             vmem_limit_bytes=VMEM_BYTES, collective_id=0, has_side_effects=True
@@ -786,7 +866,7 @@
     narrow = lax.axis_size("narrow")
     rows = tokens.reshape(token_count, D)
     head = (local_seqs, length, D)
-    q, k, v, a, att, share, logit, total, states, weights, in_w, out_w, ffn_low = forward(
+    q, k, v, a, att, share, logit, before, states, weights, in_w, out_w, ffn_low = forward(
         tokens, group_ids, domain_weight, ln_params, attn_w, ffn_w
     )
     output, dx, datt, gup, gdown, go, gln_two = feed(
@@ -800,7 +880,7 @@
         ln_params,
         length,
     )
-    dq, dk, dv, de = attend_back(q, k, v, a, share, logit, total, datt.reshape(head), states)
+    dq, dk, dv, de = attend_back(q, k, v, a, share, logit, before, datt.reshape(head), states)
     dq, dk, dv, de = (item.reshape(token_count, D) for item in (dq, dk, dv, de))
     input_grad, gw, gln_one = project_back(rows, dx, dq, dk, dv, de, in_w, ln_params)
 

time: 487 us -> 425 us (0.87)
  Pallas kernels: 223 us -> 148 us
  waiting for transfers between devices: 150 us -> 163 us
    pallas_call x1, Pallas kernels: 103 us -> 64.6 us  [forward(): pl.pallas_call(functools.partial(forward_kernel, wide=wide, narrow=narrow...]
    pallas_call x1, Pallas kernels: 50.1 us -> 25.5 us  [attend_back(): pl.pallas_call(attend_back_kernel, grid=(chunks,), in_specs=[block] * 6 +...]
    pallas_call x1, Pallas kernels: 51.8 us -> 41.2 us  [feed(): pl.pallas_call(functools.partial(feed_kernel, per_seq=length // block), g...]
    reduce_scatter x1, waiting for transfers between devices: 0.02 us -> 9.66 us  [shards(): ffn_t = lax.psum_scatter(ffn_t, 'wide', scatter_dimension=1, tiled=True)]
  transfers between devices with their start and end apart: 7 -> 7, of which waited for: 5 -> 6; matrix products, arithmetic and copies ran while one was open for 3% -> 4% of each run, Pallas kernels for 14% -> 10%
where the time goes in v3:
time: 425 us
  waiting for transfers between devices  163 us (38%)
  Pallas kernels  148 us (35%)
  blocking collectives  50.8 us (12%)
  matrix products  17.2 us (4%)
  other arithmetic  16.9 us (4%)
  between operations  15 us (4%)
  local copies, waits for them, and re-layouts  13.2 us (3%)
    pallas_call x1, Pallas kernels, forward(): pl.pallas_call(functools.partial(forward_kernel, wide=wide, narrow=narrow...  64.6 us
    psum x1, waiting for transfers between devices, shards(): gram = lax.psum(dot_tn(mine, mine), 'narrow')  52.1 us
    reduce_scatter x1, waiting for transfers between devices, sum_rows(): parts = lax.psum_scatter(parts, 'wide', scatter_dimension=2, tiled=False)  47.3 us
    pallas_call x1, Pallas kernels, feed(): pl.pallas_call(functools.partial(feed_kernel, per_seq=length // block), g...  41.2 us
    psum x1, blocking collectives, shards(): ln_sum = lax.psum(ln_full, ('wide', 'narrow'))  40.4 us
    pallas_call x1, Pallas kernels, attend_back(): pl.pallas_call(attend_back_kernel, grid=(chunks,), in_specs=[block] * 6 +...  25.5 us
    reduce_scatter x1, waiting for transfers between devices, shards(): ffn_t = lax.psum_scatter(ffn_t, 'narrow', scatter_dimension=2, tiled=True)  24 us
    reduce_scatter x1, waiting for transfers between devices, sum_rows(): parts = lax.psum_scatter(parts, 'narrow', scatter_dimension=1, tiled=False)  18.7 us
  transfers between devices with their start and end apart: 7, of which 6 were waited for; matrix products, arithmetic and copies ran while one was open for 4% of the time, Pallas kernels for 10%

profile of v3, /device:TPU:0, one launch (start us, length us, event | category | flops | bytes accessed | tf_op | source)
XLA Modules:
  0.0 424.8 jit_solution(6658228616152177309)
XLA Ops:
  7.2 0.0 reduce-scatter.9.cloned.1.call-start
  7.2 64.6 %forward.1 = (bf16[2,1024,512]{2,1,0:T(8,128)(2,1)}, bf16[2,1024,512]{2,1,0:T(8,128)(2,1)}, bf16[2,1024,512]{2,1,0:T(8,128)(2,1)}, bf16[2,1024,512]{2,1,0:T(8,12...) custom-call(s32[2]{0:T(128)} %ids_ref.3, ...), custom_call_target="tpu_custom_call" | custom-call | tf_op jit(solution)/shard_map/forward/pallas_call | solution.py:765
  71.9 41.2 %feed.1 = (bf16[2048,512]{1,0:T(8,128)(2,1)}, f32[2048,512]{1,0:T(8,128)}, bf16[2048,512]{1,0:T(8,128)(2,1)}, bf16[512,2048]{1,0:T(8,128)(2,1)}, bf16[512,2048]{...) custom-call(s32[2]{0:T(128)} %ids_ref.3, f32[8,128]{1,0:T(8,128)} %get-tuple-element.41.weight_ref, ...), custom_call_target="tpu_custom_call" | custom-call | tf_op jit(solution)/shard_map/feed/pallas_call | solution.py:318
  113.1 4.6 %pad_maximum_fusion = bf16[2,512,2048]{2,1,0:T(8,128)(2,1)} fusion(bf16[1,512,2048]{2,1,0:T(8,128)(2,1)} %bitcast.47, bf16[1,512,2048]{2,1,0:T(8,128)(2,1)} %bitcast.46), kind=kLoop, calls=%fused_computation | loop fusion | flops 2097152 | bytes 8388608 | tf_op jit(solution)/shard_map/stack | solution.py:888
  117.7 0.0 reduce-scatter.9.cloned.1.call-update
  117.7 0.0 reduce-scatter.5.cloned.1.call-start
  117.7 25.5 %attend_back.1 = (bf16[2,1024,512]{2,1,0:T(8,128)(2,1)}, bf16[2,1024,512]{2,1,0:T(8,128)(2,1)}, bf16[2,1024,512]{2,1,0:T(8,128)(2,1)}, bf16[2,1024,512]{2,1,0:T(8,128)(2,1)}) custom-call(bf16[2,1024,512]{2,1,0:T(8,128)(2,1)} %get-tuple-element.47.refs_0_, bf16[2,1024,512]{2,1,0:T(8,128)(2,1)} %get-tuple-element.48.refs_1_, ...), custom_call_target="tpu_custom_call" | custom-call | tf_op jit(solution)/shard_map/attend_back/pallas_call | solution.py:200
  143.2 17.0 %project_back.1 = (f32[2048,512]{1,0:T(8,128)}, bf16[4,512,512]{2,1,0:T(8,128)(2,1)}, f32[2,512]{1,0:T(2,128)}) custom-call(bf16[2048,512]{1,0:T(8,128)(2,1)} %bitcast.39, f32[2048,512]{1,0:T(8,128)} %get-tuple-element.46.dx_ref, bf16[2048,512]{1,0:T(8,128)(2,1)} %bitcast.48, bf16[2048,512]{1,0:T(8,128)(2,1)} %bitcast.49, bf16[2048,512]{1,0:T(8,128)(2,1)} %bitcast.50, ...), custom_call_target="tpu_custom_call" | custom-call | tf_op jit(solution)/shard_map/project_back/pallas_call | solution.py:405
  160.3 1.8 pad_maximum_fusion.1
  162.1 1.7 copy.33
  163.9 0.0 reduce-scatter.5.cloned.1.call-update
  163.9 0.0 reduce-scatter.11.cloned.1.call-start
  163.9 9.7 %reduce-scatter.9.cloned.1.call-done = bf16[2,64,2048]{2,1,0:T(8,128)(2,1)} async-done(((bf16[2,512,2048]{2,1,0:T(8,128)(2,1)}), bf16[2,64,2048]{2,1,0:T(8,128)(2,1)}) %reduce-scatter.9.cloned.1.call-update) | async-done | bytes 524304 | tf_op jit(solution)/shard_map/reduce_scatter | solution.py:889
  173.6 0.0 reduce-scatter.11.cloned.1.call-update
  173.6 0.0 reduce-scatter.7.cloned.1.call-start
  173.7 47.3 %reduce-scatter.5.cloned.1.call-done = bf16[5,4,1,16,512]{4,3,0,1,2:T(8,128)(2,1)} async-done(((bf16[5,4,8,16,512]{4,3,0,1,2:T(8,128)(2,1)}), bf16[5,4,1,16,512]{4,3,0,1,2:T(8,128)(2,1)}) %reduce-scatter.5.cloned.1.call-update) | async-done | bytes 327696 | tf_op jit(solution)/shard_map/reduce_scatter | solution.py:845
  221.0 0.0 reduce-scatter.7.cloned.1.call-update
  221.0 0.0 all-gather.5.cloned.1.call-start
  221.0 24.0 %reduce-scatter.11.cloned.1.call-done = bf16[2,64,512]{2,1,0:T(8,128)(2,1)} async-done(((bf16[2,64,2048]{2,1,0:T(8,128)(2,1)}), bf16[2,64,512]{2,1,0:T(8,128)(2,1)}) %reduce-scatter.11.cloned.1.call-update) | async-done | bytes 131088 | tf_op jit(solution)/shard_map/reduce_scatter | solution.py:890
  245.0 0.0 all-gather.5.cloned.1.call-update
  245.0 0.0 all-reduce.3.cloned.1.call-start
  245.1 1.8 copy.27
  246.9 18.7 %reduce-scatter.7.cloned.1.call-done = bf16[5,1,16,512]{3,2,0,1:T(8,128)(2,1)} async-done(((bf16[5,4,16,512]{3,2,0,1:T(8,128)(2,1)}), bf16[5,1,16,512]{3,2,0,1:T(8,128)(2,1)}) %reduce-scatter.7.cloned.1.call-update) | async-done | bytes 81936 | tf_op jit(solution)/shard_map/reduce_scatter | solution.py:846
  265.6 10.4 %all-gather = bf16[5,1,128,512]{3,2,0,1:T(8,128)(2,1)S(1)} all-gather(bf16[5,1,16,512]{3,2,0,1:T(8,128)(2,1)} %reduce-scatter.7.cloned.1.call-done), channel_id=2, replica_groups=mesh['wide'=8,'narrow'=4] {'wide'}, dimensions={2}, use_global_device_ids=true | all-gather | bytes 737280 | tf_op jit(solution)/shard_map/all_gather | solution.py:847
  275.9 2.1 fusion.37
  278.1 11.2 %all-gather.5.cloned.1.call-done = bf16[2,512,512]{2,1,0:T(8,128)(2,1)} async-done(((bf16[2,64,512]{2,1,0:T(8,128)(2,1)}), bf16[2,512,512]{2,1,0:T(8,128)(2,1)}) %all-gather.5.cloned.1.call-update) | async-done | bytes 1048592 | tf_op jit(solution)/shard_map/all_gather | solution.py:891
  289.3 2.3 fusion.36
  291.6 1.3 copy.28
  292.9 2.5 fusion.14
  295.4 0.0 all-reduce.3.cloned.1.call-update
  295.5 0.0 all-gather.7.cloned.1.call-start
  295.5 52.1 %all-reduce.3.cloned.1.call-done = f32[512,512]{1,0:T(8,128)} async-done(((f32[512,512]{1,0:T(8,128)}), f32[512,512]{1,0:T(8,128)}) %all-reduce.3.cloned.1.call-update) | async-done | bytes 1048592 | tf_op jit(solution)/shard_map/psum | solution.py:915
  347.6 1.9 select_reduce_fusion
  350.3 3.3 fusion.5
  353.6 3.2 fusion.2
  356.9 3.8 fusion.6
  360.7 0.0 all-gather.7.cloned.1.call-update
  360.7 40.4 %psum.14 = f32[4,512]{1,0:T(4,128)S(1)} all-reduce(f32[4,512]{1,0:T(4,128)S(1)} %pad_maximum_fusion.2), channel_id=1, replica_groups=mesh['wide'=8,'narrow'=4] {'wide','narrow'}, use_global_device_ids=true, to_apply=%region_4.0 | all-reduce | flops 2048 | bytes 16384 | tf_op jit(solution)/shard_map/psum | solution.py:894
  401.1 1.3 divide_subtract_fusion
  402.4 1.8 copy.31
  404.2 2.8 convert_bitcast_fusion
  407.1 3.0 copy.30
  410.1 1.2 slice-done
  411.3 2.5 fusion.39
  413.8 1.7 slice-done.1
  415.6 0.4 copy-done.1
  415.9 0.2 copy-done.2
  416.1 1.8 fusion.38
  (22 shorter events, 0.0 us)
Async XLA Ops:
  7.2 166.4 %reduce-scatter.9.cloned.1.call-start = ((), (), s32[]{:S(2)}) async-start(), calls=%async_computation.6 | async-start | bytes 4718592 | tf_op jit(solution)/shard_map/reduce_scatter | solution.py:889
  117.7 103.3 %reduce-scatter.5.cloned.1.call-start = ((), (), s32[]{:S(2)}) async-start(), calls=%async_computation.4 | async-start | bytes 2949120 | tf_op jit(solution)/shard_map/reduce_scatter | solution.py:845
  143.2 17.0 %copy-start.5 = (bf16[512,512]{1,0:T(8,128)(2,1)S(1)}, bf16[512,512]{1,0:T(8,128)(2,1)}, u32[]{:S(2)}) copy-start(bf16[512,512]{1,0:T(8,128)(2,1)} %get-tuple-element.63) | copy-start | bytes 1572868
  163.9 81.2 %copy-start.3 = (f32[2,512,512]{2,1,0:T(8,128)S(1)}, f32[2,512,512]{2,1,0:T(8,128)}, u32[]{:S(2)}) copy-start(f32[2,512,512]{2,1,0:T(8,128)} %param.18) | copy-start | bytes 6291460
  163.9 81.1 %reduce-scatter.11.cloned.1.call-start = ((), (), s32[]{:S(2)}) async-start(), calls=%async_computation.7 | async-start | bytes 655360 | tf_op jit(solution)/shard_map/reduce_scatter | solution.py:890
  173.6 92.0 %reduce-scatter.7.cloned.1.call-start = ((), (), s32[]{:S(2)}) async-start(), calls=%async_computation.5 | async-start | bytes 409600 | tf_op jit(solution)/shard_map/reduce_scatter | solution.py:846
  221.0 68.3 %all-gather.5.cloned.1.call-start = ((), (), s32[]{:S(2)}) async-start(), calls=%async_computation.8 | async-start | bytes 1179648 | tf_op jit(solution)/shard_map/all_gather | solution.py:891
  245.0 102.6 %all-reduce.3.cloned.1.call-start = ((), (), s32[]{:S(2)}) async-start(), calls=%async_computation.9 | async-start | bytes 2097152 | tf_op jit(solution)/shard_map/psum | solution.py:915
  245.1 30.8 %copy-start.4 = (f32[5,128,512]{2,1,0:T(8,128)S(1)}, f32[5,128,512]{2,1,0:T(8,128)}, u32[]{:S(2)}) copy-start(f32[5,128,512]{2,1,0:T(8,128)} %param.17) | copy-start | bytes 3932164
  295.5 114.6 %all-gather.7.cloned.1.call-start = ((), (), s32[]{:S(2)}) async-start(), calls=%async_computation.10 | async-start | bytes 4718592 | tf_op jit(solution)/shard_map/all_gather | solution.py:916
  356.8 3.8 copy-start.6
  356.8 3.9 copy-start.7
  356.8 44.3 %copy-start.8 = (f32[4,128]{1,0:T(4,128)S(1)}, f32[4,128]{1,0:T(4,128)}, u32[]{:S(2)}) copy-start(f32[4,128]{1,0:T(4,128)} %param.21) | copy-start | bytes 6148
  356.8 44.3 %copy-start.9 = (f32[4,128]{1,0:T(4,128)S(1)}, f32[4,128]{1,0:T(4,128)}, u32[]{:S(2)}) copy-start(f32[4,128]{1,0:T(4,128)} %param.20) | copy-start | bytes 6148
  407.1 3.0 copy-start
  410.1 1.2 slice-start
  413.8 1.7 slice-start.1
  413.8 2.1 copy-start.1
  413.8 2.3 copy-start.2
Sparse Core Ops, SparseCore 0:
  117.8 55.7 reduce-scatter.8
  177.3 43.6 reduce-scatter.4
  223.3 21.6 reduce-scatter.10
  247.2 18.2 reduce-scatter.6
  267.5 21.7 all-gather.4
  295.6 52.0 all-reduce.2
  360.8 36.3 all-gather.6

commit v4 on v3

--- a/solution.py
+++ b/solution.py
@@ -182,43 +182,6 @@
             stage(item)
 
 
-def attend_back_kernel(*refs):
-    *blocks, state, carry = refs
-
-    @pl.when(pl.program_id(0) == 0)
-    def _():
-        state[...] = jnp.zeros_like(state)
-        carry[...] = jnp.zeros_like(carry)
-
-    attend_back_chunk(blocks, state, carry)
-
-
-def attend_back(q, k, v, a, share, logit, before, datt, states):
-    seqs, length, _ = q.shape
-    chunks = length // CHUNK
-    block = pl.BlockSpec((seqs, CHUNK, D), lambda i: (0, chunks - 1 - i, 0))
-    return pl.pallas_call(
-        attend_back_kernel,
-        grid=(chunks,),
-        in_specs=[block] * 6
-        + [
-            pl.BlockSpec((1, seqs, 1, D), lambda i: (chunks - 1 - i, 0, 0, 0)),
-            block,
-            pl.BlockSpec(
-                (1, seqs, PAIRS, PAIR, 2 * PAIR), lambda i: (chunks - 1 - i, 0, 0, 0, 0)
-            ),
-        ],
-        out_specs=[block] * 4,
-        out_shape=[jax.ShapeDtypeStruct(q.shape, low_type)] * 4,
-        scratch_shapes=[
-            pltpu.VMEM((seqs, PAIRS, PAIR, 2 * PAIR), wide_type),
-            pltpu.VMEM((seqs, 1, D), wide_type),
-        ],
-        compiler_params=pltpu.CompilerParams(vmem_limit_bytes=VMEM_BYTES),
-        name="attend_back",
-    )(q, k, v, a, share, logit, before, datt, states)
-
-
 FF_BLOCK = 512
 gelu_root = math.sqrt(2.0 / math.pi)
 gelu_cube = 0.044715
@@ -236,8 +199,7 @@
     out_ref,
     dx_ref,
     datt_ref,
-    gup_ref,
-    gdown_ref,
+    gffn_ref,
     go_ref,
     gln_ref,
     up_sum,
@@ -302,8 +264,8 @@
 
     @pl.when(step == pl.num_programs(0) - 1)
     def _():
-        gup_ref[...] = up_sum[...].astype(low_type)
-        gdown_ref[...] = down_sum[...].astype(low_type)
+        gffn_ref[0] = up_sum[...].astype(low_type)
+        gffn_ref[1] = down_sum[...].astype(low_type)
         go_ref[...] = o_sum[...].astype(low_type)
 
 
@@ -332,8 +294,7 @@
             row_spec,
             row_spec,
             row_spec,
-            whole(D, FF),
-            whole(D, FF),
+            whole(2, D, FF),
             whole(D, D),
             whole(2, D),
         ],
@@ -341,8 +302,7 @@
             jax.ShapeDtypeStruct((count, D), low_type),
             jax.ShapeDtypeStruct((count, D), wide_type),
             jax.ShapeDtypeStruct((count, D), low_type),
-            jax.ShapeDtypeStruct((D, FF), low_type),
-            jax.ShapeDtypeStruct((D, FF), low_type),
+            jax.ShapeDtypeStruct((2, D, FF), low_type),
             jax.ShapeDtypeStruct((D, D), low_type),
             jax.ShapeDtypeStruct((2, D), wide_type),
         ],
@@ -537,6 +497,7 @@
     ffn_sems,
     ffn_far,
     out_sems,
+    out_far,
     cz_send,
     cz_recv,
     cw_send,
@@ -613,17 +574,26 @@
         block = ffn_hbm.at[core, at(from_z(place), ffn_rows)]
         return remote(block, block, ffn_sems.at[2, place], ffn_sems.at[3, place], mate)
 
+    def out_block(owner, part):
+        return out_hbm.at[at(4 * owner + part, rows // 4), at(core, D // 2)]
+
     def out_z(place):
         return remote(
-            own.at[4, at(core, half)],
-            out_hbm.at[at(2 * z + core, half)],
+            own.at[4, at(chip, rows // 4), at(core, D // 2)],
+            out_block(z, chip),
             out_sems.at[0, place],
             out_sems.at[1, place],
             column[place],
         )
 
+    def out_chip(place, hop):
+        block = out_block(from_z(place), chip)
+        return remote(
+            block, block, out_far.at[0, place, hop], out_far.at[1, place, hop], chips[hop]
+        )
+
     def out_core(place):
-        block = out_hbm.at[at(2 * from_z(place) + core, half)]
+        block = out_hbm.at[at(from_z(place), rows), at(core, D // 2)]
         return remote(block, block, out_sems.at[2, place], out_sems.at[3, place], mate)
 
     def count_z(place):
@@ -661,15 +631,15 @@
             for hop in range(3):
                 in_chip(place, hop).start()
         for place in range(narrow - 1):
+            ffn_z(place).start()
+            out_z(place).start()
+            count_z(place).start()
+        keep_ffn.start()
+        keep_out.start()
+        for place in range(narrow - 1):
             for hop in range(3):
                 in_chip(place, hop).wait_recv()
             in_core(place).start()
-        keep_ffn.start()
-        keep_out.start()
-        for place in range(narrow - 1):
-            count_z(place).start()
-            out_z(place).start()
-            ffn_z(place).start()
         for place in range(narrow - 1):
             in_core(place).wait_recv()
         keep_in.start()
@@ -698,21 +668,23 @@
             values = values + jnp.where(lanes == group, dw_ref[group], 0.0)
         weight_ref[...] = values * total_seqs / (groups * jnp.maximum(total, 1.0))
 
-    @pl.when(step == steps // 2 - 1)
+    @pl.when(step == 1)
     def _():
         for place in range(narrow - 1):
+            ffn_z(place).wait_recv()
             out_z(place).wait_recv()
-            out_core(place).start()
-            ffn_z(place).wait_recv()
             for hop in range(3):
                 ffn_chip(place, hop).start()
+                out_chip(place, hop).start()
 
     @pl.when(step == steps - 2)
     def _():
         for place in range(narrow - 1):
             for hop in range(3):
                 ffn_chip(place, hop).wait_recv()
+                out_chip(place, hop).wait_recv()
             ffn_core(place).start()
+            out_core(place).start()
 
     normed, _ = normalize(x_ref[...].reshape(seqs * CHUNK, D).astype(wide_type))
     first = (normed * ln_ref[0:1, :] + ln_ref[1:2, :]).astype(low_type)
@@ -747,6 +719,7 @@
             for hop in range(3):
                 in_chip(place, hop).wait_send()
                 ffn_chip(place, hop).wait_send()
+                out_chip(place, hop).wait_send()
             ffn_core(place).wait()
 
 
@@ -813,6 +786,7 @@
             pltpu.SemaphoreType.DMA((4, narrow - 1)),
             pltpu.SemaphoreType.DMA((2, narrow - 1, 3)),
             pltpu.SemaphoreType.DMA((4, narrow - 1)),
+            pltpu.SemaphoreType.DMA((2, narrow - 1, 3)),
             pltpu.SemaphoreType.DMA((narrow - 1,)),
             pltpu.SemaphoreType.DMA((narrow - 1,)),
             pltpu.SemaphoreType.DMA((wide - 1,)),
@@ -826,25 +800,525 @@
     )(ids, dw, tokens, ln_params, attn_w, ffn_w)
 
 
+class Place:
+    def __init__(self, narrow):
+        self.narrow = narrow
+        w = lax.axis_index("wide")
+        self.z = lax.axis_index("narrow")
+        self.core = lax.rem(w, 2)
+        self.chip = lax.rem(w // 2, 4)
+        self.other = 1 - self.core
+        self.hops = list(range(1, narrow))
+        self.column_z = [lax.rem(self.z + hop, narrow) for hop in self.hops]
+        self.column = [(w, place) for place in self.column_z]
+        self.chip_at = [lax.rem(self.chip + hop, 4) for hop in range(1, 4)]
+        self.chips = [(w - 2 * self.chip + 2 * chip, self.z) for chip in self.chip_at]
+        self.mate = (w + 1 - 2 * self.core, self.z)
+
+
+class Copies:
+    def __init__(self, sems):
+        self.sems = sems
+        self.used = 0
+
+    def remote(self, src, dst, device):
+        at = self.used
+        self.used += 2
+        return remote(src, dst, self.sems.at[at], self.sems.at[at + 1], device)
+
+    def local(self, src, dst):
+        at = self.used
+        self.used += 1
+        return pltpu.make_async_copy(src, dst, self.sems.at[at])
+
+
+def blocks_at(owner, size):
+    return pl.ds(pl.multiple_of(owner * size, size), size)
+
+
+def wide_sum(parts):
+    total = parts[0].astype(wide_type)
+    for part in parts[1:]:
+        total = total + part.astype(wide_type)
+    return total
+
+
 def newton_poly(gram):
-    scale = jnp.sqrt(jnp.trace(gram)) + 1e-07
-    eye = jnp.eye(D, dtype=wide_type)
-    gram_one = gram * (1.0 / (scale * scale))
-    poly_one = quintic_lin * eye + quintic_cube * gram_one + quintic_five * (gram_one @ gram_one)
-    gram_two = (gram_one @ poly_one) @ poly_one
-    poly_two = quintic_lin * eye + quintic_cube * gram_two + quintic_five * (gram_two @ gram_two)
-    return (poly_one @ poly_two) * (1.0 / scale)
-
-
-def sum_rows(stack, rows_at):
+    size = gram.shape[0]
+    eye = row_of((size, size)) == lane_of((size, size))
+    trace = jnp.sum(jnp.where(eye, gram, 0.0), axis=1, keepdims=True)
+    trace = jnp.sum(trace, axis=0, keepdims=True)
+    scale = 1.0 / (jnp.sqrt(trace) + 1e-07)
+
+    def low_dot(left, right):
+        return dot_nn(left.astype(low_type), right.astype(low_type))
+
+    def polynomial(one):
+        poly = quintic_cube * one + quintic_five * low_dot(one, one)
+        return poly + jnp.where(eye, quintic_lin, 0.0)
+
+    gram_one = gram * (scale * scale)
+    poly_one = polynomial(gram_one)
+    gram_two = low_dot(low_dot(gram_one, poly_one), poly_one)
+    poly_two = polynomial(gram_two)
+    return low_dot(poly_one, poly_two) * scale
+
+
+def back_kernel(*refs, narrow):
+    blocks = list(refs[:9])
+    gffn_hbm, go_hbm = refs[9:11]
+    outs = list(refs[11:15])
+    fsum_ref, osum_ref = refs[15:17]
+    (state, carry, own_f, got_f, far_f, own_o, got_o, cut_o, far_o, sems) = refs[17:]
+    step = pl.program_id(0)
+    steps = pl.num_programs(0)
+    here = Place(narrow)
+    copies = Copies(sems)
+    half = D // 2
+    part = D // 4
+    rows = cut_o.shape[2]
+
+    keep_f = copies.local(gffn_hbm.at[here.core], own_f)
+    keep_o = copies.local(go_hbm.at[:, blocks_at(here.core, half)], own_o)
+    core_f = copies.remote(gffn_hbm.at[here.other], got_f, here.mate)
+    core_o = copies.remote(go_hbm.at[:, blocks_at(here.other, half)], got_o, here.mate)
+    plane_f, plane_o = [], []
+    for hop in range(3):
+        there = here.chip_at[hop]
+        plane_f.append(
+            copies.remote(own_f.at[blocks_at(there, part)], far_f.at[hop], here.chips[hop])
+        )
+        plane_o.append(copies.remote(cut_o.at[:, there], far_o.at[hop], here.chips[hop]))
+
+    @pl.when(step == 0)
+    def _():
+        state[...] = jnp.zeros_like(state)
+        carry[...] = jnp.zeros_like(carry)
+        greet(here.chips + [here.mate])
+        for copy in (core_f, core_o, keep_f, keep_o):
+            copy.start()
+
+    @pl.when(step == steps // 4)
+    def _():
+        for copy in (core_f, core_o, keep_f, keep_o):
+            copy.wait()
+        own_f[...] = wide_sum([own_f[...], got_f[...]]).astype(low_type)
+        cut_o[...] = wide_sum([own_o[...], got_o[...]]).astype(low_type).reshape(cut_o.shape)
+        for copy in plane_f + plane_o:
+            copy.start()
+
+    attend_back_chunk(blocks + outs, state, carry)
+
+    @pl.when(step == steps - 1)
+    def _():
+        for copy in plane_f + plane_o:
+            copy.wait()
+        mine = own_f[blocks_at(here.chip, part), :]
+        fsum_ref[...] = wide_sum([mine] + [far_f[hop] for hop in range(3)]).astype(low_type)
+        mine = cut_o[:, here.chip]
+        osum_ref[...] = wide_sum([mine] + [far_o[hop] for hop in range(3)]).astype(low_type)
+
+
+def back(q, k, v, a, share, logit, before, datt, states, gffn, go):
+    seqs, length, _ = q.shape
+    chunks = length // CHUNK
+    narrow = lax.axis_size("narrow")
+    rows = D // narrow // 4
+    block = pl.BlockSpec((seqs, CHUNK, D), lambda i: (0, chunks - 1 - i, 0))
+    any_spec = pl.BlockSpec(memory_space=pl.ANY)
+    f_shape, o_shape = (D // 4, FF), (narrow, rows, D // 2)
+    return pl.pallas_call(
+        functools.partial(back_kernel, narrow=narrow),
+        grid=(chunks,),
+        in_specs=[block] * 6
+        + [
+            pl.BlockSpec((1, seqs, 1, D), lambda i: (chunks - 1 - i, 0, 0, 0)),
+            block,
+            pl.BlockSpec(
+                (1, seqs, PAIRS, PAIR, 2 * PAIR), lambda i: (chunks - 1 - i, 0, 0, 0, 0)
+            ),
+            any_spec,
+            any_spec,
+        ],
+        out_specs=[block] * 4
+        + [pl.BlockSpec(f_shape, lambda i: (0, 0)), pl.BlockSpec(o_shape, lambda i: (0, 0, 0))],
+        out_shape=[jax.ShapeDtypeStruct(q.shape, low_type)] * 4
+        + [jax.ShapeDtypeStruct(f_shape, low_type), jax.ShapeDtypeStruct(o_shape, low_type)],
+        scratch_shapes=[
+            pltpu.VMEM((seqs, PAIRS, PAIR, 2 * PAIR), wide_type),
+            pltpu.VMEM((seqs, 1, D), wide_type),
+            pltpu.VMEM((D, FF), low_type),
+            pltpu.VMEM((D, FF), low_type),
+            pltpu.VMEM((3,) + f_shape, low_type),
+            pltpu.VMEM((D, D // 2), low_type),
+            pltpu.VMEM((D, D // 2), low_type),
+            pltpu.VMEM((narrow, 4, rows, D // 2), low_type),
+            pltpu.VMEM((3,) + o_shape, low_type),
+            pltpu.SemaphoreType.DMA((24,)),
+        ],
+        compiler_params=pltpu.CompilerParams(
+            vmem_limit_bytes=VMEM_BYTES, collective_id=1, has_side_effects=True
+        ),
+        name="back",
+    )(q, k, v, a, share, logit, before, datt, states, gffn, go)
+
+
+def update_kernel(
+    gw_hbm,
+    fsum_ref,
+    osum_ref,
+    mom_in_hbm,
+    mom_o_ref,
+    mom_f_hbm,
+    ln_one_ref,
+    ln_two_ref,
+    grad_attn,
+    step_attn,
+    grad_ffn,
+    step_ffn,
+    ln_ref,
+    ln_now,
+    ln_mate,
+    ln_chips,
+    ln_column,
+    half_w,
+    half_got,
+    far_w,
+    cut_w,
+    col_w,
+    grad_w,
+    mom_w,
+    moment_w,
+    poly_w,
+    send_w,
+    all_w,
+    col_f,
+    all_f,
+    mom_f,
+    moment_f,
+    out_f,
+    col_o,
+    all_o,
+    moment_o,
+    step_o,
+    cut_gf,
+    col_gf,
+    strips_gf,
+    gram_f,
+    cut_go,
+    col_go,
+    strips_go,
+    gram_o,
+    sems,
+    *,
+    narrow,
+):
+    here = Place(narrow)
+    copies = Copies(sems)
+    z, core, chip = here.z, here.core, here.chip
+    half = D // 2
+    quarter = D // 4
+    rows = D // narrow
+    small = rows // 4
+    ffn_rows = FF // narrow
+    strip = quarter // narrow
+    column = range(narrow - 1)
+    planes = range(3)
+    own_cols = blocks_at(core, half)
+    mate_cols = blocks_at(here.other, half)
+    own_quarter = blocks_at(chip, quarter)
+    own_small = blocks_at(chip, small)
+    matrix = lax.rem(z, 4)
+
+    def to_plane(src, dst):
+        return [copies.remote(src(i), dst(i), here.chips[i]) for i in planes]
+
+    def to_column(src, dst):
+        return [copies.remote(src(i), dst(i), here.column[i]) for i in column]
+
+    def same(block):
+        return lambda i: block
+
+    keep_w = copies.local(gw_hbm.at[:, :, own_cols], half_w)
+    keep_mom = copies.local(mom_in_hbm.at[matrix], mom_w)
+    keep_f = copies.local(mom_f_hbm.at[core], mom_f)
+    mate_sum = [
+        copies.remote(gw_hbm.at[:, :, mate_cols], half_got, here.mate),
+        copies.remote(ln_now, ln_mate, here.mate),
+    ]
+    z_sum_f = to_column(
+        lambda i: fsum_ref.at[:, blocks_at(here.column_z[i], ffn_rows)], lambda i: col_f.at[i]
+    ) + to_column(lambda i: osum_ref.at[here.column_z[i]], lambda i: col_o.at[i])
+    plane_sum = to_plane(
+        lambda i: half_w.at[:, blocks_at(here.chip_at[i], quarter)], lambda i: far_w.at[i]
+    )
+    plane_ln = to_plane(same(ln_now), lambda i: ln_chips.at[i])
+    block = all_f.at[own_quarter]
+    plane_f = to_plane(same(block), same(block))
+    block = all_o.at[own_small, own_cols]
+    plane_f = plane_f + to_plane(same(block), same(block))
+    z_sum = to_column(lambda i: cut_w.at[lax.rem(here.column_z[i], 4)], lambda i: col_w.at[i])
+    z_ln = to_column(same(ln_now), lambda i: ln_column.at[i])
+    block = out_f.at[0, core]
+    mate_f = copies.remote(block, block, here.mate)
+    block = all_o.at[:, own_cols]
+    mate_o = copies.remote(block, block, here.mate)
+    z_gf = to_column(
+        lambda i: cut_gf.at[blocks_at(here.column_z[i], strip)], lambda i: col_gf.at[i]
+    )
+    block = grad_w.at[own_quarter, own_cols]
+    plane_w = to_plane(same(block), same(block))
+    z_go = to_column(
+        lambda i: cut_go.at[blocks_at(here.column_z[i], strip)], lambda i: col_go.at[i]
+    )
+    block = grad_w.at[:, own_cols]
+    mate_w = copies.remote(block, block, here.mate)
+    block = strips_gf.at[blocks_at(z, strip)]
+    z_back_f = to_column(same(block), same(block))
+    block = strips_go.at[blocks_at(z, strip)]
+    z_back_o = to_column(same(block), same(block))
+    block = gram_f.at[own_quarter]
+    plane_gf = to_plane(same(block), same(block))
+    block = gram_o.at[own_quarter, own_cols]
+    plane_go = to_plane(same(block), same(block))
+    spread = []
+    for hop in range(1, 4):
+        there = z - matrix + lax.rem(matrix + hop, 4)
+        spread.append(
+            copies.remote(
+                send_w.at[there],
+                all_w.at[matrix, :, own_small, own_cols],
+                (lax.axis_index("wide"), there),
+            )
+        )
+    block = gram_o.at[:, own_cols]
+    mate_go = copies.remote(block, block, here.mate)
+    block = out_f.at[1, core]
+    mate_x = copies.remote(block, block, here.mate)
+    block = all_w.at[:, :, own_small, own_cols]
+    plane_all = to_plane(same(block), same(block))
+    block = all_w.at[:, :, :, own_cols]
+    mate_all = copies.remote(block, block, here.mate)
+    write_f = [copies.local(out_f.at[0], grad_ffn), copies.local(out_f.at[1], step_ffn)]
+    write_o = [copies.local(all_o, grad_attn.at[4]), copies.local(step_o, step_attn.at[4])]
+    write_w = [
+        copies.local(all_w.at[:, 0], grad_attn.at[pl.ds(0, 4)]),
+        copies.local(all_w.at[:, 1], step_attn.at[pl.ds(0, 4)]),
+    ]
+    sent = []
+
+    def start(group):
+        for copy in group:
+            copy.start()
+        sent.extend(group)
+
+    def arrive(group):
+        for copy in group:
+            copy.wait_recv()
+
+    def begin(group):
+        for copy in group:
+            copy.start()
+
+    greet(here.column + here.chips + [here.mate])
+    keep_w.start()
+    ln_now[...] = jnp.zeros_like(ln_now)
+    ln_now[0:2, :] = ln_one_ref[...]
+    ln_now[2:4, :] = ln_two_ref[...]
+    start(mate_sum)
+    start(z_sum_f)
+    begin([keep_f, keep_mom])
+
+    keep_w.wait()
+    arrive(mate_sum)
+    half_w[...] = wide_sum([half_w[...], half_got[...]]).astype(low_type)
+    start(plane_sum)
+    mate_sum[1].wait_send()
+    ln_now[...] = ln_now[...] + ln_mate[...]
+    start(plane_ln)
+
+    arrive(z_sum_f)
+    total = wide_sum([fsum_ref[:, blocks_at(z, ffn_rows)]] + [col_f[i] for i in column])
+    all_f[own_quarter, :] = total.astype(low_type)
+    total = wide_sum([osum_ref[z]] + [col_o[i] for i in column])
+    all_o[own_small, own_cols] = total.astype(low_type)
+    start(plane_f)
+
+    arrive(plane_sum)
+    mine = half_w[:, own_quarter, :]
+    cut_w[...] = wide_sum([mine] + [far_w[i] for i in planes]).astype(low_type)
+    start(z_sum)
+    arrive(plane_ln)
+    for copy in plane_ln:
+        copy.wait_send()
+    ln_now[...] = ln_now[...] + ln_chips[0] + ln_chips[1] + ln_chips[2]
+    start(z_ln)
+
+    keep_f.wait()
+    arrive(plane_f)
+    start([mate_o])
+    grad = all_f[...].T
+    out_f[0, core] = grad
+    start([mate_f])
+    moment_f[...] = (momentum_keep * mom_f[...] + grad.astype(wide_type)).astype(low_type)
+    cut_gf[...] = dot_tn(moment_f[:, own_quarter], moment_f[...]).astype(low_type)
+    start(z_gf)
+
+    arrive(z_sum)
+    total = wide_sum([cut_w[matrix]] + [col_w[i] for i in column])
+    grad_w[own_quarter, own_cols] = total.astype(low_type)
+    start(plane_w)
+
+    arrive([mate_o])
+    moment = momentum_keep * mom_o_ref[...] + all_o[...].astype(wide_type)
+    moment_o[...] = moment.astype(low_type)
+    cut_go[...] = dot_tn(moment_o[:, own_quarter], moment_o[:, own_cols]).astype(low_type)
+    start(z_go)
+
+    arrive(plane_w)
+    start([mate_w])
+
+    arrive(z_gf)
+    total = wide_sum([cut_gf[blocks_at(z, strip), :]] + [col_gf[i] for i in column])
+    strips_gf[blocks_at(z, strip), :] = total.astype(low_type)
+    start(z_back_f)
+    arrive(z_go)
+    total = wide_sum([cut_go[blocks_at(z, strip), :]] + [col_go[i] for i in column])
+    strips_go[blocks_at(z, strip), :] = total.astype(low_type)
+    start(z_back_o)
+
+    keep_mom.wait()
+    arrive([mate_w])
+    moment = momentum_keep * mom_w[...].astype(wide_type) + grad_w[...].astype(wide_type)
+    moment_w[...] = moment.astype(low_type)
+    gram = dot_tn(moment_w[...], moment_w[...])
+
+    arrive(z_back_f)
+    gram_f[own_quarter, :] = strips_gf[...]
+    start(plane_gf)
+    arrive(z_back_o)
+    gram_o[own_quarter, own_cols] = strips_go[...]
+    start(plane_go)
+
+    poly_w[...] = newton_poly(gram).astype(low_type)
+    picked = [moment_w[pl.ds(pl.multiple_of(there * rows + chip * small, small), small), :] for there in range(narrow)]
+    ortho = dot_nn(jnp.concatenate(picked, axis=0), poly_w[:, own_cols]).astype(low_type)
+    for there in range(narrow):
+        place = pl.ds(pl.multiple_of(there * rows + chip * small, small), small)
+        send_w[there, 0] = grad_w[place, own_cols]
+        send_w[there, 1] = ortho[there * small : (there + 1) * small, :]
+    start(spread)
+    all_w[matrix, :, own_small, own_cols] = send_w[z]
+
+    arrive(plane_go)
+    start([mate_go])
+    arrive(plane_gf)
+    poly = newton_poly(gram_f[...].astype(wide_type)).astype(low_type)
+    out_f[1, core] = dot_nn(moment_f[...], poly).astype(low_type)
+    start([mate_x])
+
+    arrive(spread)
+    start(plane_all)
+
+    arrive([mate_go])
+    poly = newton_poly(gram_o[...].astype(wide_type)).astype(low_type)
+    step_o[...] = dot_nn(moment_o[...], poly).astype(low_type)
+    begin(write_o)
+    arrive([mate_f, mate_x])
+    begin(write_f)
+    arrive(z_ln)
+    total = ln_now[...]
+    for i in column:
+        total = total + ln_column[i]
+    ln_ref[...] = total
+
+    arrive(plane_all)
+    start([mate_all])
+    arrive([mate_all])
+    begin(write_w)
+    for copy in write_o + write_f + write_w:
+        copy.wait()
+    settled = [id(copy) for copy in [mate_sum[1]] + plane_ln]
+    for copy in sent:
+        if id(copy) not in settled:
+            copy.wait_send()
+
+
+def update(gw, fsum, osum, mom_in, mom_o, mom_f, ln_one, ln_two):
+    narrow = lax.axis_size("narrow")
+    rows, ffn_rows = D // narrow, FF // narrow
+    small, half, quarter = rows // 4, D // 2, D // 4
+    strip = quarter // narrow
+    column = narrow - 1
+    any_spec = pl.BlockSpec(memory_space=pl.ANY)
+    vmem = pl.BlockSpec(memory_space=pltpu.VMEM)
+
+    def low(*shape):
+        return pltpu.VMEM(shape, low_type)
+
+    def full(*shape):
+        return pltpu.VMEM(shape, wide_type)
+
+    scratch = [
+        full(8, D),
+        full(8, D),
+        full(3, 8, D),
+        full(column, 8, D),
+        low(4, D, half),
+        low(4, D, half),
+        low(3, 4, quarter, half),
+        low(4, quarter, half),
+        low(column, quarter, half),
+        low(D, D),
+        low(D, D),
+        low(D, D),
+        low(D, D),
+        low(narrow, 2, small, half),
+        low(4, 2, rows, D),
+        low(column, quarter, ffn_rows),
+        low(D, ffn_rows),
+        full(ffn_rows, D),
+        low(ffn_rows, D),
+        low(2, 2, ffn_rows, D),
+        low(column, small, half),
+        low(rows, D),
+        low(rows, D),
+        low(rows, D),
+        low(quarter, D),
+        low(column, strip, D),
+        low(quarter, D),
+        low(D, D),
+        low(quarter, half),
+        low(column, strip, half),
+        low(quarter, half),
+        low(D, D),
+        pltpu.SemaphoreType.DMA((9 + 2 * (10 + 27 + 9 * column),)),
+    ]
+    return pl.pallas_call(
+        functools.partial(update_kernel, narrow=narrow),
+        in_specs=[any_spec, vmem, vmem, any_spec, vmem, any_spec, vmem, vmem],
+        out_specs=[any_spec, any_spec, any_spec, any_spec, vmem],
+        out_shape=[
+            jax.ShapeDtypeStruct((5, rows, D), low_type),
+            jax.ShapeDtypeStruct((5, rows, D), low_type),
+            jax.ShapeDtypeStruct((2, ffn_rows, D), low_type),
+            jax.ShapeDtypeStruct((2, ffn_rows, D), low_type),
+            jax.ShapeDtypeStruct((8, D), wide_type),
+        ],
+        scratch_shapes=scratch,
+        compiler_params=pltpu.CompilerParams(
+            vmem_limit_bytes=VMEM_BYTES, collective_id=2, has_side_effects=True
+        ),
+        name="update",
+    )(gw, fsum, osum, mom_in, mom_o, mom_f, ln_one, ln_two)
+
+
+def group_sum(values):
     wide = lax.axis_size("wide")
-    narrow = lax.axis_size("narrow")
-    mats = stack.shape[0]
-    share = D // narrow // wide
-    parts = stack.reshape(mats, narrow, wide, share, D)
-    parts = lax.psum_scatter(parts, "wide", scatter_dimension=2, tiled=False)
-    parts = lax.psum_scatter(parts, "narrow", scatter_dimension=1, tiled=False)
-    return lax.all_gather(parts, "wide", axis=1, tiled=True)
+    if wide == 8:
+        return values
+    groups = [[place + 8 * group for group in range(wide // 8)] for place in range(8)]
+    return lax.psum(values, "wide", axis_index_groups=groups)
 
 
 def shards(
@@ -862,14 +1336,15 @@
 ):
     local_seqs, length, _ = tokens.shape
     token_count = local_seqs * length
-    wide = lax.axis_size("wide")
-    narrow = lax.axis_size("narrow")
     rows = tokens.reshape(token_count, D)
     head = (local_seqs, length, D)
     q, k, v, a, att, share, logit, before, states, weights, in_w, out_w, ffn_low = forward(
         tokens, group_ids, domain_weight, ln_params, attn_w, ffn_w
     )
-    output, dx, datt, gup, gdown, go, gln_two = feed(
+    moms = attn_mom[:4].astype(low_type)
+    moms, weights = lax.optimization_barrier((moms, weights))
+    mom_in = lax.all_gather(moms, "narrow", axis=1, tiled=True)
+    output, dx, datt, gffn, go, ln_two = feed(
         group_ids,
         weights,
         rows,
@@ -880,52 +1355,27 @@
         ln_params,
         length,
     )
-    dq, dk, dv, de = attend_back(q, k, v, a, share, logit, before, datt.reshape(head), states)
+    gffn, go, ln_two = group_sum((gffn, go, ln_two))
+    dq, dk, dv, de, fsum, osum = back(
+        q, k, v, a, share, logit, before, datt.reshape(head), states, gffn, go
+    )
     dq, dk, dv, de = (item.reshape(token_count, D) for item in (dq, dk, dv, de))
-    input_grad, gw, gln_one = project_back(rows, dx, dq, dk, dv, de, in_w, ln_params)
-
-    attn_grad = sum_rows(jnp.concatenate([gw, go[None]], axis=0), None).astype(wide_type)
-    ffn_t = jnp.stack([gup, gdown])
-    ffn_t = lax.psum_scatter(ffn_t, "wide", scatter_dimension=1, tiled=True)
-    ffn_t = lax.psum_scatter(ffn_t, "narrow", scatter_dimension=2, tiled=True)
-    ffn_t = lax.all_gather(ffn_t, "wide", axis=1, tiled=True)
-    ffn_grad = jnp.swapaxes(ffn_t, 1, 2).astype(wide_type)
-    ln_full = jnp.concatenate([gln_one, gln_two], axis=0)
-    ln_sum = lax.psum(ln_full, ("wide", "narrow"))
+    input_grad, gw, ln_one = project_back(rows, dx, dq, dk, dv, de, in_w, ln_params)
+    gw, ln_one = group_sum((gw, ln_one))
+    attn_low, attn_ortho, ffn_low_grad, ffn_ortho, ln_sum = update(
+        gw, fsum, osum, mom_in, attn_mom[4], ffn_mom, ln_one, ln_two
+    )
+    attn_grad = attn_low.astype(wide_type)
+    ffn_grad = ffn_low_grad.astype(wide_type)
+    attn_ortho = attn_ortho.astype(wide_type)
+    ffn_ortho = ffn_ortho.astype(wide_type)
     shard_width = ln_first.shape[1]
     ln_grad = lax.dynamic_slice_in_dim(
-        ln_sum, lax.axis_index("narrow") * shard_width, shard_width, 1
+        ln_sum[:4], lax.axis_index("narrow") * shard_width, shard_width, 1
     )
 
     attn_moment = momentum_keep * attn_mom + attn_grad
     ffn_moment = momentum_keep * ffn_mom + ffn_grad
-    mats = attn_w.shape[0] + ffn_w.shape[0]
-    attn_rows = attn_w.shape[1]
-    ffn_rows = ffn_w.shape[1]
-    padded = jnp.concatenate(
-        [
-            jnp.pad(attn_moment.astype(low_type), ((0, 0), (0, ffn_rows - attn_rows), (0, 0))),
-            ffn_moment.astype(low_type),
-        ],
-        axis=0,
-    )
-    mine = lax.dynamic_index_in_dim(
-        padded, jnp.minimum(lax.axis_index("wide"), mats - 1), 0, keepdims=False
-    )
-    gram = lax.psum(dot_tn(mine, mine), "narrow")
-    poly = lax.all_gather(newton_poly(gram).astype(low_type), "wide", axis=0, tiled=False)[:mats]
-    attn_ortho = jnp.einsum(
-        "jrd,jde->jre",
-        attn_moment.astype(low_type),
-        poly[: attn_w.shape[0]],
-        preferred_element_type=wide_type,
-    )
-    ffn_ortho = jnp.einsum(
-        "jrd,jde->jre",
-        ffn_moment.astype(low_type),
-        poly[attn_w.shape[0] :],
-        preferred_element_type=wide_type,
-    )
     keep_factor = 1.0 - muon_rate * muon_decay
     attn_new = keep_factor * attn_w - muon_rate * 0.2 * math.sqrt(D) * attn_ortho
     ffn_new = keep_factor * ffn_w - muon_rate * 0.2 * math.sqrt(FF) * ffn_ortho

time: 425 us -> 242 us (0.57)
  waiting for transfers between devices: 163 us -> 0.02 us
  Pallas kernels: 148 us -> 213 us
  blocking collectives: 50.8 us -> 0 us
  matrix products: 17.2 us -> 0 us
  local copies, waits for them, and re-layouts: 13.2 us -> 3.56 us
  other arithmetic: 16.9 us -> 9.75 us
    reduce_scatter x4 -> x0, waiting for transfers between devices: 99.6 us -> none  [the longest x1 47.3 us: sum_rows(): parts = lax.psum_scatter(parts, 'wide', scatter_dimension=2, tiled=False)]
    pallas_call x1 -> x2, Pallas kernels: 25.5 us -> 99.8 us  [the longest x1 60.7 us: update(): pl.pallas_call(functools.partial(update_kernel, narrow=narrow), in_specs=...]
    psum x1 -> x0, waiting for transfers between devices: 52.1 us -> none  [shards(): gram = lax.psum(dot_tn(mine, mine), 'narrow')]
    psum x1 -> x0, blocking collectives: 40.4 us -> none  [shards(): ln_sum = lax.psum(ln_full, ('wide', 'narrow'))]
    dot_general x6 -> x0, matrix products: 17.2 us -> none  [the longest x1 3.8 us: newton_poly(): return poly_one @ poly_two * (1.0 / scale)]
    all_gather x2 -> x1, waiting for transfers between devices: 11.2 us -> 0.01 us  [shards(): mom_in = lax.all_gather(moms, 'narrow', axis=1, tiled=True)]
    all_gather x1 -> x0, blocking collectives: 10.4 us -> none  [sum_rows(): return lax.all_gather(parts, 'wide', axis=1, tiled=True)]
    pallas_call x1, Pallas kernels: 64.6 us -> 55.3 us  [forward(): pl.pallas_call(functools.partial(forward_kernel, wide=wide, narrow=narrow...]
  transfers between devices with their start and end apart: 7 -> 1, of which waited for: 6 -> 0; matrix products, arithmetic and copies ran while one was open for 4% -> 0% of each run, Pallas kernels for 10% -> 40%
where the time goes in v4:
time: 242 us; the launch traced here: 240 us
  Pallas kernels  213 us (88%)
  between operations  14.1 us (6%)
  other arithmetic  9.75 us (4%)
  local copies, waits for them, and re-layouts  3.56 us (1%)
    pallas_call x1, Pallas kernels, update(): pl.pallas_call(functools.partial(update_kernel, narrow=narrow), in_specs=...  60.7 us
    pallas_call x1, Pallas kernels, forward(): pl.pallas_call(functools.partial(forward_kernel, wide=wide, narrow=narrow...  55.3 us
    pallas_call x1, Pallas kernels, feed(): pl.pallas_call(functools.partial(feed_kernel, per_seq=length // block), g...  41.4 us
    pallas_call x1, Pallas kernels, back(): pl.pallas_call(functools.partial(back_kernel, narrow=narrow), grid=(chunk...  39.1 us
    pallas_call x1, Pallas kernels, project_back(): pl.pallas_call(project_back_kernel, grid=(count // block,), in_specs=[row...  16.4 us
    add x1, other arithmetic, shards(): ffn_moment = momentum_keep * ffn_mom + ffn_grad  5.91 us
  transfers between devices with their start and end apart: 1, of which 0 were waited for; matrix products, arithmetic and copies ran while one was open for 0% of the time, Pallas kernels for 40%

profile of v4, /device:TPU:0, one launch (start us, length us, event | category | flops | bytes accessed | tf_op | source)
XLA Modules:
  0.0 240.3 jit_solution(16633312529552393156)
XLA Ops:
  7.2 0.0 all-gather.2.cloned.1.call-start
  7.2 2.1 slice.16
  9.3 55.3 %forward.1 = (bf16[2,1024,512]{2,1,0:T(8,128)(2,1)}, bf16[2,1024,512]{2,1,0:T(8,128)(2,1)}, bf16[2,1024,512]{2,1,0:T(8,128)(2,1)}, bf16[2,1024,512]{2,1,0:T(8,12...) custom-call(s32[2]{0:T(128)} %ids_ref.3, ...), custom_call_target="tpu_custom_call" | custom-call | tf_op jit(solution)/shard_map/forward/pallas_call | solution.py:738
  64.6 0.0 all-gather.2.cloned.1.call-update
  64.6 41.4 %feed.1 = (bf16[2048,512]{1,0:T(8,128)(2,1)}, f32[2048,512]{1,0:T(8,128)}, bf16[2048,512]{1,0:T(8,128)(2,1)}, bf16[2,512,2048]{2,1,0:T(8,128)(2,1)}, bf16[512,512]{1,0:T(8,128)(2,1)}, /*index=5*/f32[2,512]{1,0:T(2,128)}) custom-call(s32[2]{0:T(128)} %ids_ref.3, f32[8,128]{1,0:T(8,128)} %get-tuple-element.50.weight_ref, bf16[2048,512]{1,0:T(8,128)(2,1)} %bitcast.12, ...), custom_call_target="tpu_custom_call" | custom-call | tf_op jit(solution)/shard_map/feed/pallas_call | solution.py:280
  106.0 39.1 %back.1 = (bf16[2,1024,512]{2,1,0:T(8,128)(2,1)}, bf16[2,1024,512]{2,1,0:T(8,128)(2,1)}, bf16[2,1024,512]{2,1,0:T(8,128)(2,1)}, bf16[2,1024,512]{2,1,0:T(8,128)(...) custom-call(bf16[2,1024,512]{2,1,0:T(8,128)(2,1)} %get-tuple-element.56.refs_0_, ...), custom_call_target="tpu_custom_call" | custom-call | tf_op jit(solution)/shard_map/back/pallas_call | solution.py:930
  145.1 0.0 copy-start.2
  145.1 16.4 %project_back.1 = (f32[2048,512]{1,0:T(8,128)}, bf16[4,512,512]{2,1,0:T(8,128)(2,1)}, f32[2,512]{1,0:T(2,128)}) custom-call(bf16[2048,512]{1,0:T(8,128)(2,1)} %bitcast.13, f32[2048,512]{1,0:T(8,128)} %get-tuple-element.55.dx_ref, bf16[2048,512]{1,0:T(8,128)(2,1)} %bitcast.17, bf16[2048,512]{1,0:T(8,128)(2,1)} %bitcast.18, bf16[2048,512]{1,0:T(8,128)(2,1)} %bitcast.19, ...), custom_call_target="tpu_custom_call" | custom-call | tf_op jit(solution)/shard_map/project_back/pallas_call | solution.py:365
  161.5 0.0 copy-done.2
  161.5 0.7 slice_bitcast_fusion.mom_o_ref
  162.2 0.0 all-gather.2.cloned.1.call-done.mom_in_hbm
  162.2 0.0 copy-start
  162.2 60.7 %update.1 = (bf16[5,128,512]{2,1,0:T(8,128)(2,1)}, bf16[5,128,512]{2,1,0:T(8,128)(2,1)}, bf16[2,512,512]{2,1,0:T(8,128)(2,1)}, bf16[2,512,512]{2,1,0:T(8,128)(2,1)}, f32[8,512]{1,0:T(8,128)}) custom-call(bf16[4,512,512]{2,1,0:T(8,128)(2,1)} %get-tuple-element.73.gw_hbm, bf16[128,2048]{1,0:T(8,128)(2,1)} %get-tuple-element.74.fsum_ref, ...), custom_call_target="tpu_custom_call" | custom-call | tf_op jit(solution)/shard_map/update/pallas_call | solution.py:1297
  222.9 0.7 slice.12
  223.6 0.0 copy-done
  223.6 0.0 copy-start.1
  223.6 0.0 copy-start.3
  223.6 0.0 copy-start.4
  223.7 5.9 %multiply_add_fusion = (f32[2,512,512]{2,1,0:T(8,128)}, f32[2,512,512]{2,1,0:T(8,128)}, bf16[2,512,512]{2,1,0:T(8,128)(2,1)}, f32[2,512,512]{2,1,0:T(8,128)}) fusion(f32[2,512,512]{2,1,0:T(8,128)} %mom_f_hbm.1, bf16[2,512,512]{2,1,0:T(8,128)(2,1)} %get-tuple-element.80, bf16[2,512,512]{2,1,0:T(8,128)(2,1)} %get-tuple-element.83, f32[2,512,512]{2,1,0:T(8,128)S(1)} %copy-done), kind=kLoop, calls=%fused_computation.1 | loop fusion | flops 4194304 | bytes 13631488 | tf_op jit(solution)/shard_map/add | solution.py:1378
  229.6 0.0 copy-done.1
  229.6 0.0 copy-done.3
  229.6 0.0 copy-done.4
  229.6 0.0 copy-start.5
  229.6 0.0 copy-start.6
  229.6 2.5 %multiply_add_fusion.1 = (f32[5,128,512]{2,1,0:T(8,128)}, f32[5,128,512]{2,1,0:T(8,128)}, bf16[5,128,512]{2,1,0:T(8,128)(2,1)}, f32[5,128,512]{2,1,0:T(8,128)}) fusion(f32[5,128,512]{2,1,0:T(8,128)S(1)} %copy-done.2, bf16[5,128,512]{2,1,0:T(8,128)(2,1)S(1)} %copy-done.3, bf16[5,128,512]{2,1,0:T(8,128)(2,1)S(1)} %copy-done.4, f32[5,128,512]{2,1,0:T(8,128)S(1)} %copy-done.1), kind=kLoop, calls=%fused_computation.3 | loop fusion | flops 2621440 | bytes 8519680 | tf_op jit(solution)/shard_map/add | solution.py:1377
  232.1 0.0 copy-done.5
  232.2 0.0 copy-done.6
  232.2 1.3 divide_subtract_fusion
Async XLA Ops:
  7.2 155.1 %all-gather.2.cloned.1.call-start = ((), (), s32[]{:S(2)}) async-start(), calls=%async_computation | async-start | bytes 2621440 | tf_op jit(solution)/shard_map/all_gather | solution.py:1346
  145.1 16.4 %copy-start.2 = (f32[5,128,512]{2,1,0:T(8,128)S(1)}, f32[5,128,512]{2,1,0:T(8,128)}, u32[]{:S(2)}) copy-start(f32[5,128,512]{2,1,0:T(8,128)} %param.17) | copy-start | bytes 3932164
  162.2 61.4 %copy-start = (f32[2,512,512]{2,1,0:T(8,128)S(1)}, f32[2,512,512]{2,1,0:T(8,128)}, u32[]{:S(2)}) copy-start(f32[2,512,512]{2,1,0:T(8,128)} %ffn_ref.1) | copy-start | bytes 6291460
  223.6 5.9 %copy-start.1 = (f32[5,128,512]{2,1,0:T(8,128)S(1)}, f32[5,128,512]{2,1,0:T(8,128)}, u32[]{:S(2)}) copy-start(f32[5,128,512]{2,1,0:T(8,128)} %attn_ref.1) | copy-start | bytes 3932164
  223.6 5.9 %copy-start.3 = (bf16[5,128,512]{2,1,0:T(8,128)(2,1)S(1)}, bf16[5,128,512]{2,1,0:T(8,128)(2,1)}, u32[]{:S(2)}) copy-start(bf16[5,128,512]{2,1,0:T(8,128)(2,1)} %get-tuple-element.79) | copy-start | bytes 1966084
  223.6 5.9 %copy-start.4 = (bf16[5,128,512]{2,1,0:T(8,128)(2,1)S(1)}, bf16[5,128,512]{2,1,0:T(8,128)(2,1)}, u32[]{:S(2)}) copy-start(bf16[5,128,512]{2,1,0:T(8,128)(2,1)} %get-tuple-element.82) | copy-start | bytes 1966084
  229.6 2.6 %copy-start.5 = (f32[4,128]{1,0:T(4,128)S(1)}, f32[4,128]{1,0:T(4,128)}, u32[]{:S(2)}) copy-start(f32[4,128]{1,0:T(4,128)} %param.21) | copy-start | bytes 6148
  229.6 2.6 %copy-start.6 = (f32[4,128]{1,0:T(4,128)S(1)}, f32[4,128]{1,0:T(4,128)}, u32[]{:S(2)}) copy-start(f32[4,128]{1,0:T(4,128)} %param.20) | copy-start | bytes 6148
Sparse Core Ops, SparseCore 0:
  64.7 47.9 all-gather.1

commit v5 on v4

--- a/solution.py
+++ b/solution.py
@@ -257,8 +257,8 @@
     gln_ref[0:1, :] += jnp.sum(dsecond * normed, axis=0, keepdims=True)
     gln_ref[1:2, :] += jnp.sum(dsecond, axis=0, keepdims=True)
     dmixed = dout + norm_back(dsecond, normed, inverse, ln_ref[2:3, :])
-    dx_ref[...] = dmixed
     datt = dmixed.astype(low_type)
+    dx_ref[...] = datt
     o_sum[...] += dot_tn(att, datt)
     datt_ref[...] = dot_nt(datt, wo_ref[...]).astype(low_type)
 
@@ -300,7 +300,7 @@
         ],
         out_shape=[
             jax.ShapeDtypeStruct((count, D), low_type),
-            jax.ShapeDtypeStruct((count, D), wide_type),
+            jax.ShapeDtypeStruct((count, D), low_type),
             jax.ShapeDtypeStruct((count, D), low_type),
             jax.ShapeDtypeStruct((2, D, FF), low_type),
             jax.ShapeDtypeStruct((D, D), low_type),
@@ -316,66 +316,99 @@
     )(ids, weights, rows, att, grad, wo, ffn, ln_params)
 
 
-def project_back_kernel(
-    x_ref,
+def finish_kernel(
     dx_ref,
-    dq_ref,
-    dk_ref,
-    dv_ref,
-    de_ref,
-    w_ref,
+    dz_ref,
+    ga_ref,
+    sa_ref,
+    wa_ref,
+    ma_ref,
+    gf_ref,
+    sf_ref,
+    wf_ref,
+    mf_ref,
     ln_ref,
+    first_ref,
+    second_ref,
+    sum_ref,
     grad_ref,
-    gw_ref,
-    gln_ref,
-    w_sum,
+    ga_out,
+    ma_out,
+    wa_out,
+    ca_out,
+    gf_out,
+    mf_out,
+    wf_out,
+    cf_out,
+    gl_out,
+    first_out,
+    second_out,
+    ln_out,
 ):
-    step = pl.program_id(0)
-
-    @pl.when(step == 0)
-    def _():
-        w_sum[...] = jnp.zeros_like(w_sum)
-        gln_ref[...] = jnp.zeros_like(gln_ref)
-
-    parts = (dq_ref, dk_ref, dv_ref, de_ref)
-    dfirst = dot_nt(dq_ref[...], w_ref[0])
-    for place in range(1, 4):
-        dfirst = dfirst + dot_nt(parts[place][...], w_ref[place])
-    normed, inverse = normalize(x_ref[...].astype(wide_type))
-    first_t = (normed * ln_ref[0:1, :] + ln_ref[1:2, :]).astype(low_type).T
-    for place in range(4):
-        w_sum[place] += dot_nn(first_t, parts[place][...])
-    gln_ref[0:1, :] += jnp.sum(dfirst * normed, axis=0, keepdims=True)
-    gln_ref[1:2, :] += jnp.sum(dfirst, axis=0, keepdims=True)
-    grad_ref[...] = dx_ref[...] + norm_back(dfirst, normed, inverse, ln_ref[0:1, :])
-
-    @pl.when(step == pl.num_programs(0) - 1)
-    def _():
-        gw_ref[...] = w_sum[...].astype(low_type)
-
-
-def project_back(rows, dx, dq, dk, dv, de, weights, ln_params):
-    count = rows.shape[0]
-    block = 512
-    row_spec = pl.BlockSpec((block, D), lambda i: (i, 0))
-
-    def whole(*shape):
-        return pl.BlockSpec(shape, lambda i: (0,) * len(shape))
-
+    grad_ref[...] = dx_ref[...].astype(wide_type) + dz_ref[...].astype(wide_type)
+    keep = 1.0 - muon_rate * muon_decay
+    for refs, size in (
+        ((ga_ref, sa_ref, wa_ref, ma_ref, ga_out, ma_out, wa_out, ca_out), D),
+        ((gf_ref, sf_ref, wf_ref, mf_ref, gf_out, mf_out, wf_out, cf_out), FF),
+    ):
+        grad, ortho, weight, moment, grad_out, moment_out, weight_out, copy_out = refs
+        grad = grad[...].astype(wide_type)
+        grad_out[...] = grad
+        moment_out[...] = momentum_keep * moment[...] + grad
+        rate = muon_rate * 0.2 * math.sqrt(size)
+        new = keep * weight[...] - rate * ortho[...].astype(wide_type)
+        weight_out[...] = new
+        copy_out[...] = new.astype(low_type)
+    width = first_ref.shape[1]
+    place = lax.axis_index("narrow")
+
+    def own(ref):
+        picked = jnp.zeros((4, width), wide_type)
+        for at in range(D // width):
+            picked = picked + jnp.where(place == at, ref[0:4, at * width : (at + 1) * width], 0.0)
+        return picked
+
+    grad = own(sum_ref)
+    first = beta_first * first_ref[...] + (1.0 - beta_first) * grad
+    second = beta_second * second_ref[...] + (1.0 - beta_second) * grad * grad
+    gl_out[...] = grad
+    first_out[...] = first
+    second_out[...] = second
+    first_fix = 1.0 - beta_first**STEP
+    second_fix = 1.0 - beta_second**STEP
+    ln_out[...] = own(ln_ref) - adam_rate * (first / first_fix) / (
+        jnp.sqrt(second / second_fix) + adam_epsilon
+    )
+
+
+def finish(dx, dz, attn, ffn, ln):
+    steps = 8
+
+    def rows(item):
+        block = item.shape[0] // steps
+        return pl.BlockSpec((block, item.shape[1]), lambda i: (i, 0))
+
+    def whole(item):
+        return pl.BlockSpec(item.shape, lambda i: (0, 0))
+
+    def outs(group):
+        shape = group[0].shape
+        return [jax.ShapeDtypeStruct(shape, wide_type)] * 3 + [
+            jax.ShapeDtypeStruct(shape, low_type)
+        ]
+
+    row_items = [dx, dz] + list(attn) + list(ffn)
+    row_outs = [jax.ShapeDtypeStruct(dx.shape, wide_type)] + outs(attn) + outs(ffn)
+    ln_outs = [jax.ShapeDtypeStruct(ln[1].shape, wide_type)] * 4
     return pl.pallas_call(
-        project_back_kernel,
-        grid=(count // block,),
-        in_specs=[row_spec] * 6 + [whole(4, D, D), whole(4, D)],
-        out_specs=[row_spec, whole(4, D, D), whole(2, D)],
-        out_shape=[
-            jax.ShapeDtypeStruct((count, D), wide_type),
-            jax.ShapeDtypeStruct((4, D, D), low_type),
-            jax.ShapeDtypeStruct((2, D), wide_type),
-        ],
-        scratch_shapes=[pltpu.VMEM((4, D, D), wide_type)],
+        finish_kernel,
+        grid=(steps,),
+        in_specs=[rows(item) for item in row_items] + [whole(item) for item in ln],
+        out_specs=[rows(item) for item in row_outs] + [whole(item) for item in ln_outs],
+        out_shape=row_outs + ln_outs,
         compiler_params=pltpu.CompilerParams(vmem_limit_bytes=VMEM_BYTES),
-        name="project_back",
-    )(rows, dx, dq, dk, dv, de, weights, ln_params)
+        name="finish",
+    )(*row_items, *ln)
 
 
 MESH = pl.DeviceIdType.MESH
@@ -614,12 +647,13 @@
     def _():
         state[...] = jnp.zeros_like(state)
         carry[...] = jnp.zeros_like(carry)
-        own[...] = attn_ref[...].astype(low_type)
+        own[chip, at(core, half), :] = attn_ref[chip, at(core, half), :].astype(low_type)
         greet(column + plane)
         for place in range(narrow - 1):
             in_z(place).start()
+        own[4] = attn_ref[4].astype(low_type)
         for place in range(4):
-            in_w[place, at(z, rows), :] = own[place]
+            in_w[place, at(z, rows), :] = attn_ref[place].astype(low_type)
         own_ffn[...] = ffn_ref[...].astype(low_type)
         lanes = lane_of((8, LANES))
         count = jnp.zeros((8, LANES), wide_type)
@@ -864,111 +898,293 @@
     return low_dot(poly_one, poly_two) * scale
 
 
-def back_kernel(*refs, narrow):
+def back_kernel(*refs, narrow, chunks):
     blocks = list(refs[:9])
-    gffn_hbm, go_hbm = refs[9:11]
-    outs = list(refs[11:15])
-    fsum_ref, osum_ref = refs[15:17]
-    (state, carry, own_f, got_f, far_f, own_o, got_o, cut_o, far_o, sems) = refs[17:]
+    xc_ref, x_ref, w_ref, ln_ref, gffn_hbm, go_hbm, mom_hbm = refs[9:16]
+    dz_ref, gln_ref, wsum_ref, fsum_ref, osum_ref, mom_ref = refs[16:22]
+    state, carry, dq_all, dk_all, dv_all, de_all, first_t = refs[22:29]
+    own_f, got_f, far_f, col_f, own_o, got_o, cut_o, far_o, col_o = refs[29:38]
+    low_f, low_o, mom_own, mom_low, mom_all = refs[38:43]
+    grad_w, got_w, half_w, far_w, staged, sems = refs[43:]
     step = pl.program_id(0)
     steps = pl.num_programs(0)
     here = Place(narrow)
     copies = Copies(sems)
     half = D // 2
     part = D // 4
-    rows = cut_o.shape[2]
+    rows = D // narrow
+    ffn_rows = FF // narrow
+    column = range(narrow - 1)
+    own_cols = blocks_at(here.core, half)
+    mate_cols = blocks_at(here.other, half)
+    grads = (dq_all, dk_all, dv_all, de_all)
 
     keep_f = copies.local(gffn_hbm.at[here.core], own_f)
-    keep_o = copies.local(go_hbm.at[:, blocks_at(here.core, half)], own_o)
-    core_f = copies.remote(gffn_hbm.at[here.other], got_f, here.mate)
-    core_o = copies.remote(go_hbm.at[:, blocks_at(here.other, half)], got_o, here.mate)
-    plane_f, plane_o = [], []
+    keep_o = copies.local(go_hbm.at[:, own_cols], own_o)
+    keep_mom = copies.local(mom_hbm.at[pl.ds(0, 4)], mom_own)
+    mate_sum = [
+        copies.remote(gffn_hbm.at[here.other], got_f, here.mate),
+        copies.remote(go_hbm.at[:, mate_cols], got_o, here.mate),
+    ]
+    plane_sum = []
     for hop in range(3):
         there = here.chip_at[hop]
-        plane_f.append(
+        plane_sum.append(
             copies.remote(own_f.at[blocks_at(there, part)], far_f.at[hop], here.chips[hop])
         )
-        plane_o.append(copies.remote(cut_o.at[:, there], far_o.at[hop], here.chips[hop]))
+        plane_sum.append(copies.remote(cut_o.at[:, there], far_o.at[hop], here.chips[hop]))
+    z_sum = []
+    for i in column:
+        there = here.column_z[i]
+        z_sum.append(
+            copies.remote(low_f.at[:, blocks_at(there, ffn_rows)], col_f.at[i], here.column[i])
+        )
+        z_sum.append(copies.remote(low_o.at[there], col_o.at[i], here.column[i]))
+    z_mom = [
+        copies.remote(
+            mom_low.at[lax.rem(here.column_z[i], 4), :, own_cols],
+            mom_all.at[blocks_at(here.z, rows), own_cols],
+            here.column[i],
+        )
+        for i in column
+    ]
+    mate_mom = copies.remote(mom_all.at[:, own_cols], mom_all.at[:, own_cols], here.mate)
+    mate_w = [
+        copies.remote(grad_w.at[m, :, mate_cols], got_w.at[m], here.mate) for m in range(4)
+    ]
+    plane_w = [
+        [
+            copies.remote(
+                half_w.at[m, blocks_at(here.chip_at[hop], part)],
+                far_w.at[hop, m],
+                here.chips[hop],
+            )
+            for hop in range(3)
+        ]
+        for m in range(4)
+    ]
+
+    def gradient(m):
+        total = dot_nn(first_t[...], grads[m][...].reshape(-1, D))
+        grad_w[m] = total.astype(low_type)
+        mate_w[m].start()
+
+    def over_cores(m):
+        mate_w[m].wait()
+        half_w[m] = wide_sum([grad_w[m, :, own_cols], got_w[m]]).astype(low_type)
+        for copy in plane_w[m]:
+            copy.start()
+
+    def over_chips(m):
+        for copy in plane_w[m]:
+            copy.wait()
+        mine = half_w[m, blocks_at(here.chip, part), :]
+        wsum_ref[m] = wide_sum([mine] + [far_w[hop, m] for hop in range(3)]).astype(low_type)
 
     @pl.when(step == 0)
     def _():
         state[...] = jnp.zeros_like(state)
         carry[...] = jnp.zeros_like(carry)
-        greet(here.chips + [here.mate])
-        for copy in (core_f, core_o, keep_f, keep_o):
+        gln_ref[...] = jnp.zeros_like(gln_ref)
+        greet(here.column + here.chips + [here.mate])
+        for copy in mate_sum + [keep_f, keep_o, keep_mom]:
             copy.start()
 
-    @pl.when(step == steps // 4)
+    @pl.when(step == 1)
     def _():
-        for copy in (core_f, core_o, keep_f, keep_o):
+        keep_mom.wait()
+        mom_low[...] = mom_own[...].astype(low_type)
+        for copy in z_mom:
+            copy.start()
+        mom_all[blocks_at(here.z, rows), own_cols] = mom_low[lax.rem(here.z, 4), :, own_cols]
+
+    @pl.when(step == chunks // 4)
+    def _():
+        for copy in mate_sum + [keep_f, keep_o]:
             copy.wait()
         own_f[...] = wide_sum([own_f[...], got_f[...]]).astype(low_type)
         cut_o[...] = wide_sum([own_o[...], got_o[...]]).astype(low_type).reshape(cut_o.shape)
-        for copy in plane_f + plane_o:
+        for copy in plane_sum:
             copy.start()
 
-    attend_back_chunk(blocks + outs, state, carry)
+    @pl.when(step < chunks)
+    def _():
+        chunk = chunks - 1 - step
+        seqs = xc_ref.shape[0]
+        for seq in range(seqs):
+            normed, _ = normalize(xc_ref[seq].astype(wide_type))
+            first = (normed * ln_ref[0:1, :] + ln_ref[1:2, :]).astype(low_type)
+            first_t[:, blocks_at(chunk * seqs + seq, CHUNK)] = first.T
+        attend_back_chunk(blocks + [staged.at[place] for place in range(4)], state, carry)
+        for place in range(4):
+            grads[place][chunk] = staged[place]
+
+    @pl.when(step == chunks)
+    def _():
+        gradient(0)
+        gradient(1)
+        for copy in z_mom:
+            copy.wait_recv()
+        mate_mom.start()
+
+    @pl.when(step == chunks + 1)
+    def _():
+        over_cores(0)
+        over_cores(1)
+        for copy in plane_sum:
+            copy.wait()
+        mine = own_f[blocks_at(here.chip, part), :]
+        low_f[...] = wide_sum([mine] + [far_f[hop] for hop in range(3)]).astype(low_type)
+        mine = cut_o[:, here.chip]
+        low_o[...] = wide_sum([mine] + [far_o[hop] for hop in range(3)]).astype(low_type)
+        for copy in z_sum:
+            copy.start()
+        gradient(2)
+        gradient(3)
+
+    @pl.when(step == chunks + 2)
+    def _():
+        over_cores(2)
+        over_cores(3)
+
+    @pl.when(step >= chunks)
+    def _():
+        per = chunks // 4
+        seqs = x_ref.shape[0]
+        parts = [item[pl.ds((step - chunks) * per, per)].reshape(-1, D) for item in grads]
+        dfirst = dot_nt(parts[0], w_ref[0])
+        for place in range(1, 4):
+            dfirst = dfirst + dot_nt(parts[place], w_ref[place])
+        spans = [slice(at * CHUNK, (at + 1) * CHUNK) for at in range(per)]
+        rows_in = [x_ref[:, span, :].reshape(-1, D) for span in spans]
+        normed, inverse = normalize(jnp.concatenate(rows_in, axis=0).astype(wide_type))
+        gln_ref[0:1, :] += jnp.sum(dfirst * normed, axis=0, keepdims=True)
+        gln_ref[1:2, :] += jnp.sum(dfirst, axis=0, keepdims=True)
+        dz = norm_back(dfirst, normed, inverse, ln_ref[0:1, :]).astype(low_type)
+        for at, span in enumerate(spans):
+            size = seqs * CHUNK
+            dz_ref[:, span, :] = dz[at * size : (at + 1) * size].reshape(seqs, CHUNK, D)
 
     @pl.when(step == steps - 1)
     def _():
-        for copy in plane_f + plane_o:
+        mate_mom.wait()
+        mom_ref[...] = mom_all[...]
+        for m in range(4):
+            over_chips(m)
+        for copy in z_sum:
             copy.wait()
-        mine = own_f[blocks_at(here.chip, part), :]
-        fsum_ref[...] = wide_sum([mine] + [far_f[hop] for hop in range(3)]).astype(low_type)
-        mine = cut_o[:, here.chip]
-        osum_ref[...] = wide_sum([mine] + [far_o[hop] for hop in range(3)]).astype(low_type)
-
-
-def back(q, k, v, a, share, logit, before, datt, states, gffn, go):
+        mine = low_f[:, blocks_at(here.z, ffn_rows)]
+        fsum_ref[...] = wide_sum([mine] + [col_f[i] for i in column]).astype(low_type)
+        osum_ref[...] = wide_sum([low_o[here.z]] + [col_o[i] for i in column]).astype(low_type)
+        for copy in z_mom:
+            copy.wait_send()
+
+
+def back(q, k, v, a, share, logit, before, datt, states, tokens, in_w, ln_params, gffn, go, mom):
     seqs, length, _ = q.shape
     chunks = length // CHUNK
     narrow = lax.axis_size("narrow")
-    rows = D // narrow // 4
-    block = pl.BlockSpec((seqs, CHUNK, D), lambda i: (0, chunks - 1 - i, 0))
+    small, half, part = D // narrow // 4, D // 2, D // 4
+    ffn_rows = FF // narrow
+
+    def chunk_at(i):
+        return jnp.maximum(chunks - 1 - i, 0)
+
+    def rows_at(i):
+        return (0, jnp.maximum(i - chunks, 0), 0)
+
+    def whole(*shape):
+        return pl.BlockSpec(shape, lambda i: (0,) * len(shape))
+
+    block = pl.BlockSpec((seqs, CHUNK, D), lambda i: (0, chunk_at(i), 0))
+    row_spec = pl.BlockSpec((seqs, length // 4, D), rows_at)
     any_spec = pl.BlockSpec(memory_space=pl.ANY)
-    f_shape, o_shape = (D // 4, FF), (narrow, rows, D // 2)
+    outs = [(4, part, half), (part, ffn_rows), (small, half), (D, D)]
+
+    def low(*shape):
+        return pltpu.VMEM(shape, low_type)
+
     return pl.pallas_call(
-        functools.partial(back_kernel, narrow=narrow),
-        grid=(chunks,),
+        functools.partial(back_kernel, narrow=narrow, chunks=chunks),
+        grid=(chunks + 4,),
         in_specs=[block] * 6
         + [
-            pl.BlockSpec((1, seqs, 1, D), lambda i: (chunks - 1 - i, 0, 0, 0)),
+            pl.BlockSpec((1, seqs, 1, D), lambda i: (chunk_at(i), 0, 0, 0)),
             block,
-            pl.BlockSpec(
-                (1, seqs, PAIRS, PAIR, 2 * PAIR), lambda i: (chunks - 1 - i, 0, 0, 0, 0)
-            ),
+            pl.BlockSpec((1, seqs, PAIRS, PAIR, 2 * PAIR), lambda i: (chunk_at(i), 0, 0, 0, 0)),
+            block,
+            row_spec,
+            whole(4, D, D),
+            whole(4, D),
+            any_spec,
             any_spec,
             any_spec,
         ],
-        out_specs=[block] * 4
-        + [pl.BlockSpec(f_shape, lambda i: (0, 0)), pl.BlockSpec(o_shape, lambda i: (0, 0, 0))],
-        out_shape=[jax.ShapeDtypeStruct(q.shape, low_type)] * 4
-        + [jax.ShapeDtypeStruct(f_shape, low_type), jax.ShapeDtypeStruct(o_shape, low_type)],
+        out_specs=[row_spec, whole(2, D)] + [whole(*shape) for shape in outs],
+        out_shape=[
+            jax.ShapeDtypeStruct(q.shape, low_type),
+            jax.ShapeDtypeStruct((2, D), wide_type),
+        ]
+        + [jax.ShapeDtypeStruct(shape, low_type) for shape in outs],
         scratch_shapes=[
             pltpu.VMEM((seqs, PAIRS, PAIR, 2 * PAIR), wide_type),
             pltpu.VMEM((seqs, 1, D), wide_type),
-            pltpu.VMEM((D, FF), low_type),
-            pltpu.VMEM((D, FF), low_type),
-            pltpu.VMEM((3,) + f_shape, low_type),
-            pltpu.VMEM((D, D // 2), low_type),
-            pltpu.VMEM((D, D // 2), low_type),
-            pltpu.VMEM((narrow, 4, rows, D // 2), low_type),
-            pltpu.VMEM((3,) + o_shape, low_type),
-            pltpu.SemaphoreType.DMA((24,)),
+            low(chunks, seqs, CHUNK, D),
+            low(chunks, seqs, CHUNK, D),
+            low(chunks, seqs, CHUNK, D),
+            low(chunks, seqs, CHUNK, D),
+            low(D, seqs * length),
+            low(D, FF),
+            low(D, FF),
+            low(3, part, FF),
+            low(narrow - 1, part, ffn_rows),
+            low(D, half),
+            low(D, half),
+            low(narrow, 4, small, half),
+            low(3, narrow, small, half),
+            low(narrow - 1, small, half),
+            low(part, FF),
+            low(narrow, small, half),
+            pltpu.VMEM((4, D // narrow, D), wide_type),
+            low(4, D // narrow, D),
+            low(D, D),
+            low(4, D, D),
+            low(4, D, half),
+            low(4, D, half),
+            low(3, 4, part, half),
+            low(4, seqs, CHUNK, D),
+            pltpu.SemaphoreType.DMA((3 + 2 * (2 + 6 + 3 * (narrow - 1) + 1 + 4 + 12),)),
         ],
         compiler_params=pltpu.CompilerParams(
             vmem_limit_bytes=VMEM_BYTES, collective_id=1, has_side_effects=True
         ),
         name="back",
-    )(q, k, v, a, share, logit, before, datt, states, gffn, go)
+    )(
+        q,
+        k,
+        v,
+        a,
+        share,
+        logit,
+        before,
+        datt,
+        states,
+        tokens,
+        tokens,
+        in_w,
+        ln_params,
+        gffn,
+        go,
+        mom,
+    )
 
 
 def update_kernel(
-    gw_hbm,
+    wsum_ref,
     fsum_ref,
     osum_ref,
-    mom_in_hbm,
-    mom_o_ref,
+    mom_w_ref,
+    mom_hbm,
     mom_f_hbm,
     ln_one_ref,
     ln_two_ref,
@@ -981,23 +1197,17 @@
     ln_mate,
     ln_chips,
     ln_column,
-    half_w,
-    half_got,
-    far_w,
-    cut_w,
     col_w,
     grad_w,
-    mom_w,
     moment_w,
     poly_w,
     send_w,
     all_w,
-    col_f,
     all_f,
     mom_f,
+    mom_o,
     moment_f,
     out_f,
-    col_o,
     all_o,
     moment_o,
     step_o,
@@ -1025,7 +1235,6 @@
     column = range(narrow - 1)
     planes = range(3)
     own_cols = blocks_at(core, half)
-    mate_cols = blocks_at(here.other, half)
     own_quarter = blocks_at(chip, quarter)
     own_small = blocks_at(chip, small)
     matrix = lax.rem(z, 4)
@@ -1039,30 +1248,20 @@
     def same(block):
         return lambda i: block
 
-    keep_w = copies.local(gw_hbm.at[:, :, own_cols], half_w)
-    keep_mom = copies.local(mom_in_hbm.at[matrix], mom_w)
     keep_f = copies.local(mom_f_hbm.at[core], mom_f)
-    mate_sum = [
-        copies.remote(gw_hbm.at[:, :, mate_cols], half_got, here.mate),
-        copies.remote(ln_now, ln_mate, here.mate),
-    ]
-    z_sum_f = to_column(
-        lambda i: fsum_ref.at[:, blocks_at(here.column_z[i], ffn_rows)], lambda i: col_f.at[i]
-    ) + to_column(lambda i: osum_ref.at[here.column_z[i]], lambda i: col_o.at[i])
-    plane_sum = to_plane(
-        lambda i: half_w.at[:, blocks_at(here.chip_at[i], quarter)], lambda i: far_w.at[i]
-    )
+    keep_o = copies.local(mom_hbm.at[4], mom_o)
+    mate_ln = [copies.remote(ln_now, ln_mate, here.mate)]
     plane_ln = to_plane(same(ln_now), lambda i: ln_chips.at[i])
     block = all_f.at[own_quarter]
     plane_f = to_plane(same(block), same(block))
     block = all_o.at[own_small, own_cols]
     plane_f = plane_f + to_plane(same(block), same(block))
-    z_sum = to_column(lambda i: cut_w.at[lax.rem(here.column_z[i], 4)], lambda i: col_w.at[i])
+    z_sum = to_column(lambda i: wsum_ref.at[lax.rem(here.column_z[i], 4)], lambda i: col_w.at[i])
     z_ln = to_column(same(ln_now), lambda i: ln_column.at[i])
     block = out_f.at[0, core]
-    mate_f = copies.remote(block, block, here.mate)
+    mate_f = [copies.remote(block, block, here.mate)]
     block = all_o.at[:, own_cols]
-    mate_o = copies.remote(block, block, here.mate)
+    mate_o = [copies.remote(block, block, here.mate)]
     z_gf = to_column(
         lambda i: cut_gf.at[blocks_at(here.column_z[i], strip)], lambda i: col_gf.at[i]
     )
@@ -1072,7 +1271,7 @@
         lambda i: cut_go.at[blocks_at(here.column_z[i], strip)], lambda i: col_go.at[i]
     )
     block = grad_w.at[:, own_cols]
-    mate_w = copies.remote(block, block, here.mate)
+    mate_w = [copies.remote(block, block, here.mate)]
     block = strips_gf.at[blocks_at(z, strip)]
     z_back_f = to_column(same(block), same(block))
     block = strips_go.at[blocks_at(z, strip)]
@@ -1081,29 +1280,33 @@
     plane_gf = to_plane(same(block), same(block))
     block = gram_o.at[own_quarter, own_cols]
     plane_go = to_plane(same(block), same(block))
-    spread = []
-    for hop in range(1, 4):
-        there = z - matrix + lax.rem(matrix + hop, 4)
-        spread.append(
+    quad = [z - matrix + lax.rem(matrix + hop, 4) for hop in range(1, 4)]
+
+    def hand_back(kind):
+        spread = [
             copies.remote(
-                send_w.at[there],
-                all_w.at[matrix, :, own_small, own_cols],
+                send_w.at[kind, there],
+                all_w.at[kind, matrix, own_small, own_cols],
                 (lax.axis_index("wide"), there),
             )
-        )
+            for there in quad
+        ]
+        block = all_w.at[kind, :, own_small, own_cols]
+        plane = to_plane(same(block), same(block))
+        block = all_w.at[kind, :, :, own_cols]
+        return spread, plane, [copies.remote(block, block, here.mate)]
+
+    spread_g, plane_g, mate_g = hand_back(0)
+    spread_s, plane_s, mate_s = hand_back(1)
     block = gram_o.at[:, own_cols]
-    mate_go = copies.remote(block, block, here.mate)
+    mate_go = [copies.remote(block, block, here.mate)]
     block = out_f.at[1, core]
-    mate_x = copies.remote(block, block, here.mate)
-    block = all_w.at[:, :, own_small, own_cols]
-    plane_all = to_plane(same(block), same(block))
-    block = all_w.at[:, :, :, own_cols]
-    mate_all = copies.remote(block, block, here.mate)
+    mate_x = [copies.remote(block, block, here.mate)]
     write_f = [copies.local(out_f.at[0], grad_ffn), copies.local(out_f.at[1], step_ffn)]
     write_o = [copies.local(all_o, grad_attn.at[4]), copies.local(step_o, step_attn.at[4])]
     write_w = [
-        copies.local(all_w.at[:, 0], grad_attn.at[pl.ds(0, 4)]),
-        copies.local(all_w.at[:, 1], step_attn.at[pl.ds(0, 4)]),
+        copies.local(all_w.at[0], grad_attn.at[pl.ds(0, 4)]),
+        copies.local(all_w.at[1], step_attn.at[pl.ds(0, 4)]),
     ]
     sent = []
 
@@ -1121,130 +1324,122 @@
             copy.start()
 
     greet(here.column + here.chips + [here.mate])
-    keep_w.start()
+    start(z_sum)
+    all_f[own_quarter, :] = fsum_ref[...]
+    all_o[own_small, own_cols] = osum_ref[...]
+    start(plane_f)
+    begin([keep_f, keep_o])
     ln_now[...] = jnp.zeros_like(ln_now)
     ln_now[0:2, :] = ln_one_ref[...]
     ln_now[2:4, :] = ln_two_ref[...]
-    start(mate_sum)
-    start(z_sum_f)
-    begin([keep_f, keep_mom])
-
-    keep_w.wait()
-    arrive(mate_sum)
-    half_w[...] = wide_sum([half_w[...], half_got[...]]).astype(low_type)
-    start(plane_sum)
-    mate_sum[1].wait_send()
+    start(mate_ln)
+
+    arrive(z_sum)
+    total = wide_sum([wsum_ref[matrix]] + [col_w[i] for i in column])
+    grad_w[own_quarter, own_cols] = total.astype(low_type)
+    start(plane_w)
+    arrive(mate_ln)
+    mate_ln[0].wait_send()
     ln_now[...] = ln_now[...] + ln_mate[...]
     start(plane_ln)
 
-    arrive(z_sum_f)
-    total = wide_sum([fsum_ref[:, blocks_at(z, ffn_rows)]] + [col_f[i] for i in column])
-    all_f[own_quarter, :] = total.astype(low_type)
-    total = wide_sum([osum_ref[z]] + [col_o[i] for i in column])
-    all_o[own_small, own_cols] = total.astype(low_type)
-    start(plane_f)
-
-    arrive(plane_sum)
-    mine = half_w[:, own_quarter, :]
-    cut_w[...] = wide_sum([mine] + [far_w[i] for i in planes]).astype(low_type)
-    start(z_sum)
+    keep_f.wait()
+    arrive(plane_f)
+    start(mate_o)
+    grad = all_f[...].T
+    out_f[0, core] = grad
+    start(mate_f)
+    moment_f[...] = (momentum_keep * mom_f[...] + grad.astype(wide_type)).astype(low_type)
+    cut_gf[...] = dot_tn(moment_f[:, own_quarter], moment_f[...]).astype(low_type)
+    start(z_gf)
+
+    arrive(plane_w)
+    start(mate_w)
     arrive(plane_ln)
     for copy in plane_ln:
         copy.wait_send()
     ln_now[...] = ln_now[...] + ln_chips[0] + ln_chips[1] + ln_chips[2]
     start(z_ln)
 
-    keep_f.wait()
-    arrive(plane_f)
-    start([mate_o])
-    grad = all_f[...].T
-    out_f[0, core] = grad
-    start([mate_f])
-    moment_f[...] = (momentum_keep * mom_f[...] + grad.astype(wide_type)).astype(low_type)
-    cut_gf[...] = dot_tn(moment_f[:, own_quarter], moment_f[...]).astype(low_type)
-    start(z_gf)
-
-    arrive(z_sum)
-    total = wide_sum([cut_w[matrix]] + [col_w[i] for i in column])
-    grad_w[own_quarter, own_cols] = total.astype(low_type)
-    start(plane_w)
-
-    arrive([mate_o])
-    moment = momentum_keep * mom_o_ref[...] + all_o[...].astype(wide_type)
+    arrive(mate_o)
+    keep_o.wait()
+    moment = momentum_keep * mom_o[...] + all_o[...].astype(wide_type)
     moment_o[...] = moment.astype(low_type)
     cut_go[...] = dot_tn(moment_o[:, own_quarter], moment_o[:, own_cols]).astype(low_type)
     start(z_go)
 
-    arrive(plane_w)
-    start([mate_w])
-
+    def small_rows(there):
+        return pl.ds(pl.multiple_of(there * rows + chip * small, small), small)
+
+    arrive(mate_w)
+    for there in range(narrow):
+        send_w[0, there] = grad_w[small_rows(there), own_cols]
+    start(spread_g)
+    all_w[0, matrix, own_small, own_cols] = send_w[0, z]
+    moment = momentum_keep * mom_w_ref[...].astype(wide_type) + grad_w[...].astype(wide_type)
+    moment_w[...] = moment.astype(low_type)
+    gram = dot_tn(moment_w[...], moment_w[...])
     arrive(z_gf)
     total = wide_sum([cut_gf[blocks_at(z, strip), :]] + [col_gf[i] for i in column])
     strips_gf[blocks_at(z, strip), :] = total.astype(low_type)
     start(z_back_f)
+    poly_w[...] = newton_poly(gram).astype(low_type)
+    picked = jnp.concatenate([moment_w[small_rows(there), :] for there in range(narrow)], axis=0)
+    ortho = dot_nn(picked, poly_w[:, own_cols]).astype(low_type)
+    for there in range(narrow):
+        send_w[1, there] = ortho[there * small : (there + 1) * small, :]
+    start(spread_s)
+    all_w[1, matrix, own_small, own_cols] = send_w[1, z]
+
     arrive(z_go)
     total = wide_sum([cut_go[blocks_at(z, strip), :]] + [col_go[i] for i in column])
     strips_go[blocks_at(z, strip), :] = total.astype(low_type)
     start(z_back_o)
-
-    keep_mom.wait()
-    arrive([mate_w])
-    moment = momentum_keep * mom_w[...].astype(wide_type) + grad_w[...].astype(wide_type)
-    moment_w[...] = moment.astype(low_type)
-    gram = dot_tn(moment_w[...], moment_w[...])
-
     arrive(z_back_f)
     gram_f[own_quarter, :] = strips_gf[...]
     start(plane_gf)
+    arrive(spread_g)
+    start(plane_g)
     arrive(z_back_o)
     gram_o[own_quarter, own_cols] = strips_go[...]
     start(plane_go)
-
-    poly_w[...] = newton_poly(gram).astype(low_type)
-    picked = [moment_w[pl.ds(pl.multiple_of(there * rows + chip * small, small), small), :] for there in range(narrow)]
-    ortho = dot_nn(jnp.concatenate(picked, axis=0), poly_w[:, own_cols]).astype(low_type)
-    for there in range(narrow):
-        place = pl.ds(pl.multiple_of(there * rows + chip * small, small), small)
-        send_w[there, 0] = grad_w[place, own_cols]
-        send_w[there, 1] = ortho[there * small : (there + 1) * small, :]
-    start(spread)
-    all_w[matrix, :, own_small, own_cols] = send_w[z]
-
-    arrive(plane_go)
-    start([mate_go])
+    arrive(spread_s)
+    start(plane_s)
     arrive(plane_gf)
     poly = newton_poly(gram_f[...].astype(wide_type)).astype(low_type)
     out_f[1, core] = dot_nn(moment_f[...], poly).astype(low_type)
-    start([mate_x])
-
-    arrive(spread)
-    start(plane_all)
-
-    arrive([mate_go])
+    start(mate_x)
+    arrive(plane_g)
+    start(mate_g)
+    arrive(plane_go)
+    start(mate_go)
+    arrive(plane_s)
+    start(mate_s)
+    arrive(mate_go)
     poly = newton_poly(gram_o[...].astype(wide_type)).astype(low_type)
     step_o[...] = dot_nn(moment_o[...], poly).astype(low_type)
     begin(write_o)
-    arrive([mate_f, mate_x])
+    arrive(mate_f)
+    arrive(mate_x)
     begin(write_f)
     arrive(z_ln)
     total = ln_now[...]
     for i in column:
         total = total + ln_column[i]
     ln_ref[...] = total
-
-    arrive(plane_all)
-    start([mate_all])
-    arrive([mate_all])
-    begin(write_w)
+    arrive(mate_g)
+    begin(write_w[:1])
+    arrive(mate_s)
+    begin(write_w[1:])
     for copy in write_o + write_f + write_w:
         copy.wait()
-    settled = [id(copy) for copy in [mate_sum[1]] + plane_ln]
+    settled = [id(copy) for copy in mate_ln + plane_ln]
     for copy in sent:
         if id(copy) not in settled:
             copy.wait_send()
 
 
-def update(gw, fsum, osum, mom_in, mom_o, mom_f, ln_one, ln_two):
+def update(wsum, fsum, osum, mom_in, mom, mom_f, ln_one, ln_two):
     narrow = lax.axis_size("narrow")
     rows, ffn_rows = D // narrow, FF // narrow
     small, half, quarter = rows // 4, D // 2, D // 4
@@ -1264,23 +1459,17 @@
         full(8, D),
         full(3, 8, D),
         full(column, 8, D),
-        low(4, D, half),
-        low(4, D, half),
-        low(3, 4, quarter, half),
-        low(4, quarter, half),
         low(column, quarter, half),
         low(D, D),
         low(D, D),
         low(D, D),
-        low(D, D),
-        low(narrow, 2, small, half),
-        low(4, 2, rows, D),
-        low(column, quarter, ffn_rows),
+        low(2, narrow, small, half),
+        low(2, 4, rows, D),
         low(D, ffn_rows),
         full(ffn_rows, D),
+        full(rows, D),
         low(ffn_rows, D),
         low(2, 2, ffn_rows, D),
-        low(column, small, half),
         low(rows, D),
         low(rows, D),
         low(rows, D),
@@ -1292,11 +1481,11 @@
         low(column, strip, half),
         low(quarter, half),
         low(D, D),
-        pltpu.SemaphoreType.DMA((9 + 2 * (10 + 27 + 9 * column),)),
+        pltpu.SemaphoreType.DMA((8 + 2 * (38 + 6 * column),)),
     ]
     return pl.pallas_call(
         functools.partial(update_kernel, narrow=narrow),
-        in_specs=[any_spec, vmem, vmem, any_spec, vmem, any_spec, vmem, vmem],
+        in_specs=[vmem, vmem, vmem, vmem, any_spec, any_spec, vmem, vmem],
         out_specs=[any_spec, any_spec, any_spec, any_spec, vmem],
         out_shape=[
             jax.ShapeDtypeStruct((5, rows, D), low_type),
@@ -1310,7 +1499,7 @@
             vmem_limit_bytes=VMEM_BYTES, collective_id=2, has_side_effects=True
         ),
         name="update",
-    )(gw, fsum, osum, mom_in, mom_o, mom_f, ln_one, ln_two)
+    )(wsum, fsum, osum, mom_in, mom, mom_f, ln_one, ln_two)
 
 
 def group_sum(values):
@@ -1341,9 +1530,6 @@
     q, k, v, a, att, share, logit, before, states, weights, in_w, out_w, ffn_low = forward(
         tokens, group_ids, domain_weight, ln_params, attn_w, ffn_w
     )
-    moms = attn_mom[:4].astype(low_type)
-    moms, weights = lax.optimization_barrier((moms, weights))
-    mom_in = lax.all_gather(moms, "narrow", axis=1, tiled=True)
     output, dx, datt, gffn, go, ln_two = feed(
         group_ids,
         weights,
@@ -1355,52 +1541,51 @@
         ln_params,
         length,
     )
-    gffn, go, ln_two = group_sum((gffn, go, ln_two))
-    dq, dk, dv, de, fsum, osum = back(
-        q, k, v, a, share, logit, before, datt.reshape(head), states, gffn, go
+    dz, ln_one, wsum, fsum, osum, mom_in = back(
+        q,
+        k,
+        v,
+        a,
+        share,
+        logit,
+        before,
+        datt.reshape(head),
+        states,
+        tokens,
+        in_w,
+        ln_params,
+        gffn,
+        go,
+        attn_mom,
     )
-    dq, dk, dv, de = (item.reshape(token_count, D) for item in (dq, dk, dv, de))
-    input_grad, gw, ln_one = project_back(rows, dx, dq, dk, dv, de, in_w, ln_params)
-    gw, ln_one = group_sum((gw, ln_one))
-    attn_low, attn_ortho, ffn_low_grad, ffn_ortho, ln_sum = update(
-        gw, fsum, osum, mom_in, attn_mom[4], ffn_mom, ln_one, ln_two
+    wsum, fsum, osum, ln_one, ln_two = group_sum((wsum, fsum, osum, ln_one, ln_two))
+    attn_grad, attn_step, ffn_grad, ffn_step, ln_sum = update(
+        wsum, fsum, osum, mom_in, attn_mom, ffn_mom, ln_one, ln_two
     )
-    attn_grad = attn_low.astype(wide_type)
-    ffn_grad = ffn_low_grad.astype(wide_type)
-    attn_ortho = attn_ortho.astype(wide_type)
-    ffn_ortho = ffn_ortho.astype(wide_type)
-    shard_width = ln_first.shape[1]
-    ln_grad = lax.dynamic_slice_in_dim(
-        ln_sum[:4], lax.axis_index("narrow") * shard_width, shard_width, 1
+    def flat(*items):
+        return [item.reshape(-1, D) for item in items]
+
+    results = finish(
+        dx,
+        dz.reshape(token_count, D),
+        flat(attn_grad, attn_step, attn_w, attn_mom),
+        flat(ffn_grad, ffn_step, ffn_w, ffn_mom),
+        (ln_params, ln_first, ln_second, ln_sum),
     )
-
-    attn_moment = momentum_keep * attn_mom + attn_grad
-    ffn_moment = momentum_keep * ffn_mom + ffn_grad
-    keep_factor = 1.0 - muon_rate * muon_decay
-    attn_new = keep_factor * attn_w - muon_rate * 0.2 * math.sqrt(D) * attn_ortho
-    ffn_new = keep_factor * ffn_w - muon_rate * 0.2 * math.sqrt(FF) * ffn_ortho
-    own_params = lax.dynamic_slice_in_dim(
-        ln_params, lax.axis_index("narrow") * shard_width, shard_width, 1
-    )
-    first_new = beta_first * ln_first + (1.0 - beta_first) * ln_grad
-    second_new = beta_second * ln_second + (1.0 - beta_second) * ln_grad * ln_grad
-    first_fix = 1.0 - beta_first**STEP
-    second_fix = 1.0 - beta_second**STEP
-    ln_new = own_params - adam_rate * (first_new / first_fix) / (
-        jnp.sqrt(second_new / second_fix) + adam_epsilon
-    )
+    input_grad, ga, ma, wa, ca, gf, mf, wf, cf, ln_grad, first_new, second_new, ln_new = results
+    attn, ffn = attn_w.shape, ffn_w.shape
     return (
         output.reshape(tokens.shape),
         input_grad.reshape(tokens.shape),
-        attn_grad,
-        ffn_grad,
+        ga.reshape(attn),
+        gf.reshape(ffn),
         ln_grad,
-        attn_moment,
-        ffn_moment,
-        attn_new,
-        ffn_new,
-        attn_new.astype(low_type),
-        ffn_new.astype(low_type),
+        ma.reshape(attn),
+        mf.reshape(ffn),
+        wa.reshape(attn),
+        wf.reshape(ffn),
+        ca.reshape(attn),
+        cf.reshape(ffn),
         first_new,
         second_new,
         ln_new,

time: 242 us -> 211 us (0.87)
  between operations: 14.1 us -> 0.87 us
  other arithmetic: 9.75 us -> 0 us
  local copies, waits for them, and re-layouts: 3.56 us -> 0 us
  Pallas kernels: 213 us -> 210 us
    pallas_call x1, Pallas kernels: 60.7 us -> 43.9 us  [update(): pl.pallas_call(functools.partial(update_kernel, narrow=narrow), in_specs=...]
    pallas_call x2, Pallas kernels: 55.5 us -> 69 us  [the longest x1 56.1 us: back(): pl.pallas_call(functools.partial(back_kernel, narrow=narrow, chunks=chunk...]
    add x2 -> x0, other arithmetic: 8.46 us -> none  [the longest x1 5.91 us: shards(): ffn_moment = momentum_keep * ffn_mom + ffn_grad]
    slice x2 -> x0, local copies, waits for them, and re-layouts: 2.81 us -> none  [the longest x1 2.09 us: shards(): moms = attn_mom[:4].astype(low_type)]
  transfers between devices with their start and end apart: 1 -> 0, of which waited for: 0 -> 0; matrix products, arithmetic and copies ran while one was open for 0% -> 0% of each run, Pallas kernels for 40% -> 0%
where the time goes in v5:
time: 211 us; the launch traced here: 210 us
  Pallas kernels  210 us (100%)
    pallas_call x1, Pallas kernels, back(): pl.pallas_call(functools.partial(back_kernel, narrow=narrow, chunks=chunk...  56.1 us
    pallas_call x1, Pallas kernels, forward(): pl.pallas_call(functools.partial(forward_kernel, wide=wide, narrow=narrow...  55.3 us
    pallas_call x1, Pallas kernels, update(): pl.pallas_call(functools.partial(update_kernel, narrow=narrow), in_specs=...  43.9 us
    pallas_call x1, Pallas kernels, feed(): pl.pallas_call(functools.partial(feed_kernel, per_seq=length // block), g...  41.3 us
    pallas_call x1, Pallas kernels, finish(): pl.pallas_call(finish_kernel, grid=(steps,), in_specs=[rows(item) for ite...  12.9 us

profile of v5, /device:TPU:0, one launch (start us, length us, event | category | flops | bytes accessed | tf_op | source)
XLA Modules:
  0.0 210.4 jit_solution(2617827150597698338)
XLA Ops:
  0.6 55.3 %forward.1 = (bf16[2,1024,512]{2,1,0:T(8,128)(2,1)}, bf16[2,1024,512]{2,1,0:T(8,128)(2,1)}, bf16[2,1024,512]{2,1,0:T(8,128)(2,1)}, bf16[2,1024,512]{2,1,0:T(8,12...) custom-call(s32[2]{0:T(128)} %ids_ref.3, ...), custom_call_target="tpu_custom_call" | custom-call | tf_op jit(solution)/shard_map/forward/pallas_call | solution.py:772
  56.0 41.3 %feed.1 = (bf16[2048,512]{1,0:T(8,128)(2,1)}, bf16[2048,512]{1,0:T(8,128)(2,1)}, bf16[2048,512]{1,0:T(8,128)(2,1)}, bf16[2,512,2048]{2,1,0:T(8,128)(2,1)}, bf16[512,512]{1,0:T(8,128)(2,1)}, /*index=5*/f32[2,512]{1,0:T(2,128)}) custom-call(s32[2]{0:T(128)} %ids_ref.3, f32[8,128]{1,0:T(8,128)} %get-tuple-element.57.weight_ref, bf16[2048,512]{1,0:T(8,128)(2,1)} %bitcast.23, ...), custom_call_target="tpu_custom_call" | custom-call | tf_op jit(solution)/shard_map/feed/pallas_call | solution.py:280
  97.3 56.1 %back.1 = (bf16[2,1024,512]{2,1,0:T(8,128)(2,1)}, f32[2,512]{1,0:T(2,128)}, bf16[4,128,256]{2,1,0:T(8,128)(2,1)}, bf16[128,512]{1,0:T(8,128)(2,1)}, bf16[32,256]{1,0:T(8,128)(2,1)}, /*index=5*/bf16[512,512]{1,0:T(8,128)(2,1)}) custom-call(bf16[2,1024,512]{2,1,0:T(8,128)(2,1)} %get-tuple-element.63.refs_0_, bf16[2,1024,512]{2,1,0:T(8,128)(2,1)} %get-tuple-element.64.refs_1_, ...), custom_call_target="tpu_custom_call" | custom-call | tf_op jit(solution)/shard_map/back/pallas_call | solution.py:1107
  153.4 43.9 %update.1 = (bf16[5,128,512]{2,1,0:T(8,128)(2,1)}, bf16[5,128,512]{2,1,0:T(8,128)(2,1)}, bf16[2,512,512]{2,1,0:T(8,128)(2,1)}, bf16[2,512,512]{2,1,0:T(8,128)(2,1)}, f32[8,512]{1,0:T(8,128)}) custom-call(bf16[4,128,256]{2,1,0:T(8,128)(2,1)} %get-tuple-element.76.wsum_ref, bf16[128,512]{1,0:T(8,128)(2,1)} %get-tuple-element.77.fsum_ref, ...), custom_call_target="tpu_custom_call" | custom-call | tf_op jit(solution)/shard_map/update/pallas_call | solution.py:1486
  197.3 12.9 %finish.1 = (f32[2048,512]{1,0:T(8,128)}, f32[640,512]{1,0:T(8,128)}, f32[640,512]{1,0:T(8,128)}, f32[640,512]{1,0:T(8,128)}, bf16[640,512]{1,0:T(8,128)(2,1)}, ...) custom-call(bf16[2048,512]{1,0:T(8,128)(2,1)} %get-tuple-element.62., ...), custom_call_target="tpu_custom_call" | custom-call | tf_op jit(solution)/shard_map/finish/pallas_call | solution.py:403

commit v6 on v5

--- a/solution.py
+++ b/solution.py
@@ -382,7 +382,7 @@
 
 
 def finish(dx, dz, attn, ffn, ln):
-    steps = 8
+    steps = 4
 
     def rows(item):
         block = item.shape[0] // steps
@@ -433,8 +433,9 @@
     pl.semaphore_wait(barrier, len(devices))
 
 
-def attend_chunks(q_all, k_all, v_all, a_all, refs, seqs):
+def attend_chunks(source, refs, seqs, asides):
     att_ref, share_ref, logit_ref, before_ref, state_ref, state, carry = refs
+    q_in, k_in, v_in, a_in = source
     first_head = lane_of((CHUNK, PAIR)) < HEAD_DIM
     causal = row_of((CHUNK, 2 * CHUNK)) >= lane_of((CHUNK, 2 * CHUNK)) % CHUNK
     same_head = (row_of((PAIR, 2 * PAIR)) // HEAD_DIM) == (
@@ -446,7 +447,7 @@
         part = slice(seq * CHUNK, (seq + 1) * CHUNK)
         before = carry[seq]
         before_ref[0, seq] = before
-        total = dot_nn(lower, a_all[part]) + before
+        total = dot_nn(lower, a_in[part, :]) + before
         carry[seq] = total[CHUNK - 1 :, :]
         inv = 1.0 / total
         for pair in range(PAIRS):
@@ -456,10 +457,10 @@
                     seq=seq,
                     pair=pair,
                     lanes=lanes,
-                    q=q_all[part, lanes] * low_type(HEAD_DIM**-0.5),
-                    k=k_all[part, lanes],
-                    v=v_all[part, lanes],
-                    a=a_all[part, lanes],
+                    q=q_in[part, lanes] * low_type(HEAD_DIM**-0.5),
+                    k=k_in[part, lanes],
+                    v=v_in[part, lanes],
+                    a=a_in[part, lanes],
                     inv=inv[:, lanes],
                 )
             )
@@ -486,24 +487,27 @@
         raw = dot_nt(t["share"], t["a_two"])
         t["mix"] = jnp.where(causal, raw, 0.0).astype(low_type)
 
-    def finish(t):
+    def finish_item(t):
         att = dot_nn(t["mix"], split_pair(t["v"], first_head))
         att = att + dot_nn(t["share"], t["now"][:, PAIR:])
         att_ref[t["seq"], :, t["lanes"]] = att.astype(low_type)
         state[t["seq"], t["pair"]] += dot_tn(t["a"], jnp.concatenate([t["k"], t["v"]], axis=1))
 
-    for stage in (score, gather, soften, blend, finish):
-        for item in items:
+    for stage, aside in zip((score, gather, soften, blend, finish_item), asides):
+        for place, item in enumerate(items):
             stage(item)
+            if place == len(items) // 2 - 1 and aside is not None:
+                aside()
 
 
 def forward_kernel(
     ids_ref,
     dw_ref,
+    x_first_ref,
     x_ref,
     ln_ref,
-    attn_ref,
-    ffn_ref,
+    attn_hbm,
+    ffn_w_hbm,
     q_ref,
     k_ref,
     v_ref,
@@ -519,25 +523,19 @@
     ffn_hbm,
     state,
     carry,
+    held,
     in_w,
+    piece_ref,
+    attn_ref,
+    ffn_ref,
     own,
     own_ffn,
     counts,
     counts_z,
-    counts_w,
-    in_sems,
-    in_far,
-    ffn_sems,
-    ffn_far,
-    out_sems,
-    out_far,
-    cz_send,
-    cz_recv,
-    cw_send,
-    cw_recv,
-    local_sems,
+    counts_chip,
+    counts_mate,
+    sems,
     *,
-    wide,
     narrow,
     total_seqs,
     groups,
@@ -545,198 +543,248 @@
     step = pl.program_id(0)
     steps = pl.num_programs(0)
     seqs = x_ref.shape[0]
-    w = lax.axis_index("wide")
-    z = lax.axis_index("narrow")
-    core = lax.rem(w, 2)
-    mate = (w + 1 - 2 * core, z)
-    other = 1 - core
+    here = Place(narrow)
+    copies = Copies(sems)
+    z, core, chip = here.z, here.core, here.chip
     rows = attn_ref.shape[1]
     ffn_rows = ffn_ref.shape[1]
     half = rows // 2
+    bit = half // 2
     quarter = ffn_rows // 4
-    chip = lax.rem(w // 2, 4)
-    hops = list(range(1, narrow))
-    column = [(w, lax.rem(z + hop, narrow)) for hop in hops]
-    plane = [(lax.rem(w + hop, wide), z) for hop in range(1, wide)]
-    chips = [(w - 2 * chip + 2 * lax.rem(chip + hop, 4), z) for hop in range(1, 4)]
-
-    def at(owner, size):
-        return pl.ds(pl.multiple_of(owner * size, size), size)
+    small = rows // 4
+    w = lax.axis_index("wide")
+    column = range(narrow - 1)
+    planes = range(3)
+    rounds = range(1, narrow)
+    cols = blocks_at(core, D // 2)
+
+    def inside(shard):
+        return jnp.clip(shard, 0, narrow - 1)
 
     def from_z(place):
-        return lax.rem(z + narrow - hops[place], narrow)
-
-    def in_part(owner, matrix):
-        return in_w.at[matrix, at(2 * owner + core, half)]
-
-    def in_z(place):
-        return remote(
-            own.at[chip, at(core, half)],
-            in_part(z, chip),
-            in_sems.at[0, place],
-            in_sems.at[1, place],
-            column[place],
+        return lax.rem(z + narrow - here.hops[place], narrow)
+
+    def in_rows(owner, part):
+        return blocks_at(4 * owner + 2 * core + part, bit)
+
+    in_z, in_chip, in_core = [], [], []
+    for part in range(2):
+        in_z.append(
+            [
+                copies.remote(
+                    own.at[chip, blocks_at(2 * core + part, bit)],
+                    in_w.at[chip, in_rows(z, part)],
+                    here.column[i],
+                )
+                for i in column
+            ]
         )
-
-    def in_chip(place, hop):
-        block = in_part(from_z(place), chip)
-        return remote(
-            block, block, in_far.at[0, place, hop], in_far.at[1, place, hop], chips[hop]
+        blocks = [in_w.at[chip, in_rows(from_z(i), part)] for i in column]
+        in_chip.append(
+            [[copies.remote(block, block, here.chips[p]) for p in planes] for block in blocks]
         )
-
-    def in_core(place):
-        block = in_w.at[:, at(2 * from_z(place) + core, half)]
-        return remote(block, block, in_sems.at[2, place], in_sems.at[3, place], mate)
-
-    def ffn_z(place):
-        return remote(
-            own_ffn.at[core, at(chip, quarter)],
-            ffn_hbm.at[core, at(4 * z + chip, quarter)],
-            ffn_sems.at[0, place],
-            ffn_sems.at[1, place],
-            column[place],
-        )
-
-    def ffn_chip(place, hop):
-        block = ffn_hbm.at[core, at(4 * from_z(place) + chip, quarter)]
-        return remote(
-            block, block, ffn_far.at[0, place, hop], ffn_far.at[1, place, hop], chips[hop]
-        )
-
-    def ffn_core(place):
-        block = ffn_hbm.at[core, at(from_z(place), ffn_rows)]
-        return remote(block, block, ffn_sems.at[2, place], ffn_sems.at[3, place], mate)
-
-    def out_block(owner, part):
-        return out_hbm.at[at(4 * owner + part, rows // 4), at(core, D // 2)]
-
-    def out_z(place):
-        return remote(
-            own.at[4, at(chip, rows // 4), at(core, D // 2)],
-            out_block(z, chip),
-            out_sems.at[0, place],
-            out_sems.at[1, place],
-            column[place],
-        )
-
-    def out_chip(place, hop):
-        block = out_block(from_z(place), chip)
-        return remote(
-            block, block, out_far.at[0, place, hop], out_far.at[1, place, hop], chips[hop]
-        )
-
-    def out_core(place):
-        block = out_hbm.at[at(from_z(place), rows), at(core, D // 2)]
-        return remote(block, block, out_sems.at[2, place], out_sems.at[3, place], mate)
-
-    def count_z(place):
-        return remote(
-            counts, counts_z.at[place], cz_send.at[place], cz_recv.at[place], column[place]
-        )
-
-    def count_w(place):
-        return remote(
-            counts, counts_w.at[place], cw_send.at[place], cw_recv.at[place], plane[place]
-        )
-
-    keep_ffn = pltpu.make_async_copy(own_ffn, ffn_hbm.at[:, at(z, ffn_rows)], local_sems.at[0])
-    keep_out = pltpu.make_async_copy(own.at[4], out_hbm.at[at(z, rows)], local_sems.at[1])
-    keep_in = pltpu.make_async_copy(in_w, in_hbm, local_sems.at[2])
+        blocks = [in_w.at[:, in_rows(from_z(i), part)] for i in column]
+        in_core.append([copies.remote(block, block, here.mate) for block in blocks])
+
+    def ffn_block(shard):
+        return ffn_hbm.at[core, blocks_at(4 * shard + chip, quarter)]
+
+    def out_block(shard):
+        return out_hbm.at[blocks_at(4 * shard + chip, small), cols]
+
+    def sends(way, turn):
+        if way == 0:
+            return jnp.logical_and(z < narrow - 1, z + 1 - turn >= 0)
+        return jnp.logical_and(z > 0, z - 1 + turn <= narrow - 1)
+
+    def gets(way, turn):
+        return z - turn >= 0 if way == 0 else z + turn <= narrow - 1
+
+    relay, spread, passed = {}, {}, {}
+    for turn in rounds:
+        for way in range(2):
+            sign = 1 if way == 0 else -1
+            there = (w, inside(z + sign))
+            shard = inside(z + sign * (1 - turn))
+            if turn == 1:
+                sources = [
+                    own_ffn.at[core, blocks_at(chip, quarter)],
+                    own.at[4, blocks_at(chip, small), cols],
+                ]
+            else:
+                sources = [ffn_block(shard), out_block(shard)]
+            targets = [ffn_block(shard), out_block(shard)]
+            relay[way, turn] = [
+                copies.remote(src, dst, there) for src, dst in zip(sources, targets)
+            ]
+            got = inside(z - sign * turn)
+            spread[way, turn] = [
+                copies.remote(block, block, here.chips[p])
+                for block in (ffn_block(got), out_block(got))
+                for p in planes
+            ]
+            passed[way, turn] = [
+                copies.remote(block, block, here.mate)
+                for block in (
+                    ffn_hbm.at[core, blocks_at(got, ffn_rows)],
+                    out_hbm.at[blocks_at(got, rows), cols],
+                )
+            ]
+
+    def relay_send(turn):
+        for way in range(2):
+
+            @pl.when(sends(way, turn))
+            def _():
+                for copy in relay[way, turn]:
+                    copy.start()
+
+    def relay_get(turn):
+        for way in range(2):
+
+            @pl.when(gets(way, turn))
+            def _():
+                for copy in relay[way, turn]:
+                    copy.wait_recv()
+                for copy in spread[way, turn]:
+                    copy.start()
+
+        if turn + 1 < narrow:
+            relay_send(turn + 1)
+
+    def pass_on(turn):
+        for way in range(2):
+
+            @pl.when(gets(way, turn))
+            def _():
+                for copy in spread[way, turn]:
+                    copy.wait_recv()
+                for copy in passed[way, turn]:
+                    copy.start()
+
+    count_z = [copies.remote(counts, counts_z.at[i], here.column[i]) for i in column]
+    count_chip = [copies.remote(counts, counts_chip.at[p], here.chips[p]) for p in planes]
+    count_mate = copies.remote(counts, counts_mate, here.mate)
+    load_piece = copies.local(attn_hbm.at[chip, blocks_at(core, half)], piece_ref)
+    load_attn = copies.local(attn_hbm, attn_ref)
+    load_ffn = copies.local(ffn_w_hbm, ffn_ref)
+    keep_ffn = copies.local(own_ffn, ffn_hbm.at[:, blocks_at(z, ffn_rows)])
+    keep_out = copies.local(own.at[4], out_hbm.at[blocks_at(z, rows)])
+    keep_in = copies.local(in_w, in_hbm)
+
+    def normal(ref):
+        normed, _ = normalize(ref[...].reshape(seqs * CHUNK, D).astype(wide_type))
+        return (normed * ln_ref[0:1, :] + ln_ref[1:2, :]).astype(low_type)
+
+    def product(first, place):
+        out = dot_nn(first, in_w[place])
+        held[place] = (jnp.exp(out) if place == 3 else out).astype(low_type)
 
     @pl.when(step == 0)
     def _():
+        for copy in (load_piece, load_attn, load_ffn):
+            copy.start()
         state[...] = jnp.zeros_like(state)
         carry[...] = jnp.zeros_like(carry)
-        own[chip, at(core, half), :] = attn_ref[chip, at(core, half), :].astype(low_type)
-        greet(column + plane)
-        for place in range(narrow - 1):
-            in_z(place).start()
+        greet(here.column + here.chips + [here.mate])
+        load_piece.wait()
+        own[chip, blocks_at(core, half), :] = piece_ref[...].astype(low_type)
+        for part in range(2):
+            for i in column:
+                in_z[part][i].start()
+        load_attn.wait()
+        load_ffn.wait()
+        for place in range(4):
+            in_w[place, blocks_at(z, rows), :] = attn_ref[place].astype(low_type)
         own[4] = attn_ref[4].astype(low_type)
-        for place in range(4):
-            in_w[place, at(z, rows), :] = attn_ref[place].astype(low_type)
         own_ffn[...] = ffn_ref[...].astype(low_type)
         lanes = lane_of((8, LANES))
         count = jnp.zeros((8, LANES), wide_type)
-        for seq in range(seqs):
+        for seq in range(ids_ref.shape[0]):
             count = count + (lanes == ids_ref[seq]).astype(wide_type)
         counts[...] = count
-        for place in range(narrow - 1):
-            in_z(place).wait_recv()
-            for hop in range(3):
-                in_chip(place, hop).start()
-        for place in range(narrow - 1):
-            ffn_z(place).start()
-            out_z(place).start()
-            count_z(place).start()
+        for part in range(2):
+            for i in column:
+                in_z[part][i].wait_recv()
+                for p in planes:
+                    in_chip[part][i][p].start()
+        relay_send(1)
+        for copy in count_z:
+            copy.start()
         keep_ffn.start()
         keep_out.start()
-        for place in range(narrow - 1):
-            for hop in range(3):
-                in_chip(place, hop).wait_recv()
-            in_core(place).start()
-        for place in range(narrow - 1):
-            in_core(place).wait_recv()
+        for part in range(2):
+            for i in column:
+                for p in planes:
+                    in_chip[part][i][p].wait_recv()
+                in_core[part][i].start()
+        relay_get(1)
+        for part in range(2):
+            for i in column:
+                in_core[part][i].wait_recv()
         keep_in.start()
+        first = normal(x_first_ref)
+        for place in range(4):
+            product(first, place)
+        if narrow > 2:
+            relay_get(2)
+
+    for turn in range(3, narrow):
+
+        @pl.when(step == turn - 1)
+        def _():
+            relay_get(turn)
 
     @pl.when(step == 1)
     def _():
-        for place in range(narrow - 1):
-            count_z(place).wait()
-        total = counts[...]
-        for place in range(narrow - 1):
-            total = total + counts_z[place]
-        counts[...] = total
-        for place in range(wide - 1):
-            count_w(place).start()
+        for copy in count_z:
+            copy.wait()
+        counts[...] = counts[...] + sum(counts_z[i] for i in column)
+        for copy in count_chip:
+            copy.start()
 
     @pl.when(step == 2)
     def _():
-        for place in range(wide - 1):
-            count_w(place).wait()
-        total = counts[...]
-        for place in range(wide - 1):
-            total = total + counts_w[place]
+        for copy in count_chip:
+            copy.wait()
+        counts[...] = counts[...] + sum(counts_chip[p] for p in planes)
+        count_mate.start()
+
+    @pl.when(step == 3)
+    def _():
+        count_mate.wait()
+        total = counts[...] + counts_mate[...]
         lanes = lane_of((8, LANES))
         values = jnp.zeros((8, LANES), wide_type)
         for group in range(groups):
             values = values + jnp.where(lanes == group, dw_ref[group], 0.0)
         weight_ref[...] = values * total_seqs / (groups * jnp.maximum(total, 1.0))
 
-    @pl.when(step == 1)
-    def _():
-        for place in range(narrow - 1):
-            ffn_z(place).wait_recv()
-            out_z(place).wait_recv()
-            for hop in range(3):
-                ffn_chip(place, hop).start()
-                out_chip(place, hop).start()
-
-    @pl.when(step == steps - 2)
-    def _():
-        for place in range(narrow - 1):
-            for hop in range(3):
-                ffn_chip(place, hop).wait_recv()
-                out_chip(place, hop).wait_recv()
-            ffn_core(place).start()
-            out_core(place).start()
-
-    normed, _ = normalize(x_ref[...].reshape(seqs * CHUNK, D).astype(wide_type))
-    first = (normed * ln_ref[0:1, :] + ln_ref[1:2, :]).astype(low_type)
-    q_all = dot_nn(first, in_w[0]).astype(low_type)
-    k_all = dot_nn(first, in_w[1]).astype(low_type)
-    v_all = dot_nn(first, in_w[2]).astype(low_type)
-    a_all = jnp.exp(dot_nn(first, in_w[3])).astype(low_type)
-    q_ref[...] = q_all.reshape(q_ref.shape)
-    k_ref[...] = k_all.reshape(q_ref.shape)
-    v_ref[...] = v_all.reshape(q_ref.shape)
-    a_ref[...] = a_all.reshape(q_ref.shape)
+    for turn in rounds:
+
+        @pl.when(step == jnp.minimum(steps - 1, turn + 4))
+        def _():
+            pass_on(turn)
+
+    source = [held[place] for place in range(4)]
+    for ref, item in zip((q_ref, k_ref, v_ref, a_ref), source):
+        ref[...] = item.reshape(ref.shape)
+    later = {}
+
+    def aside_norm():
+        later["first"] = normal(x_ref)
+
     attend_chunks(
-        q_all,
-        k_all,
-        v_all,
-        a_all,
+        source,
         (att_ref, share_ref, logit_ref, before_ref, state_ref, state, carry),
         seqs,
+        (
+            aside_norm,
+            lambda: product(later["first"], 0),
+            lambda: product(later["first"], 1),
+            lambda: product(later["first"], 2),
+            lambda: product(later["first"], 3),
+        ),
     )
 
     @pl.when(step == steps - 1)
@@ -744,17 +792,26 @@
         keep_ffn.wait()
         keep_out.wait()
         keep_in.wait()
-        for place in range(narrow - 1):
-            in_z(place).wait_send()
-            in_core(place).wait_send()
-            out_z(place).wait_send()
-            out_core(place).wait()
-            ffn_z(place).wait_send()
-            for hop in range(3):
-                in_chip(place, hop).wait_send()
-                ffn_chip(place, hop).wait_send()
-                out_chip(place, hop).wait_send()
-            ffn_core(place).wait()
+        for part in range(2):
+            for i in column:
+                in_z[part][i].wait_send()
+                for p in planes:
+                    in_chip[part][i][p].wait_send()
+                in_core[part][i].wait_send()
+        for turn in rounds:
+            for way in range(2):
+
+                @pl.when(sends(way, turn))
+                def _():
+                    for copy in relay[way, turn]:
+                        copy.wait_send()
+
+                @pl.when(gets(way, turn))
+                def _():
+                    for copy in spread[way, turn]:
+                        copy.wait_send()
+                    for copy in passed[way, turn]:
+                        copy.wait()
 
 
 def forward(tokens, ids, dw, ln_params, attn_w, ffn_w):
@@ -762,17 +819,22 @@
     chunks = length // CHUNK
     wide = lax.axis_size("wide")
     narrow = lax.axis_size("narrow")
+    if wide > 8:
+        sets = [[place + 8 * group for group in range(wide // 8)] for place in range(8)]
+        ids = lax.all_gather(ids, "wide", axis_index_groups=sets, tiled=True)
     block = pl.BlockSpec((seqs, CHUNK, D), lambda i: (0, i, 0))
+    ahead = pl.BlockSpec((seqs, CHUNK, D), lambda i: (0, jnp.minimum(i + 1, chunks - 1), 0))
     low_out = jax.ShapeDtypeStruct(tokens.shape, low_type)
     any_spec = pl.BlockSpec(memory_space=pl.ANY)
 
     def whole(*shape):
         return pl.BlockSpec(shape, lambda i: (0,) * len(shape))
 
+    column = narrow - 1
+    sems = 6 + 2 * (10 * column + 2 * column * 10 + column + 4)
     return pl.pallas_call(
         functools.partial(
             forward_kernel,
-            wide=wide,
             narrow=narrow,
             total_seqs=seqs * wide * narrow,
             groups=dw.shape[0],
@@ -781,10 +843,11 @@
         in_specs=[
             pl.BlockSpec(memory_space=pltpu.SMEM),
             pl.BlockSpec(memory_space=pltpu.SMEM),
-            block,
+            whole(seqs, CHUNK, D),
+            ahead,
             whole(4, D),
-            whole(*attn_w.shape),
-            whole(*ffn_w.shape),
+            any_spec,
+            any_spec,
         ],
         out_specs=[block] * 7
         + [
@@ -807,31 +870,24 @@
         scratch_shapes=[
             pltpu.VMEM((seqs, PAIRS, PAIR, 2 * PAIR), wide_type),
             pltpu.VMEM((seqs, 1, D), wide_type),
+            pltpu.VMEM((4, seqs * CHUNK, D), low_type),
             pltpu.VMEM((4, D, D), low_type),
+            pltpu.VMEM((attn_w.shape[1] // 2, D), wide_type),
+            pltpu.VMEM(attn_w.shape, wide_type),
+            pltpu.VMEM(ffn_w.shape, wide_type),
             pltpu.VMEM(attn_w.shape, low_type),
             pltpu.VMEM(ffn_w.shape, low_type),
             pltpu.VMEM((8, LANES), wide_type),
-            pltpu.VMEM((narrow - 1, 8, LANES), wide_type),
-            pltpu.VMEM((wide - 1, 8, LANES), wide_type),
-        ]
-        + [
-            pltpu.SemaphoreType.DMA((4, narrow - 1)),
-            pltpu.SemaphoreType.DMA((2, narrow - 1, 3)),
-            pltpu.SemaphoreType.DMA((4, narrow - 1)),
-            pltpu.SemaphoreType.DMA((2, narrow - 1, 3)),
-            pltpu.SemaphoreType.DMA((4, narrow - 1)),
-            pltpu.SemaphoreType.DMA((2, narrow - 1, 3)),
-            pltpu.SemaphoreType.DMA((narrow - 1,)),
-            pltpu.SemaphoreType.DMA((narrow - 1,)),
-            pltpu.SemaphoreType.DMA((wide - 1,)),
-            pltpu.SemaphoreType.DMA((wide - 1,)),
-        ]
-        + [pltpu.SemaphoreType.DMA((3,))],
+            pltpu.VMEM((column, 8, LANES), wide_type),
+            pltpu.VMEM((3, 8, LANES), wide_type),
+            pltpu.VMEM((8, LANES), wide_type),
+            pltpu.SemaphoreType.DMA((sems,)),
+        ],
         compiler_params=pltpu.CompilerParams(
             vmem_limit_bytes=VMEM_BYTES, collective_id=0, has_side_effects=True
         ),
         name="forward",
-    )(ids, dw, tokens, ln_params, attn_w, ffn_w)
+    )(ids, dw, tokens, tokens, ln_params, attn_w, ffn_w)
 
 
 class Place:
@@ -898,291 +954,9 @@
     return low_dot(poly_one, poly_two) * scale
 
 
-def back_kernel(*refs, narrow, chunks):
-    blocks = list(refs[:9])
-    xc_ref, x_ref, w_ref, ln_ref, gffn_hbm, go_hbm, mom_hbm = refs[9:16]
-    dz_ref, gln_ref, wsum_ref, fsum_ref, osum_ref, mom_ref = refs[16:22]
-    state, carry, dq_all, dk_all, dv_all, de_all, first_t = refs[22:29]
-    own_f, got_f, far_f, col_f, own_o, got_o, cut_o, far_o, col_o = refs[29:38]
-    low_f, low_o, mom_own, mom_low, mom_all = refs[38:43]
-    grad_w, got_w, half_w, far_w, staged, sems = refs[43:]
-    step = pl.program_id(0)
-    steps = pl.num_programs(0)
-    here = Place(narrow)
-    copies = Copies(sems)
-    half = D // 2
-    part = D // 4
-    rows = D // narrow
-    ffn_rows = FF // narrow
-    column = range(narrow - 1)
-    own_cols = blocks_at(here.core, half)
-    mate_cols = blocks_at(here.other, half)
-    grads = (dq_all, dk_all, dv_all, de_all)
-
-    keep_f = copies.local(gffn_hbm.at[here.core], own_f)
-    keep_o = copies.local(go_hbm.at[:, own_cols], own_o)
-    keep_mom = copies.local(mom_hbm.at[pl.ds(0, 4)], mom_own)
-    mate_sum = [
-        copies.remote(gffn_hbm.at[here.other], got_f, here.mate),
-        copies.remote(go_hbm.at[:, mate_cols], got_o, here.mate),
-    ]
-    plane_sum = []
-    for hop in range(3):
-        there = here.chip_at[hop]
-        plane_sum.append(
-            copies.remote(own_f.at[blocks_at(there, part)], far_f.at[hop], here.chips[hop])
-        )
-        plane_sum.append(copies.remote(cut_o.at[:, there], far_o.at[hop], here.chips[hop]))
-    z_sum = []
-    for i in column:
-        there = here.column_z[i]
-        z_sum.append(
-            copies.remote(low_f.at[:, blocks_at(there, ffn_rows)], col_f.at[i], here.column[i])
-        )
-        z_sum.append(copies.remote(low_o.at[there], col_o.at[i], here.column[i]))
-    z_mom = [
-        copies.remote(
-            mom_low.at[lax.rem(here.column_z[i], 4), :, own_cols],
-            mom_all.at[blocks_at(here.z, rows), own_cols],
-            here.column[i],
-        )
-        for i in column
-    ]
-    mate_mom = copies.remote(mom_all.at[:, own_cols], mom_all.at[:, own_cols], here.mate)
-    mate_w = [
-        copies.remote(grad_w.at[m, :, mate_cols], got_w.at[m], here.mate) for m in range(4)
-    ]
-    plane_w = [
-        [
-            copies.remote(
-                half_w.at[m, blocks_at(here.chip_at[hop], part)],
-                far_w.at[hop, m],
-                here.chips[hop],
-            )
-            for hop in range(3)
-        ]
-        for m in range(4)
-    ]
-
-    def gradient(m):
-        total = dot_nn(first_t[...], grads[m][...].reshape(-1, D))
-        grad_w[m] = total.astype(low_type)
-        mate_w[m].start()
-
-    def over_cores(m):
-        mate_w[m].wait()
-        half_w[m] = wide_sum([grad_w[m, :, own_cols], got_w[m]]).astype(low_type)
-        for copy in plane_w[m]:
-            copy.start()
-
-    def over_chips(m):
-        for copy in plane_w[m]:
-            copy.wait()
-        mine = half_w[m, blocks_at(here.chip, part), :]
-        wsum_ref[m] = wide_sum([mine] + [far_w[hop, m] for hop in range(3)]).astype(low_type)
-
-    @pl.when(step == 0)
-    def _():
-        state[...] = jnp.zeros_like(state)
-        carry[...] = jnp.zeros_like(carry)
-        gln_ref[...] = jnp.zeros_like(gln_ref)
-        greet(here.column + here.chips + [here.mate])
-        for copy in mate_sum + [keep_f, keep_o, keep_mom]:
-            copy.start()
-
-    @pl.when(step == 1)
-    def _():
-        keep_mom.wait()
-        mom_low[...] = mom_own[...].astype(low_type)
-        for copy in z_mom:
-            copy.start()
-        mom_all[blocks_at(here.z, rows), own_cols] = mom_low[lax.rem(here.z, 4), :, own_cols]
-
-    @pl.when(step == chunks // 4)
-    def _():
-        for copy in mate_sum + [keep_f, keep_o]:
-            copy.wait()
-        own_f[...] = wide_sum([own_f[...], got_f[...]]).astype(low_type)
-        cut_o[...] = wide_sum([own_o[...], got_o[...]]).astype(low_type).reshape(cut_o.shape)
-        for copy in plane_sum:
-            copy.start()
-
-    @pl.when(step < chunks)
-    def _():
-        chunk = chunks - 1 - step
-        seqs = xc_ref.shape[0]
-        for seq in range(seqs):
-            normed, _ = normalize(xc_ref[seq].astype(wide_type))
-            first = (normed * ln_ref[0:1, :] + ln_ref[1:2, :]).astype(low_type)
-            first_t[:, blocks_at(chunk * seqs + seq, CHUNK)] = first.T
-        attend_back_chunk(blocks + [staged.at[place] for place in range(4)], state, carry)
-        for place in range(4):
-            grads[place][chunk] = staged[place]
-
-    @pl.when(step == chunks)
-    def _():
-        gradient(0)
-        gradient(1)
-        for copy in z_mom:
-            copy.wait_recv()
-        mate_mom.start()
-
-    @pl.when(step == chunks + 1)
-    def _():
-        over_cores(0)
-        over_cores(1)
-        for copy in plane_sum:
-            copy.wait()
-        mine = own_f[blocks_at(here.chip, part), :]
-        low_f[...] = wide_sum([mine] + [far_f[hop] for hop in range(3)]).astype(low_type)
-        mine = cut_o[:, here.chip]
-        low_o[...] = wide_sum([mine] + [far_o[hop] for hop in range(3)]).astype(low_type)
-        for copy in z_sum:
-            copy.start()
-        gradient(2)
-        gradient(3)
-
-    @pl.when(step == chunks + 2)
-    def _():
-        over_cores(2)
-        over_cores(3)
-
-    @pl.when(step >= chunks)
-    def _():
-        per = chunks // 4
-        seqs = x_ref.shape[0]
-        parts = [item[pl.ds((step - chunks) * per, per)].reshape(-1, D) for item in grads]
-        dfirst = dot_nt(parts[0], w_ref[0])
-        for place in range(1, 4):
-            dfirst = dfirst + dot_nt(parts[place], w_ref[place])
-        spans = [slice(at * CHUNK, (at + 1) * CHUNK) for at in range(per)]
-        rows_in = [x_ref[:, span, :].reshape(-1, D) for span in spans]
-        normed, inverse = normalize(jnp.concatenate(rows_in, axis=0).astype(wide_type))
-        gln_ref[0:1, :] += jnp.sum(dfirst * normed, axis=0, keepdims=True)
-        gln_ref[1:2, :] += jnp.sum(dfirst, axis=0, keepdims=True)
-        dz = norm_back(dfirst, normed, inverse, ln_ref[0:1, :]).astype(low_type)
-        for at, span in enumerate(spans):
-            size = seqs * CHUNK
-            dz_ref[:, span, :] = dz[at * size : (at + 1) * size].reshape(seqs, CHUNK, D)
-
-    @pl.when(step == steps - 1)
-    def _():
-        mate_mom.wait()
-        mom_ref[...] = mom_all[...]
-        for m in range(4):
-            over_chips(m)
-        for copy in z_sum:
-            copy.wait()
-        mine = low_f[:, blocks_at(here.z, ffn_rows)]
-        fsum_ref[...] = wide_sum([mine] + [col_f[i] for i in column]).astype(low_type)
-        osum_ref[...] = wide_sum([low_o[here.z]] + [col_o[i] for i in column]).astype(low_type)
-        for copy in z_mom:
-            copy.wait_send()
-
-
-def back(q, k, v, a, share, logit, before, datt, states, tokens, in_w, ln_params, gffn, go, mom):
-    seqs, length, _ = q.shape
-    chunks = length // CHUNK
-    narrow = lax.axis_size("narrow")
-    small, half, part = D // narrow // 4, D // 2, D // 4
-    ffn_rows = FF // narrow
-
-    def chunk_at(i):
-        return jnp.maximum(chunks - 1 - i, 0)
-
-    def rows_at(i):
-        return (0, jnp.maximum(i - chunks, 0), 0)
-
-    def whole(*shape):
-        return pl.BlockSpec(shape, lambda i: (0,) * len(shape))
-
-    block = pl.BlockSpec((seqs, CHUNK, D), lambda i: (0, chunk_at(i), 0))
-    row_spec = pl.BlockSpec((seqs, length // 4, D), rows_at)
-    any_spec = pl.BlockSpec(memory_space=pl.ANY)
-    outs = [(4, part, half), (part, ffn_rows), (small, half), (D, D)]
-
-    def low(*shape):
-        return pltpu.VMEM(shape, low_type)
-
-    return pl.pallas_call(
-        functools.partial(back_kernel, narrow=narrow, chunks=chunks),
-        grid=(chunks + 4,),
-        in_specs=[block] * 6
-        + [
-            pl.BlockSpec((1, seqs, 1, D), lambda i: (chunk_at(i), 0, 0, 0)),
-            block,
-            pl.BlockSpec((1, seqs, PAIRS, PAIR, 2 * PAIR), lambda i: (chunk_at(i), 0, 0, 0, 0)),
-            block,
-            row_spec,
-            whole(4, D, D),
-            whole(4, D),
-            any_spec,
-            any_spec,
-            any_spec,
-        ],
-        out_specs=[row_spec, whole(2, D)] + [whole(*shape) for shape in outs],
-        out_shape=[
-            jax.ShapeDtypeStruct(q.shape, low_type),
-            jax.ShapeDtypeStruct((2, D), wide_type),
-        ]
-        + [jax.ShapeDtypeStruct(shape, low_type) for shape in outs],
-        scratch_shapes=[
-            pltpu.VMEM((seqs, PAIRS, PAIR, 2 * PAIR), wide_type),
-            pltpu.VMEM((seqs, 1, D), wide_type),
-            low(chunks, seqs, CHUNK, D),
-            low(chunks, seqs, CHUNK, D),
-            low(chunks, seqs, CHUNK, D),
-            low(chunks, seqs, CHUNK, D),
-            low(D, seqs * length),
-            low(D, FF),
-            low(D, FF),
-            low(3, part, FF),
-            low(narrow - 1, part, ffn_rows),
-            low(D, half),
-            low(D, half),
-            low(narrow, 4, small, half),
-            low(3, narrow, small, half),
-            low(narrow - 1, small, half),
-            low(part, FF),
-            low(narrow, small, half),
-            pltpu.VMEM((4, D // narrow, D), wide_type),
-            low(4, D // narrow, D),
-            low(D, D),
-            low(4, D, D),
-            low(4, D, half),
-            low(4, D, half),
-            low(3, 4, part, half),
-            low(4, seqs, CHUNK, D),
-            pltpu.SemaphoreType.DMA((3 + 2 * (2 + 6 + 3 * (narrow - 1) + 1 + 4 + 12),)),
-        ],
-        compiler_params=pltpu.CompilerParams(
-            vmem_limit_bytes=VMEM_BYTES, collective_id=1, has_side_effects=True
-        ),
-        name="back",
-    )(
-        q,
-        k,
-        v,
-        a,
-        share,
-        logit,
-        before,
-        datt,
-        states,
-        tokens,
-        tokens,
-        in_w,
-        ln_params,
-        gffn,
-        go,
-        mom,
-    )
-
-
-def update_kernel(
+def update_body(
     wsum_ref,
-    fsum_ref,
-    osum_ref,
+    take_f,
     mom_w_ref,
     mom_hbm,
     mom_f_hbm,
@@ -1219,12 +993,12 @@
     col_go,
     strips_go,
     gram_o,
-    sems,
     *,
     narrow,
+    here,
+    copies,
+    over_groups,
 ):
-    here = Place(narrow)
-    copies = Copies(sems)
     z, core, chip = here.z, here.core, here.chip
     half = D // 2
     quarter = D // 4
@@ -1323,16 +1097,17 @@
         for copy in group:
             copy.start()
 
-    greet(here.column + here.chips + [here.mate])
     start(z_sum)
-    all_f[own_quarter, :] = fsum_ref[...]
-    all_o[own_small, own_cols] = osum_ref[...]
-    start(plane_f)
     begin([keep_f, keep_o])
     ln_now[...] = jnp.zeros_like(ln_now)
     ln_now[0:2, :] = ln_one_ref[...]
     ln_now[2:4, :] = ln_two_ref[...]
+    over_groups(ln_now, 2)
     start(mate_ln)
+    grad_f, grad_o = take_f()
+    all_f[own_quarter, :] = grad_f
+    all_o[own_small, own_cols] = grad_o
+    start(plane_f)
 
     arrive(z_sum)
     total = wide_sum([wsum_ref[matrix]] + [col_w[i] for i in column])
@@ -1383,6 +1158,10 @@
     total = wide_sum([cut_gf[blocks_at(z, strip), :]] + [col_gf[i] for i in column])
     strips_gf[blocks_at(z, strip), :] = total.astype(low_type)
     start(z_back_f)
+    arrive(z_go)
+    total = wide_sum([cut_go[blocks_at(z, strip), :]] + [col_go[i] for i in column])
+    strips_go[blocks_at(z, strip), :] = total.astype(low_type)
+    start(z_back_o)
     poly_w[...] = newton_poly(gram).astype(low_type)
     picked = jnp.concatenate([moment_w[small_rows(there), :] for there in range(narrow)], axis=0)
     ortho = dot_nn(picked, poly_w[:, own_cols]).astype(low_type)
@@ -1391,30 +1170,26 @@
     start(spread_s)
     all_w[1, matrix, own_small, own_cols] = send_w[1, z]
 
-    arrive(z_go)
-    total = wide_sum([cut_go[blocks_at(z, strip), :]] + [col_go[i] for i in column])
-    strips_go[blocks_at(z, strip), :] = total.astype(low_type)
-    start(z_back_o)
     arrive(z_back_f)
     gram_f[own_quarter, :] = strips_gf[...]
     start(plane_gf)
     arrive(spread_g)
     start(plane_g)
+    arrive(spread_s)
+    start(plane_s)
     arrive(z_back_o)
     gram_o[own_quarter, own_cols] = strips_go[...]
     start(plane_go)
-    arrive(spread_s)
-    start(plane_s)
     arrive(plane_gf)
     poly = newton_poly(gram_f[...].astype(wide_type)).astype(low_type)
     out_f[1, core] = dot_nn(moment_f[...], poly).astype(low_type)
     start(mate_x)
     arrive(plane_g)
     start(mate_g)
+    arrive(plane_s)
+    start(mate_s)
     arrive(plane_go)
     start(mate_go)
-    arrive(plane_s)
-    start(mate_s)
     arrive(mate_go)
     poly = newton_poly(gram_o[...].astype(wide_type)).astype(low_type)
     step_o[...] = dot_nn(moment_o[...], poly).astype(low_type)
@@ -1439,75 +1214,385 @@
             copy.wait_send()
 
 
-def update(wsum, fsum, osum, mom_in, mom, mom_f, ln_one, ln_two):
+def back_kernel(*refs, narrow, chunks, sets):
+    blocks = list(refs[:9])
+    xc_ref, x_ref, w_ref, ln_ref, gffn_hbm, go_hbm, mom_hbm, mom_f_hbm, ln_two_ref = refs[9:18]
+    dz_ref, grad_attn, step_attn, grad_ffn, step_ffn, ln_sum_ref = refs[18:24]
+    state, carry, dq_all, dk_all, dv_all, de_all, first_t = refs[24:31]
+    own_f, got_f, far_f, col_f, own_o, got_o, cut_o, far_o, col_o = refs[31:40]
+    low_f, low_o, mom_own, mom_low, mom_all = refs[40:45]
+    grad_w, got_w, half_w, far_w, staged, gln_ref, wsum_ref = refs[45:52]
+    sums = refs[52:54]
+    group_w, group_f, group_o, group_ln = refs[54:58]
+    *update_refs, sems = refs[58:]
+    step = pl.program_id(0)
+    steps = pl.num_programs(0)
+    here = Place(narrow)
+    copies = Copies(sems)
+    half = D // 2
+    part = D // 4
+    rows = D // narrow
+    ffn_rows = FF // narrow
+    column = range(narrow - 1)
+    own_cols = blocks_at(here.core, half)
+    mate_cols = blocks_at(here.other, half)
+    grads = (dq_all, dk_all, dv_all, de_all)
+    w = lax.axis_index("wide")
+    peers = [(lax.rem(w + 8 * at, 8 * sets), here.z) for at in range(1, sets)]
+
+    keep_f = copies.local(gffn_hbm.at[here.core], own_f)
+    keep_o = copies.local(go_hbm.at[:, own_cols], own_o)
+    keep_mom = copies.local(mom_hbm.at[pl.ds(0, 4)], mom_own)
+    pieces = [blocks_at(there, part) for there in here.chip_at + [here.chip]]
+    mate_f = [
+        copies.remote(gffn_hbm.at[here.other, piece], got_f.at[piece], here.mate)
+        for piece in pieces
+    ]
+    mate_o = copies.remote(go_hbm.at[:, mate_cols], got_o, here.mate)
+    plane_f = [
+        copies.remote(own_f.at[pieces[hop]], far_f.at[hop], here.chips[hop]) for hop in range(3)
+    ]
+    plane_o = [
+        copies.remote(cut_o.at[:, here.chip_at[hop]], far_o.at[hop], here.chips[hop])
+        for hop in range(3)
+    ]
+    z_sum = []
+    for i in column:
+        there = here.column_z[i]
+        z_sum.append(
+            copies.remote(low_f.at[:, blocks_at(there, ffn_rows)], col_f.at[i], here.column[i])
+        )
+        z_sum.append(copies.remote(low_o.at[there], col_o.at[i], here.column[i]))
+    z_mom = [
+        copies.remote(
+            mom_low.at[lax.rem(here.column_z[i], 4), :, own_cols],
+            mom_all.at[blocks_at(here.z, rows), own_cols],
+            here.column[i],
+        )
+        for i in column
+    ]
+    mate_mom = copies.remote(mom_all.at[:, own_cols], mom_all.at[:, own_cols], here.mate)
+    mate_w = [
+        copies.remote(grad_w.at[m, :, mate_cols], got_w.at[m], here.mate) for m in range(4)
+    ]
+    plane_w = [
+        [
+            copies.remote(
+                half_w.at[m, blocks_at(here.chip_at[hop], part)],
+                far_w.at[hop, m],
+                here.chips[hop],
+            )
+            for hop in range(3)
+        ]
+        for m in range(4)
+    ]
+
+    def gradient(m):
+        total = dot_nn(first_t[...], grads[m][...].reshape(-1, D))
+        grad_w[m] = total.astype(low_type)
+        mate_w[m].start()
+
+    def over_cores(m):
+        mate_w[m].wait()
+        half_w[m] = wide_sum([grad_w[m, :, own_cols], got_w[m]]).astype(low_type)
+        for copy in plane_w[m]:
+            copy.start()
+
+    def over_chips(m):
+        for copy in plane_w[m]:
+            copy.wait()
+        mine = half_w[m, blocks_at(here.chip, part), :]
+        wsum_ref[m] = wide_sum([mine] + [far_w[hop, m] for hop in range(3)]).astype(low_type)
+
+    @pl.when(step == 0)
+    def _():
+        state[...] = jnp.zeros_like(state)
+        carry[...] = jnp.zeros_like(carry)
+        gln_ref[...] = jnp.zeros_like(gln_ref)
+        greet(here.column + here.chips + [here.mate] + peers)
+        for copy in [keep_f] + mate_f + [keep_o, mate_o, keep_mom]:
+            copy.start()
+
+    @pl.when(step == 1)
+    def _():
+        keep_mom.wait()
+        mom_low[...] = mom_own[...].astype(low_type)
+        for copy in z_mom:
+            copy.start()
+        mom_all[blocks_at(here.z, rows), own_cols] = mom_low[lax.rem(here.z, 4), :, own_cols]
+
+    def piece_sum(at):
+        mate_f[at].wait()
+        piece = pieces[at]
+        own_f[piece, :] = wide_sum([own_f[piece, :], got_f[piece, :]]).astype(low_type)
+        if at < 3:
+            plane_f[at].start()
+
+    @pl.when(step == 1)
+    def _():
+        keep_f.wait()
+        for at in range(2):
+            piece_sum(at)
+
+    @pl.when(step == 2)
+    def _():
+        for at in range(2, 4):
+            piece_sum(at)
+        keep_o.wait()
+        mate_o.wait()
+        cut_o[...] = wide_sum([own_o[...], got_o[...]]).astype(low_type).reshape(cut_o.shape)
+        for copy in plane_o:
+            copy.start()
+
+    @pl.when(step < chunks)
+    def _():
+        chunk = chunks - 1 - step
+        seqs = xc_ref.shape[0]
+
+        for seq in range(seqs):
+            normed, _ = normalize(xc_ref[seq].astype(wide_type))
+            first = (normed * ln_ref[0:1, :] + ln_ref[1:2, :]).astype(low_type)
+            first_t[:, blocks_at(chunk * seqs + seq, CHUNK)] = first.T
+        attend_back_chunk(blocks + [staged.at[place] for place in range(4)], state, carry)
+        for place in range(4):
+            grads[place][chunk] = staged[place]
+
+    @pl.when(step == chunks)
+    def _():
+        for copy in plane_f + plane_o:
+            copy.wait()
+        mine = own_f[blocks_at(here.chip, part), :]
+        low_f[...] = wide_sum([mine] + [far_f[hop] for hop in range(3)]).astype(low_type)
+        mine = cut_o[:, here.chip]
+        low_o[...] = wide_sum([mine] + [far_o[hop] for hop in range(3)]).astype(low_type)
+        for copy in z_sum:
+            copy.start()
+        gradient(0)
+        gradient(1)
+        over_cores(0)
+        gradient(2)
+        over_cores(1)
+        gradient(3)
+        for copy in z_mom:
+            copy.wait_recv()
+        mate_mom.start()
+
+    @pl.when(step == chunks + 1)
+    def _():
+        over_cores(2)
+        over_cores(3)
+
+    @pl.when(step >= chunks)
+    def _():
+        per = chunks // 4
+        seqs = x_ref.shape[0]
+        parts = [item[pl.ds((step - chunks) * per, per)].reshape(-1, D) for item in grads]
+        dfirst = dot_nt(parts[0], w_ref[0])
+        for place in range(1, 4):
+            dfirst = dfirst + dot_nt(parts[place], w_ref[place])
+        spans = [slice(at * CHUNK, (at + 1) * CHUNK) for at in range(per)]
+        rows_in = [x_ref[:, span, :].reshape(-1, D) for span in spans]
+        normed, inverse = normalize(jnp.concatenate(rows_in, axis=0).astype(wide_type))
+        gln_ref[0:1, :] += jnp.sum(dfirst * normed, axis=0, keepdims=True)
+        gln_ref[1:2, :] += jnp.sum(dfirst, axis=0, keepdims=True)
+        dz = norm_back(dfirst, normed, inverse, ln_ref[0:1, :]).astype(low_type)
+        for at, span in enumerate(spans):
+            size = seqs * CHUNK
+            dz_ref[:, span, :] = dz[at * size : (at + 1) * size].reshape(seqs, CHUNK, D)
+
+    def over_groups(ref, number):
+        if sets == 1:
+            return
+        slots = (group_w, group_f, group_ln, group_o)[number]
+        exchange = [
+            copies.remote(ref, slots.at[at], peer) for at, peer in enumerate(peers)
+        ]
+        for copy in exchange:
+            copy.start()
+        for copy in exchange:
+            copy.wait()
+        total = wide_sum([ref[...]] + [slots[at] for at in range(len(peers))])
+        ref[...] = total.astype(ref.dtype)
+
+    def take_f():
+        for copy in z_sum:
+            copy.wait()
+        sum_f, sum_o = sums
+        mine = low_f[:, blocks_at(here.z, ffn_rows)]
+        sum_f[...] = wide_sum([mine] + [col_f[i] for i in column]).astype(low_type)
+        sum_o[...] = wide_sum([low_o[here.z]] + [col_o[i] for i in column]).astype(low_type)
+        over_groups(sum_f, 1)
+        over_groups(sum_o, 3)
+        return sum_f[...], sum_o[...]
+
+    @pl.when(step == steps - 1)
+    def _():
+        for m in range(4):
+            over_chips(m)
+        over_groups(wsum_ref, 0)
+        mate_mom.wait()
+        for copy in z_mom:
+            copy.wait_send()
+        update_body(
+            wsum_ref,
+            take_f,
+            mom_all,
+            mom_hbm,
+            mom_f_hbm,
+            gln_ref,
+            ln_two_ref,
+            grad_attn,
+            step_attn,
+            grad_ffn,
+            step_ffn,
+            ln_sum_ref,
+            *update_refs,
+            narrow=narrow,
+            here=here,
+            copies=copies,
+            over_groups=over_groups,
+        )
+
+
+def back(q, k, v, a, share, logit, before, datt, states, tokens, in_w, ln_params, gffn, go, mom, mom_f, ln_two):
+    seqs, length, _ = q.shape
+    chunks = length // CHUNK
     narrow = lax.axis_size("narrow")
-    rows, ffn_rows = D // narrow, FF // narrow
-    small, half, quarter = rows // 4, D // 2, D // 4
-    strip = quarter // narrow
-    column = narrow - 1
+    small, half, part = D // narrow // 4, D // 2, D // 4
+    ffn_rows = FF // narrow
+
+    def chunk_at(i):
+        return jnp.maximum(chunks - 1 - i, 0)
+
+    def rows_at(i):
+        return (0, jnp.maximum(i - chunks, 0), 0)
+
+    def whole(*shape):
+        return pl.BlockSpec(shape, lambda i: (0,) * len(shape))
+
+    block = pl.BlockSpec((seqs, CHUNK, D), lambda i: (0, chunk_at(i), 0))
+    row_spec = pl.BlockSpec((seqs, length // 4, D), rows_at)
     any_spec = pl.BlockSpec(memory_space=pl.ANY)
-    vmem = pl.BlockSpec(memory_space=pltpu.VMEM)
+    rows, strip, column = D // narrow, part // narrow, narrow - 1
+    sets = lax.axis_size("wide") // 8
+    spare = max(sets - 1, 1)
+    outs = [(5, rows, D), (5, rows, D), (2, ffn_rows, D), (2, ffn_rows, D)]
+
+    def full(*shape):
+        return pltpu.VMEM(shape, wide_type)
 
     def low(*shape):
         return pltpu.VMEM(shape, low_type)
 
-    def full(*shape):
-        return pltpu.VMEM(shape, wide_type)
-
-    scratch = [
-        full(8, D),
-        full(8, D),
-        full(3, 8, D),
-        full(column, 8, D),
-        low(column, quarter, half),
-        low(D, D),
-        low(D, D),
-        low(D, D),
-        low(2, narrow, small, half),
-        low(2, 4, rows, D),
-        low(D, ffn_rows),
-        full(ffn_rows, D),
-        full(rows, D),
-        low(ffn_rows, D),
-        low(2, 2, ffn_rows, D),
-        low(rows, D),
-        low(rows, D),
-        low(rows, D),
-        low(quarter, D),
-        low(column, strip, D),
-        low(quarter, D),
-        low(D, D),
-        low(quarter, half),
-        low(column, strip, half),
-        low(quarter, half),
-        low(D, D),
-        pltpu.SemaphoreType.DMA((8 + 2 * (38 + 6 * column),)),
-    ]
     return pl.pallas_call(
-        functools.partial(update_kernel, narrow=narrow),
-        in_specs=[vmem, vmem, vmem, vmem, any_spec, any_spec, vmem, vmem],
-        out_specs=[any_spec, any_spec, any_spec, any_spec, vmem],
-        out_shape=[
-            jax.ShapeDtypeStruct((5, rows, D), low_type),
-            jax.ShapeDtypeStruct((5, rows, D), low_type),
-            jax.ShapeDtypeStruct((2, ffn_rows, D), low_type),
-            jax.ShapeDtypeStruct((2, ffn_rows, D), low_type),
-            jax.ShapeDtypeStruct((8, D), wide_type),
+        functools.partial(back_kernel, narrow=narrow, chunks=chunks, sets=sets),
+        grid=(chunks + 4,),
+        in_specs=[block] * 6
+        + [
+            pl.BlockSpec((1, seqs, 1, D), lambda i: (chunk_at(i), 0, 0, 0)),
+            block,
+            pl.BlockSpec((1, seqs, PAIRS, PAIR, 2 * PAIR), lambda i: (chunk_at(i), 0, 0, 0, 0)),
+            block,
+            row_spec,
+            whole(4, D, D),
+            whole(4, D),
+            any_spec,
+            any_spec,
+            any_spec,
+            any_spec,
+            whole(2, D),
         ],
-        scratch_shapes=scratch,
+        out_specs=[row_spec] + [any_spec] * 4 + [whole(8, D)],
+        out_shape=[jax.ShapeDtypeStruct(q.shape, low_type)]
+        + [jax.ShapeDtypeStruct(shape, low_type) for shape in outs]
+        + [jax.ShapeDtypeStruct((8, D), wide_type)],
+        scratch_shapes=[
+            pltpu.VMEM((seqs, PAIRS, PAIR, 2 * PAIR), wide_type),
+            pltpu.VMEM((seqs, 1, D), wide_type),
+            low(chunks, seqs, CHUNK, D),
+            low(chunks, seqs, CHUNK, D),
+            low(chunks, seqs, CHUNK, D),
+            low(chunks, seqs, CHUNK, D),
+            low(D, seqs * length),
+            low(D, FF),
+            low(D, FF),
+            low(3, part, FF),
+            low(narrow - 1, part, ffn_rows),
+            low(D, half),
+            low(D, half),
+            low(narrow, 4, small, half),
+            low(3, narrow, small, half),
+            low(narrow - 1, small, half),
+            low(part, FF),
+            low(narrow, small, half),
+            pltpu.VMEM((4, D // narrow, D), wide_type),
+            low(4, D // narrow, D),
+            low(D, D),
+            low(4, D, D),
+            low(4, D, half),
+            low(4, D, half),
+            low(3, 4, part, half),
+            low(4, seqs, CHUNK, D),
+            full(2, D),
+            low(4, part, half),
+            low(part, ffn_rows),
+            low(small, half),
+            low(spare, 4, part, half),
+            low(spare, part, ffn_rows),
+            low(spare, small, half),
+            full(spare, 8, D),
+            full(8, D),
+            full(8, D),
+            full(3, 8, D),
+            full(column, 8, D),
+            low(column, part, half),
+            low(D, D),
+            low(D, D),
+            low(D, D),
+            low(2, narrow, small, half),
+            low(2, 4, rows, D),
+            low(D, ffn_rows),
+            full(ffn_rows, D),
+            full(rows, D),
+            low(ffn_rows, D),
+            low(2, 2, ffn_rows, D),
+            low(rows, D),
+            low(rows, D),
+            low(rows, D),
+            low(part, D),
+            low(column, strip, D),
+            low(part, D),
+            low(D, D),
+            low(part, half),
+            low(column, strip, half),
+            low(part, half),
+            low(D, D),
+            pltpu.SemaphoreType.DMA((11 + 2 * (65 + 9 * column + 4 * spare),)),
+        ],
         compiler_params=pltpu.CompilerParams(
-            vmem_limit_bytes=VMEM_BYTES, collective_id=2, has_side_effects=True
+            vmem_limit_bytes=VMEM_BYTES, collective_id=1, has_side_effects=True
         ),
-        name="update",
-    )(wsum, fsum, osum, mom_in, mom, mom_f, ln_one, ln_two)
-
-
-def group_sum(values):
-    wide = lax.axis_size("wide")
-    if wide == 8:
-        return values
-    groups = [[place + 8 * group for group in range(wide // 8)] for place in range(8)]
-    return lax.psum(values, "wide", axis_index_groups=groups)
+        name="back",
+    )(
+        q,
+        k,
+        v,
+        a,
+        share,
+        logit,
+        before,
+        datt,
+        states,
+        tokens,
+        tokens,
+        in_w,
+        ln_params,
+        gffn,
+        go,
+        mom,
+        mom_f,
+        ln_two,
+    )
 
 
 def shards(
@@ -1541,7 +1626,7 @@
         ln_params,
         length,
     )
-    dz, ln_one, wsum, fsum, osum, mom_in = back(
+    dz, attn_grad, attn_step, ffn_grad, ffn_step, ln_sum = back(
         q,
         k,
         v,
@@ -1557,11 +1642,10 @@
         gffn,
         go,
         attn_mom,
+        ffn_mom,
+        ln_two,
     )
-    wsum, fsum, osum, ln_one, ln_two = group_sum((wsum, fsum, osum, ln_one, ln_two))
-    attn_grad, attn_step, ffn_grad, ffn_step, ln_sum = update(
-        wsum, fsum, osum, mom_in, attn_mom, ffn_mom, ln_one, ln_two
-    )
+
     def flat(*items):
         return [item.reshape(-1, D) for item in items]
 

time: 211 us -> 202 us (0.957)
  Pallas kernels: 210 us -> 200 us
    pallas_call x2 -> x1, Pallas kernels: 99.2 us -> 50.3 us  [forward(): pl.pallas_call(functools.partial(forward_kernel, narrow=narrow, total_seq...]
    pallas_call x1, Pallas kernels: 56.1 us -> 97.8 us  [back(): pl.pallas_call(functools.partial(back_kernel, narrow=narrow, chunks=chunk...]
where the time goes in v6:
time: 202 us; the launch traced here: 201 us
  Pallas kernels  200 us (99%)
    pallas_call x1, Pallas kernels, back(): pl.pallas_call(functools.partial(back_kernel, narrow=narrow, chunks=chunk...  97.8 us
    pallas_call x1, Pallas kernels, forward(): pl.pallas_call(functools.partial(forward_kernel, narrow=narrow, total_seq...  50.3 us
    pallas_call x1, Pallas kernels, feed(): pl.pallas_call(functools.partial(feed_kernel, per_seq=length // block), g...  41.3 us
    pallas_call x1, Pallas kernels, finish(): pl.pallas_call(finish_kernel, grid=(steps,), in_specs=[rows(item) for ite...  10.9 us

profile of v6, /device:TPU:0, one launch (start us, length us, event | category | flops | bytes accessed | tf_op | source)
XLA Modules:
  0.0 201.2 jit_solution(2163116907797691711)
XLA Ops:
  0.6 50.3 %forward.1 = (bf16[2,1024,512]{2,1,0:T(8,128)(2,1)}, bf16[2,1024,512]{2,1,0:T(8,128)(2,1)}, bf16[2,1024,512]{2,1,0:T(8,128)(2,1)}, bf16[2,1024,512]{2,1,0:T(8,12...) custom-call(s32[2]{0:T(128)} %ids_ref.3, ...), custom_call_target="tpu_custom_call" | custom-call | tf_op jit(solution)/shard_map/forward/pallas_call | solution.py:835
  50.9 41.3 %feed.1 = (bf16[2048,512]{1,0:T(8,128)(2,1)}, bf16[2048,512]{1,0:T(8,128)(2,1)}, bf16[2048,512]{1,0:T(8,128)(2,1)}, bf16[2,512,2048]{2,1,0:T(8,128)(2,1)}, bf16[512,512]{1,0:T(8,128)(2,1)}, /*index=5*/f32[2,512]{1,0:T(2,128)}) custom-call(s32[2]{0:T(128)} %ids_ref.3, f32[8,128]{1,0:T(8,128)} %get-tuple-element.52.weight_ref, bf16[2048,512]{1,0:T(8,128)(2,1)} %bitcast.23, ...), custom_call_target="tpu_custom_call" | custom-call | tf_op jit(solution)/shard_map/feed/pallas_call | solution.py:280
  92.3 97.8 %back.1 = (bf16[2,1024,512]{2,1,0:T(8,128)(2,1)}, bf16[5,128,512]{2,1,0:T(8,128)(2,1)}, bf16[5,128,512]{2,1,0:T(8,128)(2,1)}, bf16[2,512,512]{2,1,0:T(8,128)(2,1...) custom-call(bf16[2,1024,512]{2,1,0:T(8,128)(2,1)} %get-tuple-element.58.refs_0_, ...), custom_call_target="tpu_custom_call" | custom-call | tf_op jit(solution)/shard_map/back/pallas_call | solution.py:1487
  190.1 10.9 %finish.1 = (f32[2048,512]{1,0:T(8,128)}, f32[640,512]{1,0:T(8,128)}, f32[640,512]{1,0:T(8,128)}, f32[640,512]{1,0:T(8,128)}, bf16[640,512]{1,0:T(8,128)(2,1)}, ...) custom-call(bf16[2048,512]{1,0:T(8,128)(2,1)} %get-tuple-element.57., ...), custom_call_target="tpu_custom_call" | custom-call | tf_op jit(solution)/shard_map/finish/pallas_call | solution.py:403

commit v7 on v6

--- a/solution.py
+++ b/solution.py
@@ -182,7 +182,7 @@
             stage(item)
 
 
-FF_BLOCK = 512
+FF_BLOCK = 256
 gelu_root = math.sqrt(2.0 / math.pi)
 gelu_cube = 0.044715
 
@@ -205,6 +205,8 @@
     up_sum,
     down_sum,
     o_sum,
+    hidden,
+    dinner,
     *,
     per_seq,
 ):
@@ -227,32 +229,29 @@
     dy = dout.astype(low_type)
     second_t = second.T
     dy_t = dy.T
-    parts = [dict(rows=slice(part * FF_BLOCK, (part + 1) * FF_BLOCK)) for part in range(FF // FF_BLOCK)]
-
-    def open_part(t):
-        t["up"] = ffn_ref[0, t["rows"], :]
-        t["down"] = ffn_ref[1, t["rows"], :]
-        t["inner"] = dot_nt(second, t["up"])
-        t["dhidden"] = dot_nt(dy, t["down"])
-
-    result, dsecond = mixed, 0.0
-    open_part(parts[0])
-    for place, t in enumerate(parts):
+    parts = [slice(part * FF_BLOCK, (part + 1) * FF_BLOCK) for part in range(FF // FF_BLOCK)]
+
+    def open_part(part):
+        return dot_nt(second, ffn_ref[0, part, :]), dot_nt(dy, ffn_ref[1, part, :])
+
+    ahead = open_part(parts[0])
+    for place, part in enumerate(parts):
+        inner, dhidden = ahead
         if place + 1 < len(parts):
-            open_part(parts[place + 1])
-        inner = t["inner"]
+            ahead = open_part(parts[place + 1])
         square = inner * inner
         bend = jnp.tanh(inner * (gelu_root + (gelu_root * gelu_cube) * square))
         half = 0.5 + 0.5 * bend
-        hidden = (inner * half).astype(low_type)
+        hidden[:, part] = (inner * half).astype(low_type)
         slope = half + (0.5 * inner) * (1.0 - bend * bend) * (
             gelu_root + (3.0 * gelu_root * gelu_cube) * square
         )
-        dinner = (t["dhidden"] * slope).astype(low_type)
-        result = result + dot_nn(hidden, t["down"])
-        down_sum[:, t["rows"]] += dot_nn(dy_t, hidden)
-        up_sum[:, t["rows"]] += dot_nn(second_t, dinner)
-        dsecond = dsecond + dot_nn(dinner, t["up"])
+        dinner[:, part] = (dhidden * slope).astype(low_type)
+    result = mixed + dot_nn(hidden[...], ffn_ref[1])
+    dsecond = dot_nn(dinner[...], ffn_ref[0])
+    for part in parts:
+        down_sum[:, part] += dot_nn(dy_t, hidden[:, part])
+        up_sum[:, part] += dot_nn(second_t, dinner[:, part])
     out_ref[...] = result.astype(low_type)
     gln_ref[0:1, :] += jnp.sum(dsecond * normed, axis=0, keepdims=True)
     gln_ref[1:2, :] += jnp.sum(dsecond, axis=0, keepdims=True)
@@ -310,6 +309,8 @@
             pltpu.VMEM((D, FF), wide_type),
             pltpu.VMEM((D, FF), wide_type),
             pltpu.VMEM((D, D), wide_type),
+            pltpu.VMEM((block, FF), low_type),
+            pltpu.VMEM((block, FF), low_type),
         ],
         compiler_params=pltpu.CompilerParams(vmem_limit_bytes=VMEM_BYTES),
         name="feed",
@@ -1109,15 +1110,6 @@
     all_o[own_small, own_cols] = grad_o
     start(plane_f)
 
-    arrive(z_sum)
-    total = wide_sum([wsum_ref[matrix]] + [col_w[i] for i in column])
-    grad_w[own_quarter, own_cols] = total.astype(low_type)
-    start(plane_w)
-    arrive(mate_ln)
-    mate_ln[0].wait_send()
-    ln_now[...] = ln_now[...] + ln_mate[...]
-    start(plane_ln)
-
     keep_f.wait()
     arrive(plane_f)
     start(mate_o)
@@ -1128,6 +1120,31 @@
     cut_gf[...] = dot_tn(moment_f[:, own_quarter], moment_f[...]).astype(low_type)
     start(z_gf)
 
+    keep_o.wait()
+    arrive(mate_o)
+    moment = momentum_keep * mom_o[...] + all_o[...].astype(wide_type)
+    moment_o[...] = moment.astype(low_type)
+    cut_go[...] = dot_tn(moment_o[:, own_quarter], moment_o[:, own_cols]).astype(low_type)
+    start(z_go)
+
+    arrive(z_sum)
+    total = wide_sum([wsum_ref[matrix]] + [col_w[i] for i in column])
+    grad_w[own_quarter, own_cols] = total.astype(low_type)
+    start(plane_w)
+    arrive(mate_ln)
+    mate_ln[0].wait_send()
+    ln_now[...] = ln_now[...] + ln_mate[...]
+    start(plane_ln)
+
+    arrive(z_gf)
+    total = wide_sum([cut_gf[blocks_at(z, strip), :]] + [col_gf[i] for i in column])
+    strips_gf[blocks_at(z, strip), :] = total.astype(low_type)
+    start(z_back_f)
+    arrive(z_go)
+    total = wide_sum([cut_go[blocks_at(z, strip), :]] + [col_go[i] for i in column])
+    strips_go[blocks_at(z, strip), :] = total.astype(low_type)
+    start(z_back_o)
+
     arrive(plane_w)
     start(mate_w)
     arrive(plane_ln)
@@ -1135,13 +1152,6 @@
         copy.wait_send()
     ln_now[...] = ln_now[...] + ln_chips[0] + ln_chips[1] + ln_chips[2]
     start(z_ln)
-
-    arrive(mate_o)
-    keep_o.wait()
-    moment = momentum_keep * mom_o[...] + all_o[...].astype(wide_type)
-    moment_o[...] = moment.astype(low_type)
-    cut_go[...] = dot_tn(moment_o[:, own_quarter], moment_o[:, own_cols]).astype(low_type)
-    start(z_go)
 
     def small_rows(there):
         return pl.ds(pl.multiple_of(there * rows + chip * small, small), small)
@@ -1154,14 +1164,13 @@
     moment = momentum_keep * mom_w_ref[...].astype(wide_type) + grad_w[...].astype(wide_type)
     moment_w[...] = moment.astype(low_type)
     gram = dot_tn(moment_w[...], moment_w[...])
-    arrive(z_gf)
-    total = wide_sum([cut_gf[blocks_at(z, strip), :]] + [col_gf[i] for i in column])
-    strips_gf[blocks_at(z, strip), :] = total.astype(low_type)
-    start(z_back_f)
-    arrive(z_go)
-    total = wide_sum([cut_go[blocks_at(z, strip), :]] + [col_go[i] for i in column])
-    strips_go[blocks_at(z, strip), :] = total.astype(low_type)
-    start(z_back_o)
+    arrive(z_back_f)
+    gram_f[own_quarter, :] = strips_gf[...]
+    start(plane_gf)
+    arrive(z_back_o)
+    gram_o[own_quarter, own_cols] = strips_go[...]
+    start(plane_go)
+
     poly_w[...] = newton_poly(gram).astype(low_type)
     picked = jnp.concatenate([moment_w[small_rows(there), :] for there in range(narrow)], axis=0)
     ortho = dot_nn(picked, poly_w[:, own_cols]).astype(low_type)
@@ -1169,30 +1178,24 @@
         send_w[1, there] = ortho[there * small : (there + 1) * small, :]
     start(spread_s)
     all_w[1, matrix, own_small, own_cols] = send_w[1, z]
-
-    arrive(z_back_f)
-    gram_f[own_quarter, :] = strips_gf[...]
-    start(plane_gf)
     arrive(spread_g)
     start(plane_g)
-    arrive(spread_s)
-    start(plane_s)
-    arrive(z_back_o)
-    gram_o[own_quarter, own_cols] = strips_go[...]
-    start(plane_go)
+
     arrive(plane_gf)
     poly = newton_poly(gram_f[...].astype(wide_type)).astype(low_type)
     out_f[1, core] = dot_nn(moment_f[...], poly).astype(low_type)
     start(mate_x)
+    arrive(spread_s)
+    start(plane_s)
+    arrive(plane_go)
+    start(mate_go)
     arrive(plane_g)
     start(mate_g)
-    arrive(plane_s)
-    start(mate_s)
-    arrive(plane_go)
-    start(mate_go)
     arrive(mate_go)
     poly = newton_poly(gram_o[...].astype(wide_type)).astype(low_type)
     step_o[...] = dot_nn(moment_o[...], poly).astype(low_type)
+    arrive(plane_s)
+    start(mate_s)
     begin(write_o)
     arrive(mate_f)
     arrive(mate_x)
@@ -1359,6 +1362,11 @@
 
     @pl.when(step == chunks)
     def _():
+        gradient(0)
+        gradient(1)
+        gradient(2)
+        over_cores(0)
+        over_cores(1)
         for copy in plane_f + plane_o:
             copy.wait()
         mine = own_f[blocks_at(here.chip, part), :]
@@ -1367,20 +1375,12 @@
         low_o[...] = wide_sum([mine] + [far_o[hop] for hop in range(3)]).astype(low_type)
         for copy in z_sum:
             copy.start()
-        gradient(0)
-        gradient(1)
-        over_cores(0)
-        gradient(2)
-        over_cores(1)
         gradient(3)
+        over_cores(2)
+        over_cores(3)
         for copy in z_mom:
             copy.wait_recv()
         mate_mom.start()
-
-    @pl.when(step == chunks + 1)
-    def _():
-        over_cores(2)
-        over_cores(3)
 
     @pl.when(step >= chunks)
     def _():

time: 202 us -> 198 us (0.980)
  Pallas kernels: 200 us -> 197 us
where the time goes in v7:
time: 198 us
  Pallas kernels  197 us (99%)
    pallas_call x1, Pallas kernels, back(): pl.pallas_call(functools.partial(back_kernel, narrow=narrow, chunks=chunk...  95.9 us
    pallas_call x1, Pallas kernels, forward(): pl.pallas_call(functools.partial(forward_kernel, narrow=narrow, total_seq...  50.3 us
    pallas_call x1, Pallas kernels, feed(): pl.pallas_call(functools.partial(feed_kernel, per_seq=length // block), g...  40 us
    pallas_call x1, Pallas kernels, finish(): pl.pallas_call(finish_kernel, grid=(steps,), in_specs=[rows(item) for ite...  10.9 us

profile of v7, /device:TPU:0, one launch (start us, length us, event | category | flops | bytes accessed | tf_op | source)
XLA Modules:
  0.0 198.0 jit_solution(14548977954097670134)
XLA Ops:
  0.6 50.3 %forward.1 = (bf16[2,1024,512]{2,1,0:T(8,128)(2,1)}, bf16[2,1024,512]{2,1,0:T(8,128)(2,1)}, bf16[2,1024,512]{2,1,0:T(8,128)(2,1)}, bf16[2,1024,512]{2,1,0:T(8,12...) custom-call(s32[2]{0:T(128)} %ids_ref.3, ...), custom_call_target="tpu_custom_call" | custom-call | tf_op jit(solution)/shard_map/forward/pallas_call | solution.py:836
  50.9 40.0 %feed.1 = (bf16[2048,512]{1,0:T(8,128)(2,1)}, bf16[2048,512]{1,0:T(8,128)(2,1)}, bf16[2048,512]{1,0:T(8,128)(2,1)}, bf16[2,512,2048]{2,1,0:T(8,128)(2,1)}, bf16[512,512]{1,0:T(8,128)(2,1)}, /*index=5*/f32[2,512]{1,0:T(2,128)}) custom-call(s32[2]{0:T(128)} %ids_ref.3, f32[8,128]{1,0:T(8,128)} %get-tuple-element.52.weight_ref, bf16[2048,512]{1,0:T(8,128)(2,1)} %bitcast.23, ...), custom_call_target="tpu_custom_call" | custom-call | tf_op jit(solution)/shard_map/feed/pallas_call | solution.py:279
  91.0 95.9 %back.1 = (bf16[2,1024,512]{2,1,0:T(8,128)(2,1)}, bf16[5,128,512]{2,1,0:T(8,128)(2,1)}, bf16[5,128,512]{2,1,0:T(8,128)(2,1)}, bf16[2,512,512]{2,1,0:T(8,128)(2,1...) custom-call(bf16[2,1024,512]{2,1,0:T(8,128)(2,1)} %get-tuple-element.58.refs_0_, ...), custom_call_target="tpu_custom_call" | custom-call | tf_op jit(solution)/shard_map/back/pallas_call | solution.py:1487
  186.9 10.9 %finish.1 = (f32[2048,512]{1,0:T(8,128)}, f32[640,512]{1,0:T(8,128)}, f32[640,512]{1,0:T(8,128)}, f32[640,512]{1,0:T(8,128)}, bf16[640,512]{1,0:T(8,128)(2,1)}, ...) custom-call(bf16[2048,512]{1,0:T(8,128)(2,1)} %get-tuple-element.57., ...), custom_call_target="tpu_custom_call" | custom-call | tf_op jit(solution)/shard_map/finish/pallas_call | solution.py:404

commit v8 on v7

--- a/solution.py
+++ b/solution.py
@@ -587,8 +587,13 @@
         blocks = [in_w.at[:, in_rows(from_z(i), part)] for i in column]
         in_core.append([copies.remote(block, block, here.mate) for block in blocks])
 
-    def ffn_block(shard):
-        return ffn_hbm.at[core, blocks_at(4 * shard + chip, quarter)]
+    side = lax.rem(chip, 2)
+    pieces = (side, 2 + chip // 2)
+    beside = (w - 2 * chip + 2 * (chip + 1 - 2 * side), z)
+    neighbours = (beside, here.chips[1])
+
+    def ffn_block(shard, piece):
+        return ffn_hbm.at[core, blocks_at(4 * shard + piece, quarter)]
 
     def out_block(shard):
         return out_hbm.at[blocks_at(4 * shard + chip, small), cols]
@@ -608,22 +613,21 @@
             there = (w, inside(z + sign))
             shard = inside(z + sign * (1 - turn))
             if turn == 1:
-                sources = [
-                    own_ffn.at[core, blocks_at(chip, quarter)],
-                    own.at[4, blocks_at(chip, small), cols],
-                ]
+                sources = [own_ffn.at[core, blocks_at(piece, quarter)] for piece in pieces]
+                sources.append(own.at[4, blocks_at(chip, small), cols])
             else:
-                sources = [ffn_block(shard), out_block(shard)]
-            targets = [ffn_block(shard), out_block(shard)]
+                sources = [ffn_block(shard, piece) for piece in pieces] + [out_block(shard)]
+            targets = [ffn_block(shard, piece) for piece in pieces] + [out_block(shard)]
             relay[way, turn] = [
                 copies.remote(src, dst, there) for src, dst in zip(sources, targets)
             ]
             got = inside(z - sign * turn)
-            spread[way, turn] = [
-                copies.remote(block, block, here.chips[p])
-                for block in (ffn_block(got), out_block(got))
-                for p in planes
-            ]
+            spread[way, turn] = []
+            for piece, device in zip(pieces, neighbours):
+                block = ffn_block(got, piece)
+                spread[way, turn].append(copies.remote(block, block, device))
+            block = out_block(got)
+            spread[way, turn] += [copies.remote(block, block, here.chips[p]) for p in planes]
             passed[way, turn] = [
                 copies.remote(block, block, here.mate)
                 for block in (

time: 198 us -> 190 us (0.960)
  Pallas kernels: 197 us -> 189 us
    pallas_call x1, Pallas kernels: 95.9 us -> 90.6 us  [back(): pl.pallas_call(functools.partial(back_kernel, narrow=narrow, chunks=chunk...]
    pallas_call x1, Pallas kernels: 50.3 us -> 47.7 us  [forward(): pl.pallas_call(functools.partial(forward_kernel, narrow=narrow, total_seq...]
where the time goes in v8:
time: 190 us
  Pallas kernels  189 us (99%)
    pallas_call x1, Pallas kernels, back(): pl.pallas_call(functools.partial(back_kernel, narrow=narrow, chunks=chunk...  90.6 us
    pallas_call x1, Pallas kernels, forward(): pl.pallas_call(functools.partial(forward_kernel, narrow=narrow, total_seq...  47.7 us
    pallas_call x1, Pallas kernels, feed(): pl.pallas_call(functools.partial(feed_kernel, per_seq=length // block), g...  40 us
    pallas_call x1, Pallas kernels, finish(): pl.pallas_call(finish_kernel, grid=(steps,), in_specs=[rows(item) for ite...  10.9 us

profile of v8, /device:TPU:0, one launch (start us, length us, event | category | flops | bytes accessed | tf_op | source)
XLA Modules:
  0.0 190.1 jit_solution(6762772057261086711)
XLA Ops:
  0.6 47.7 %forward.1 = (bf16[2,1024,512]{2,1,0:T(8,128)(2,1)}, bf16[2,1024,512]{2,1,0:T(8,128)(2,1)}, bf16[2,1024,512]{2,1,0:T(8,128)(2,1)}, bf16[2,1024,512]{2,1,0:T(8,12...) custom-call(s32[2]{0:T(128)} %ids_ref.3, ...), custom_call_target="tpu_custom_call" | custom-call | tf_op jit(solution)/shard_map/forward/pallas_call | solution.py:840
  48.3 40.0 %feed.1 = (bf16[2048,512]{1,0:T(8,128)(2,1)}, bf16[2048,512]{1,0:T(8,128)(2,1)}, bf16[2048,512]{1,0:T(8,128)(2,1)}, bf16[2,512,2048]{2,1,0:T(8,128)(2,1)}, bf16[512,512]{1,0:T(8,128)(2,1)}, /*index=5*/f32[2,512]{1,0:T(2,128)}) custom-call(s32[2]{0:T(128)} %ids_ref.3, f32[8,128]{1,0:T(8,128)} %get-tuple-element.52.weight_ref, bf16[2048,512]{1,0:T(8,128)(2,1)} %bitcast.23, ...), custom_call_target="tpu_custom_call" | custom-call | tf_op jit(solution)/shard_map/feed/pallas_call | solution.py:279
  88.4 90.6 %back.1 = (bf16[2,1024,512]{2,1,0:T(8,128)(2,1)}, bf16[5,128,512]{2,1,0:T(8,128)(2,1)}, bf16[5,128,512]{2,1,0:T(8,128)(2,1)}, bf16[2,512,512]{2,1,0:T(8,128)(2,1...) custom-call(bf16[2,1024,512]{2,1,0:T(8,128)(2,1)} %get-tuple-element.58.refs_0_, ...), custom_call_target="tpu_custom_call" | custom-call | tf_op jit(solution)/shard_map/back/pallas_call | solution.py:1491
  179.0 10.9 %finish.1 = (f32[2048,512]{1,0:T(8,128)}, f32[640,512]{1,0:T(8,128)}, f32[640,512]{1,0:T(8,128)}, f32[640,512]{1,0:T(8,128)}, bf16[640,512]{1,0:T(8,128)(2,1)}, ...) custom-call(bf16[2048,512]{1,0:T(8,128)(2,1)} %get-tuple-element.57., ...), custom_call_target="tpu_custom_call" | custom-call | tf_op jit(solution)/shard_map/finish/pallas_call | solution.py:404

commit v9 on v8

--- a/solution.py
+++ b/solution.py
@@ -383,7 +383,7 @@
 
 
 def finish(dx, dz, attn, ffn, ln):
-    steps = 4
+    steps = 2
 
     def rows(item):
         block = item.shape[0] // steps
@@ -731,10 +731,8 @@
         first = normal(x_first_ref)
         for place in range(4):
             product(first, place)
-        if narrow > 2:
-            relay_get(2)
-
-    for turn in range(3, narrow):
+
+    for turn in range(2, narrow):
 
         @pl.when(step == turn - 1)
         def _():
@@ -956,7 +954,11 @@
     poly_one = polynomial(gram_one)
     gram_two = low_dot(low_dot(gram_one, poly_one), poly_one)
     poly_two = polynomial(gram_two)
-    return low_dot(poly_one, poly_two) * scale
+    return poly_one.astype(low_type), (poly_two * scale).astype(low_type)
+
+
+def newton_step(rows, polys):
+    return dot_nn(dot_nn(rows, polys[0]).astype(low_type), polys[1]).astype(low_type)
 
 
 def update_body(
@@ -1175,9 +1177,9 @@
     gram_o[own_quarter, own_cols] = strips_go[...]
     start(plane_go)
 
-    poly_w[...] = newton_poly(gram).astype(low_type)
+    poly_one, poly_w[...] = newton_poly(gram)
     picked = jnp.concatenate([moment_w[small_rows(there), :] for there in range(narrow)], axis=0)
-    ortho = dot_nn(picked, poly_w[:, own_cols]).astype(low_type)
+    ortho = newton_step(picked, (poly_one, poly_w[:, own_cols]))
     for there in range(narrow):
         send_w[1, there] = ortho[there * small : (there + 1) * small, :]
     start(spread_s)
@@ -1186,8 +1188,7 @@
     start(plane_g)
 
     arrive(plane_gf)
-    poly = newton_poly(gram_f[...].astype(wide_type)).astype(low_type)
-    out_f[1, core] = dot_nn(moment_f[...], poly).astype(low_type)
+    out_f[1, core] = newton_step(moment_f[...], newton_poly(gram_f[...].astype(wide_type)))
     start(mate_x)
     arrive(spread_s)
     start(plane_s)
@@ -1196,8 +1197,7 @@
     arrive(plane_g)
     start(mate_g)
     arrive(mate_go)
-    poly = newton_poly(gram_o[...].astype(wide_type)).astype(low_type)
-    step_o[...] = dot_nn(moment_o[...], poly).astype(low_type)
+    step_o[...] = newton_step(moment_o[...], newton_poly(gram_o[...].astype(wide_type)))
     arrive(plane_s)
     start(mate_s)
     begin(write_o)

time: 190 us -> 189 us (level)
  no operation moved by 1% of the time
where the time goes in v9:
time: 189 us
  Pallas kernels  188 us (99%)
    pallas_call x1, Pallas kernels, back(): pl.pallas_call(functools.partial(back_kernel, narrow=narrow, chunks=chunk...  90.4 us
    pallas_call x1, Pallas kernels, forward(): pl.pallas_call(functools.partial(forward_kernel, narrow=narrow, total_seq...  47.7 us
    pallas_call x1, Pallas kernels, feed(): pl.pallas_call(functools.partial(feed_kernel, per_seq=length // block), g...  40 us
    pallas_call x1, Pallas kernels, finish(): pl.pallas_call(finish_kernel, grid=(steps,), in_specs=[rows(item) for ite...  10.1 us

profile of v9, /device:TPU:0, one launch (start us, length us, event | category | flops | bytes accessed | tf_op | source)
XLA Modules:
  0.0 189.1 jit_solution(12495005358812974670)
XLA Ops:
  0.6 47.7 %forward.1 = (bf16[2,1024,512]{2,1,0:T(8,128)(2,1)}, bf16[2,1024,512]{2,1,0:T(8,128)(2,1)}, bf16[2,1024,512]{2,1,0:T(8,128)(2,1)}, bf16[2,1024,512]{2,1,0:T(8,12...) custom-call(s32[2]{0:T(128)} %ids_ref.3, ...), custom_call_target="tpu_custom_call" | custom-call | tf_op jit(solution)/shard_map/forward/pallas_call | solution.py:838
  48.3 40.0 %feed.1 = (bf16[2048,512]{1,0:T(8,128)(2,1)}, bf16[2048,512]{1,0:T(8,128)(2,1)}, bf16[2048,512]{1,0:T(8,128)(2,1)}, bf16[2,512,2048]{2,1,0:T(8,128)(2,1)}, bf16[512,512]{1,0:T(8,128)(2,1)}, /*index=5*/f32[2,512]{1,0:T(2,128)}) custom-call(s32[2]{0:T(128)} %ids_ref.3, f32[8,128]{1,0:T(8,128)} %get-tuple-element.52.weight_ref, bf16[2048,512]{1,0:T(8,128)(2,1)} %bitcast.23, ...), custom_call_target="tpu_custom_call" | custom-call | tf_op jit(solution)/shard_map/feed/pallas_call | solution.py:279
  88.4 90.4 %back.1 = (bf16[2,1024,512]{2,1,0:T(8,128)(2,1)}, bf16[5,128,512]{2,1,0:T(8,128)(2,1)}, bf16[5,128,512]{2,1,0:T(8,128)(2,1)}, bf16[2,512,512]{2,1,0:T(8,128)(2,1...) custom-call(bf16[2,1024,512]{2,1,0:T(8,128)(2,1)} %get-tuple-element.58.refs_0_, ...), custom_call_target="tpu_custom_call" | custom-call | tf_op jit(solution)/shard_map/back/pallas_call | solution.py:1491
  178.8 10.1 %finish.1 = (f32[2048,512]{1,0:T(8,128)}, f32[640,512]{1,0:T(8,128)}, f32[640,512]{1,0:T(8,128)}, f32[640,512]{1,0:T(8,128)}, bf16[640,512]{1,0:T(8,128)(2,1)}, ...) custom-call(bf16[2048,512]{1,0:T(8,128)(2,1)} %get-tuple-element.57., ...), custom_call_target="tpu_custom_call" | custom-call | tf_op jit(solution)/shard_map/finish/pallas_call | solution.py:404
